TPU v7x, 32 devices: a whole 2x2x4 slice. The times are simulated.
32 devices in a mesh: dp: 8 (over z, y), tier: 2 (over x), head: 2 (over core).
Axes of the slice: x: 2, y: 2, z: 4, core: 2. Of those that a mesh axis runs over, the one named last changes fastest.
Arguments:
- inputs: bfloat16 [24, 512, 1024], P('dp', 'tier'), may hold values from -6 to 6
- memories: bfloat16 [24, 2, 512, 1024], P('dp', 'tier'), may hold values from -6 to 6
- seg_len: int32 [24], P('dp'), may hold values from 128 to 512, as said below
- mem_count: int32 [24, 2], P('dp', 'tier'), may hold values from 1 to 512, as said below
- w_query: bfloat16 [1024, 1024], P(None, 'head'), may hold values from -0.1875 to 0.1875
- w_key: bfloat16 [1024, 1024], P(None, 'head'), may hold values from -0.1875 to 0.1875
- w_value: bfloat16 [1024, 1024], P(None, 'head'), may hold values from -0.1875 to 0.1875
- w_attn_out: bfloat16 [1024, 1024], P('head'), may hold values from -3 to 3
- w_ffn_in: bfloat16 [1024, 4096], P(None, 'head'), may hold values from -0.1875 to 0.1875
- w_ffn_out: bfloat16 [4096, 1024], P('head'), may hold values from -0.09375 to 0.09375
- w_compress: bfloat16 [3, 1024, 1024], P(None, None, ('tier', 'head')), may hold values from -0.109375 to 0.109375
- gain_attn: float32 [1024], replicated, may hold values from 0.25 to 1.75
- bias_attn: float32 [1024], replicated, may hold values from -2.5 to 2.5
- gain_ffn: float32 [1024], replicated, may hold values from 0.25 to 1.75
- bias_ffn: float32 [1024], replicated, may hold values from -2.5 to 2.5
- cotan_output: bfloat16 [24, 512, 1024], P('dp', 'tier'), may hold values from -6 to 6
- cotan_compressed: bfloat16 [24, 170, 1024], P('dp', None, ('tier', 'head')), may hold values from -6 to 6
Outputs:
- layer_output: bfloat16 [24, 512, 1024], P('dp', 'tier')
- compressed: bfloat16 [24, 170, 1024], P('dp', None, ('tier', 'head'))
- grad_inputs: bfloat16 [24, 512, 1024], P('dp', 'tier')
- grad_query: float32 [1024, 1024], P(None, 'head')
- grad_key: float32 [1024, 1024], P(None, 'head')
- grad_value: float32 [1024, 1024], P(None, 'head')
- grad_attn_out: float32 [1024, 1024], P('head')
- grad_ffn_in: float32 [1024, 4096], P(None, 'head')
- grad_ffn_out: float32 [4096, 1024], P('head')
- grad_compress: float32 [3, 1024, 1024], P(None, None, ('tier', 'head'))
- grad_gain_attn: float32 [1024], replicated
- grad_bias_attn: float32 [1024], replicated
- grad_gain_ffn: float32 [1024], replicated
- grad_bias_ffn: float32 [1024], replicated
Inputs may be any that keep to these rules, and one draw needn't show every extreme that they name: `seg_len`: each segment holds 512, 256 or 128 tokens; in each group of streams k * 3 to k * 3 + 2, one holds 512 (others may too). `mem_count`: in each group of streams k * 3 to k * 3 + 2, one has a full recent memory and one a full compressed memory (others may too).
All inputs are finite; a program needn't handle non-finite values.
Results may differ from a plain program's by a relative error of at most 0.017.
Values may be sent and summed in bfloat16 or wider, within the bound.
No kernel may reach another device: no remote copies, remote signals or barrier semaphores. Data moves between devices by JAX's collectives and lax.ppermute only.
A program may use at most 192 MiB of HBM per device.

v0:
```python
import jax
import jax.numpy as jnp
from jax import lax
from jax.sharding import PartitionSpec as P

HD = 128
SEG = 512
MEM = 512
RATE = 3
COMP = 170


EPS = 1e-05
NEG = -1000000000.0


def from_behind(value, axis, by):
    peers = lax.axis_size(axis)
    pairs = [(i, i + by) for i in range(peers) if 0 <= i + by < peers]
    return lax.ppermute(value, axis, pairs)


def norm_stats(values):
    centre = values - jnp.mean(values, axis=-1, keepdims=True)
    inverse = lax.rsqrt(jnp.mean(centre * centre, axis=-1, keepdims=True) + EPS)
    return (centre * inverse, inverse)


def norm_back(grad_normed, normed, inverse, gain_vector):
    scaled = grad_normed * gain_vector
    return inverse * (
        scaled
        - jnp.mean(scaled, axis=-1, keepdims=True)
        - normed * jnp.mean(scaled * normed, axis=-1, keepdims=True)
    )


def split_heads(values):
    return values.reshape(values.shape[0], -1, HD).transpose(1, 0, 2)


def join_heads(values):
    return values.transpose(1, 0, 2).reshape(values.shape[1], -1)


def product(first_operand, second_operand):
    return jnp.dot(first_operand, second_operand, preferred_element_type=jnp.float32)


def scores_of(queries, key_heads, allowed):
    raw_scores = jnp.einsum(
        "hqd,hkd->hqk", queries, key_heads, preferred_element_type=jnp.float32
    ) * HD ** (-0.5)
    return jnp.where(allowed[None], raw_scores, NEG)


def masks_of(length, filled):
    row_index = jnp.arange(SEG)
    slot_index = jnp.arange(MEM)
    memory_ok = jnp.broadcast_to(slot_index[None, :] < filled, (SEG, MEM))
    causal_ok = (row_index[None, :] <= row_index[:, None]) & (row_index[None, :] < length)
    return (memory_ok, causal_ok)


def forward_part(queries, key_heads, value_heads, allowed):
    scores = scores_of(queries, key_heads, allowed)
    totals = jax.nn.logsumexp(scores, axis=-1, keepdims=True)
    weights = jnp.exp(scores - totals).astype(jnp.bfloat16)
    partial_value = jnp.einsum(
        "hqk,hkd->hqd", weights, value_heads, preferred_element_type=jnp.float32
    )
    return (join_heads(partial_value), totals[..., 0].T)


def backward_part(queries, key_heads, value_heads, allowed, own_column, offset, grad_part):
    scores = scores_of(queries, key_heads, allowed)
    raw_weights = jnp.exp(scores - own_column)
    grad_weights = jnp.einsum(
        "hqd,hkd->hqk", grad_part, value_heads, preferred_element_type=jnp.float32
    )
    spent_sum = jnp.sum(raw_weights * grad_weights, axis=-1, keepdims=True)
    grad_scores = (raw_weights * (grad_weights + offset - spent_sum)).astype(jnp.bfloat16)
    factor = HD ** (-0.5)
    grad_queries = (
        jnp.einsum("hqk,hkd->hqd", grad_scores, key_heads, preferred_element_type=jnp.float32)
        * factor
    )
    grad_keys = (
        jnp.einsum("hqk,hqd->hkd", grad_scores, queries, preferred_element_type=jnp.float32)
        * factor
    )
    grad_values = jnp.einsum(
        "hqk,hqd->hkd",
        raw_weights.astype(jnp.bfloat16),
        grad_part,
        preferred_element_type=jnp.float32,
    )
    return (join_heads(grad_queries), join_heads(grad_keys), join_heads(grad_values))


def on_device(
    inputs,
    memories,
    seg_len,
    mem_count,
    w_query,
    w_key,
    w_value,
    w_attn_out,
    w_ffn_in,
    w_ffn_out,
    w_compress,
    gain_attn,
    bias_attn,
    gain_ffn,
    bias_ffn,
    cotan_output,
    cotan_compressed,
):
    tier_index = lax.axis_index("tier")
    streams, half_rows, model_width = inputs.shape
    features = w_query.shape[1]
    heads_here = features // HD
    tokens = inputs.astype(jnp.float32)
    row_index = tier_index * half_rows + jnp.arange(half_rows)
    row_valid = (row_index[None, :] < seg_len[:, None])[..., None]
    normed_first, inverse_first = norm_stats(tokens)
    normed_own = (normed_first * gain_attn + bias_attn).astype(jnp.bfloat16)
    normed_full = lax.all_gather(normed_own, "tier", axis=1, tiled=True)
    stored = memories[:, 0].astype(jnp.float32)
    stored_normed, stored_inverse = norm_stats(stored)
    stored_low = (stored_normed * gain_attn + bias_attn).astype(jnp.bfloat16)
    counts = mem_count[:, 0]

    def attend(stream_item):
        segment_normed, memory_rows, length, filled = stream_item
        queries = product(segment_normed, w_query).astype(jnp.bfloat16)
        memory_keys = product(memory_rows, w_key).astype(jnp.bfloat16)
        memory_values = product(memory_rows, w_value).astype(jnp.bfloat16)
        memory_ok, causal_ok = masks_of(length, filled)

        def near_side(unused):
            segment_keys = product(segment_normed, w_key).astype(jnp.bfloat16)
            segment_values = product(segment_normed, w_value).astype(jnp.bfloat16)
            partial_value, totals = forward_part(
                split_heads(queries),
                split_heads(jnp.concatenate([memory_keys, segment_keys], 0)),
                split_heads(jnp.concatenate([memory_values, segment_values], 0)),
                jnp.concatenate([memory_ok, causal_ok], 1),
            )
            return (partial_value, totals, segment_keys, segment_values)

        def far_side(unused):
            partial_value, totals = forward_part(
                split_heads(queries),
                split_heads(memory_keys),
                split_heads(memory_values),
                memory_ok,
            )
            empty_rows = jnp.zeros_like(queries)
            return (partial_value, totals, empty_rows, empty_rows)

        partial_value, totals, segment_keys, segment_values = lax.cond(
            tier_index == 0, near_side, far_side, 0
        )
        return (
            partial_value,
            totals,
            queries,
            memory_keys,
            memory_values,
            segment_keys,
            segment_values,
        )

    partials, own_totals, queries, memory_keys, memory_values, segment_keys, segment_values = (
        lax.map(attend, (normed_full, stored_low, seg_len, counts))
    )
    both_parts, both_totals = (
        lax.all_to_all(partials[None], "tier", split_axis=2, concat_axis=0, tiled=True),
        lax.all_to_all(own_totals[None], "tier", split_axis=2, concat_axis=0, tiled=True),
    )
    merged_totals = jnp.logaddexp(both_totals[0], both_totals[1])
    mixing = jnp.exp(both_totals - merged_totals[None])
    merged = jnp.sum(
        both_parts.reshape(2, streams, half_rows, heads_here, HD) * mixing[..., None], axis=0
    ).reshape(streams, half_rows, features)
    merged_low = merged.astype(jnp.bfloat16)
    attended = lax.psum(product(merged_low, w_attn_out).astype(jnp.bfloat16), "head").astype(
        jnp.float32
    )
    hidden = tokens + attended
    normed_second, inverse_second = norm_stats(hidden)
    hidden_low = (normed_second * gain_ffn + bias_ffn).astype(jnp.bfloat16)
    lifted = product(hidden_low, w_ffn_in)
    activated = jax.nn.gelu(lifted).astype(jnp.bfloat16)
    ffn_result = lax.psum(product(activated, w_ffn_out).astype(jnp.bfloat16), "head").astype(
        jnp.float32
    )
    layer_output = jnp.where(row_valid, hidden + ffn_result, 0.0).astype(jnp.bfloat16)
    slot_valid = (jnp.arange(MEM)[None, :] < counts[:, None])[..., None]
    evicted_own = jnp.where(slot_valid, memories[:, 0], jnp.zeros_like(memories[:, 0]))[
        :, : COMP * RATE
    ]
    evicted_sent = from_behind(evicted_own, "tier", 1)
    evicted = jnp.where(tier_index == 0, evicted_own, evicted_sent).reshape(
        streams * COMP, RATE * model_width
    )
    squeeze_valid = (jnp.arange(COMP)[None, :] < (seg_len // RATE)[:, None])[..., None]
    squeezed = product(evicted, w_compress.reshape(RATE * model_width, -1)).reshape(
        streams, COMP, -1
    )
    compressed = jnp.where(squeeze_valid, squeezed, 0.0).astype(jnp.bfloat16)
    grad_squeezed = jnp.where(
        squeeze_valid, cotan_compressed, jnp.zeros_like(cotan_compressed)
    ).reshape(streams * COMP, -1)
    grad_compress = lax.psum(
        jnp.einsum("rk,rc->kc", evicted, grad_squeezed, preferred_element_type=jnp.float32), "dp"
    ).reshape(RATE, model_width, -1)
    grad_out = jnp.where(row_valid, cotan_output.astype(jnp.float32), 0.0)
    grad_ffn_low = grad_out.astype(jnp.bfloat16)
    grad_ffn_out = jnp.einsum(
        "srk,srd->kd", activated, grad_ffn_low, preferred_element_type=jnp.float32
    )
    grad_activated = jnp.einsum(
        "srd,kd->srk", grad_ffn_low, w_ffn_out, preferred_element_type=jnp.float32
    )
    gelu_value, gelu_pull = jax.vjp(jax.nn.gelu, lifted)
    grad_lifted = gelu_pull(grad_activated)[0].astype(jnp.bfloat16)
    grad_ffn_in = jnp.einsum(
        "srd,srk->dk", hidden_low, grad_lifted, preferred_element_type=jnp.float32
    )
    grad_hidden_normed = lax.psum(
        jnp.einsum("srk,dk->srd", grad_lifted, w_ffn_in, preferred_element_type=jnp.float32).astype(
            jnp.bfloat16
        ),
        "head",
    ).astype(jnp.float32)
    grad_gain_ffn = jnp.sum(grad_hidden_normed * normed_second, axis=(0, 1))
    grad_bias_ffn = jnp.sum(grad_hidden_normed, axis=(0, 1))
    grad_hidden = grad_out + norm_back(grad_hidden_normed, normed_second, inverse_second, gain_ffn)
    grad_attended = grad_hidden.astype(jnp.bfloat16)
    grad_attn_out = jnp.einsum(
        "srf,srd->fd", merged_low, grad_attended, preferred_element_type=jnp.float32
    )
    grad_merged = jnp.einsum(
        "srd,fd->srf", grad_attended, w_attn_out, preferred_element_type=jnp.float32
    ).astype(jnp.bfloat16)
    grad_merged_wide = grad_merged.astype(jnp.float32)
    delta_rows = jnp.sum(
        (grad_merged_wide * merged).reshape(streams, half_rows, heads_here, HD), axis=-1
    )
    grad_full, delta_full, totals_full = (
        lax.all_gather(grad_merged_wide, "tier", axis=1, tiled=True),
        lax.all_gather(delta_rows, "tier", axis=1, tiled=True),
        lax.all_gather(merged_totals, "tier", axis=1, tiled=True),
    )

    def attend_back(stream_item):
        (
            queries_one,
            memory_keys_one,
            memory_values_one,
            segment_keys_one,
            segment_values_one,
            partial_one,
            own_one,
            grad_one,
            delta_one,
            total_one,
            length,
            filled,
        ) = stream_item
        weight_own = jnp.exp(own_one - total_one)
        grad_heads = grad_one.reshape(SEG, heads_here, HD)
        own_dot = jnp.sum(grad_heads * partial_one.reshape(SEG, heads_here, HD), axis=-1)
        offset = (weight_own * (own_dot - delta_one)).T[:, :, None]
        grad_part = split_heads(
            (grad_heads * weight_own[..., None]).reshape(SEG, features).astype(jnp.bfloat16)
        )
        own_column = own_one.T[:, :, None]
        memory_ok, causal_ok = masks_of(length, filled)
        query_heads = split_heads(queries_one)

        def near_back(unused):
            grad_queries, grad_keys, grad_values = backward_part(
                query_heads,
                split_heads(jnp.concatenate([memory_keys_one, segment_keys_one], 0)),
                split_heads(jnp.concatenate([memory_values_one, segment_values_one], 0)),
                jnp.concatenate([memory_ok, causal_ok], 1),
                own_column,
                offset,
                grad_part,
            )
            return (
                grad_queries,
                grad_keys[:MEM],
                grad_values[:MEM],
                grad_keys[MEM:],
                grad_values[MEM:],
            )

        def far_back(unused):
            grad_queries, grad_keys, grad_values = backward_part(
                query_heads,
                split_heads(memory_keys_one),
                split_heads(memory_values_one),
                memory_ok,
                own_column,
                offset,
                grad_part,
            )
            empty_rows = jnp.zeros((SEG, features), jnp.float32)
            return (grad_queries, grad_keys, grad_values, empty_rows, empty_rows)

        return lax.cond(tier_index == 0, near_back, far_back, 0)

    grad_queries, grad_memory_keys, grad_memory_values, grad_segment_keys, grad_segment_values = (
        lax.map(
            attend_back,
            (
                queries,
                memory_keys,
                memory_values,
                segment_keys,
                segment_values,
                partials,
                own_totals,
                grad_full,
                delta_full,
                totals_full,
                seg_len,
                counts,
            ),
        )
    )
    summed_queries, summed_keys, summed_values = (
        lax.psum_scatter(
            grad_queries.astype(jnp.bfloat16), "tier", scatter_dimension=1, tiled=True
        ).astype(jnp.float32),
        lax.psum_scatter(
            grad_segment_keys.astype(jnp.bfloat16), "tier", scatter_dimension=1, tiled=True
        ).astype(jnp.float32),
        lax.psum_scatter(
            grad_segment_values.astype(jnp.bfloat16), "tier", scatter_dimension=1, tiled=True
        ).astype(jnp.float32),
    )
    grad_queries_low = summed_queries.astype(jnp.bfloat16)
    grad_keys_low = summed_keys.astype(jnp.bfloat16)
    grad_values_low = summed_values.astype(jnp.bfloat16)
    grad_mem_keys = grad_memory_keys.astype(jnp.bfloat16)
    grad_mem_values = grad_memory_values.astype(jnp.bfloat16)
    grad_query = jnp.einsum(
        "srd,srf->df", normed_own, grad_queries_low, preferred_element_type=jnp.float32
    )
    grad_key = jnp.einsum(
        "srd,srf->df", normed_own, grad_keys_low, preferred_element_type=jnp.float32
    ) + jnp.einsum("smd,smf->df", stored_low, grad_mem_keys, preferred_element_type=jnp.float32)
    grad_value = jnp.einsum(
        "srd,srf->df", normed_own, grad_values_low, preferred_element_type=jnp.float32
    ) + jnp.einsum("smd,smf->df", stored_low, grad_mem_values, preferred_element_type=jnp.float32)
    grad_normed_part = (
        jnp.einsum("srf,df->srd", grad_queries_low, w_query, preferred_element_type=jnp.float32)
        + jnp.einsum("srf,df->srd", grad_keys_low, w_key, preferred_element_type=jnp.float32)
        + jnp.einsum("srf,df->srd", grad_values_low, w_value, preferred_element_type=jnp.float32)
    )
    grad_stored_part = jnp.einsum(
        "smf,df->smd", grad_mem_keys, w_key, preferred_element_type=jnp.float32
    ) + jnp.einsum("smf,df->smd", grad_mem_values, w_value, preferred_element_type=jnp.float32)
    stored_gain_part = jnp.sum(grad_stored_part * stored_normed, axis=(0, 1))
    stored_bias_part = jnp.sum(grad_stored_part, axis=(0, 1))
    grad_normed, stored_gain, stored_bias = (
        lax.psum(grad_normed_part.astype(jnp.bfloat16), "head").astype(jnp.float32),
        lax.psum(stored_gain_part.astype(jnp.bfloat16), "head").astype(jnp.float32),
        lax.psum(stored_bias_part.astype(jnp.bfloat16), "head").astype(jnp.float32),
    )
    grad_gain_attn = jnp.sum(grad_normed * normed_first, axis=(0, 1)) + stored_gain
    grad_bias_attn = jnp.sum(grad_normed, axis=(0, 1)) + stored_bias
    grad_inputs = (
        grad_hidden + norm_back(grad_normed, normed_first, inverse_first, gain_attn)
    ).astype(jnp.bfloat16)
    shares = (
        lax.psum_scatter(grad_query, ("dp", "tier"), scatter_dimension=0, tiled=True),
        lax.psum_scatter(grad_key, ("dp", "tier"), scatter_dimension=0, tiled=True),
        lax.psum_scatter(grad_value, ("dp", "tier"), scatter_dimension=0, tiled=True),
        lax.psum_scatter(grad_attn_out, ("dp", "tier"), scatter_dimension=1, tiled=True),
        lax.psum_scatter(grad_gain_attn, ("dp", "tier"), scatter_dimension=0, tiled=True),
        lax.psum_scatter(grad_bias_attn, ("dp", "tier"), scatter_dimension=0, tiled=True),
        lax.psum_scatter(grad_ffn_in, ("dp", "tier"), scatter_dimension=0, tiled=True),
        lax.psum_scatter(grad_ffn_out, ("dp", "tier"), scatter_dimension=1, tiled=True),
        lax.psum_scatter(grad_gain_ffn, ("dp", "tier"), scatter_dimension=0, tiled=True),
        lax.psum_scatter(grad_bias_ffn, ("dp", "tier"), scatter_dimension=0, tiled=True),
    )
    gathered = (
        lax.all_gather(shares[0].astype(jnp.bfloat16), ("dp", "tier"), axis=0, tiled=True).astype(
            jnp.float32
        ),
        lax.all_gather(shares[1].astype(jnp.bfloat16), ("dp", "tier"), axis=0, tiled=True).astype(
            jnp.float32
        ),
        lax.all_gather(shares[2].astype(jnp.bfloat16), ("dp", "tier"), axis=0, tiled=True).astype(
            jnp.float32
        ),
        lax.all_gather(shares[3].astype(jnp.bfloat16), ("dp", "tier"), axis=1, tiled=True).astype(
            jnp.float32
        ),
        lax.all_gather(shares[4].astype(jnp.bfloat16), ("dp", "tier"), axis=0, tiled=True).astype(
            jnp.float32
        ),
        lax.all_gather(shares[5].astype(jnp.bfloat16), ("dp", "tier"), axis=0, tiled=True).astype(
            jnp.float32
        ),
        lax.all_gather(shares[6].astype(jnp.bfloat16), ("dp", "tier"), axis=0, tiled=True).astype(
            jnp.float32
        ),
        lax.all_gather(shares[7].astype(jnp.bfloat16), ("dp", "tier"), axis=1, tiled=True).astype(
            jnp.float32
        ),
        lax.all_gather(shares[8].astype(jnp.bfloat16), ("dp", "tier"), axis=0, tiled=True).astype(
            jnp.float32
        ),
        lax.all_gather(shares[9].astype(jnp.bfloat16), ("dp", "tier"), axis=0, tiled=True).astype(
            jnp.float32
        ),
    )
    return (
        layer_output,
        compressed,
        grad_inputs,
        gathered[0],
        gathered[1],
        gathered[2],
        gathered[3],
        gathered[6],
        gathered[7],
        grad_compress,
        gathered[4],
        gathered[5],
        gathered[8],
        gathered[9],
    )


def solution(mesh):
    return jax.shard_map(
        on_device,
        mesh=mesh,
        in_specs=(
            P("dp", "tier", None),
            P("dp", "tier", None, None),
            P("dp"),
            P("dp", "tier"),
            P(None, "head"),
            P(None, "head"),
            P(None, "head"),
            P("head", None),
            P(None, "head"),
            P("head", None),
            P(None, None, ("tier", "head")),
            P(),
            P(),
            P(),
            P(),
            P("dp", "tier", None),
            P("dp", None, ("tier", "head")),
        ),
        out_specs=(
            P("dp", "tier", None),
            P("dp", None, ("tier", "head")),
            P("dp", "tier", None),
            P(None, "head"),
            P(None, "head"),
            P(None, "head"),
            P("head", None),
            P(None, "head"),
            P("head", None),
            P(None, None, ("tier", "head")),
            P(),
            P(),
            P(),
            P(),
        ),
        check_vma=False,
    )
```

profile of v0, /device:TPU:0, one launch (start us, length us, event | category | flops | bytes accessed | tf_op | source)
XLA Modules:
  0.0 1896.5 jit_solution(12305209345695678502)
XLA Ops:
  20.0 41.4 %all-gather.10.cloned.1.call-done = bf16[3,512,1024]{2,1,0:T(8,128)(2,1)} async-done(((bf16[3,256,1024]{2,1,0:T(8,128)(2,1)}), bf16[3,512,1024]{2,1,0:T(8,128)(2,1)}) %all-gather.10.cloned.1.call-update) | async-done | bytes 3145744 | tf_op jit(solution)/shard_map/all_gather | solution.py:129
  61.3 130.6 %while.46 = (s32[]{:T(128)}, f32[3,512,512]{1,2,0:T(8,128)}, f32[3,512,4]{1,2,0:T(4,128)S(1)}, bf16[3,512,512]{2,1,0:T(8,128)(2,1)}, bf16[3,512,512]{2,1,0:T(8,1...) while((s32[]{:T(128)}, f32[3,512,512]{1,2,0:T(8,128)}, ...), condition=%wide.region_11.12_spmd.clone, body=%wide.region_4.11_spmd.sunk.clone | while | flops 3787736064 | bytes 121763368 | solution.py:177
  74.4 24.7 %conditional.6 = (f32[1,512,512]{1,2,0:T(8,128)}, f32[1,512,4]{1,2,0:T(4,128)S(1)}, bf16[1,512,512]{2,1,0:T(8,128)(2,1)}, bf16[1,512,512]{2,1,0:T(8,128)(2,1)}) conditional(s32[]{:T(128)} %convert_element_type.520, (pred[1,512]{1,0:T(4,128)(4,1)S(1)}, bf16[512,512]{1,0:T(8,128)(2,1)}, bf16[512,512]{1,0:T(8,128)(2,1)}, ...), branch_computations={%region_5.7_spmd, %region_8.10_spmd} | conditional | flops 2176336384 | bytes 89234136 | solution.py:163
  92.0 7.0 fusion.15
  117.7 24.7 %conditional.6 = (f32[1,512,512]{1,2,0:T(8,128)}, f32[1,512,4]{1,2,0:T(4,128)S(1)}, bf16[1,512,512]{2,1,0:T(8,128)(2,1)}, bf16[1,512,512]{2,1,0:T(8,128)(2,1)}) conditional(s32[]{:T(128)} %convert_element_type.520, (pred[1,512]{1,0:T(4,128)(4,1)S(1)}, bf16[512,512]{1,0:T(8,128)(2,1)}, bf16[512,512]{1,0:T(8,128)(2,1)}, ...), branch_computations={%region_5.7_spmd, %region_8.10_spmd} | conditional | flops 2176336384 | bytes 89234136 | solution.py:163
  135.3 7.0 fusion.15
  160.9 24.7 %conditional.6 = (f32[1,512,512]{1,2,0:T(8,128)}, f32[1,512,4]{1,2,0:T(4,128)S(1)}, bf16[1,512,512]{2,1,0:T(8,128)(2,1)}, bf16[1,512,512]{2,1,0:T(8,128)(2,1)}) conditional(s32[]{:T(128)} %convert_element_type.520, (pred[1,512]{1,0:T(4,128)(4,1)S(1)}, bf16[512,512]{1,0:T(8,128)(2,1)}, bf16[512,512]{1,0:T(8,128)(2,1)}, ...), branch_computations={%region_5.7_spmd, %region_8.10_spmd} | conditional | flops 2176336384 | bytes 89234136 | solution.py:163
  178.6 7.0 fusion.15
  201.1 8.5 copy.273
  209.5 5.3 all-to-all-start
  221.3 5.0 mul.283
  226.4 24.9 %all-to-all-done = f32[1,3,512,512]{3,0,1,2:T(1,128)} async-done(((f32[1,3,512,512]{3,0,1,2:T(1,128)}), f32[1,3,512,512]{3,0,1,2:T(1,128)}, u32[]{:S(2)}, u32[]{:S(2)}) %all-to-all-start) | async-done | bytes 3145760 | tf_op jit(solution)/shard_map/all_to_all | solution.py:180
  261.2 20.3 %all-reduce.17.cloned.1.call-done = bf16[3,256,1024]{2,1,0:T(8,128)(2,1)} async-done(((bf16[3,256,1024]{2,1,0:T(8,128)(2,1)}), bf16[3,256,1024]{2,1,0:T(8,128)(2,1)}) %all-reduce.17.cloned.1.call-update) | async-done | bytes 1572880 | tf_op jit(solution)/shard_map/psum | solution.py:189
  288.4 7.3 fusion.83
  297.4 4.5 fusion.120
  302.0 21.7 %all-reduce.19.cloned.1.call-done = bf16[3,256,1024]{2,1,0:T(8,128)(2,1)} async-done(((bf16[3,256,1024]{2,1,0:T(8,128)(2,1)}), bf16[3,256,1024]{2,1,0:T(8,128)(2,1)}) %all-reduce.19.cloned.1.call-update) | async-done | bytes 1572880 | tf_op jit(solution)/shard_map/psum | solution.py:233
  327.6 5.2 fusion.160
  337.8 4.5 all-gather
  345.0 20.5 %all_gather.45 = f32[3,512,4]{2,1,0:T(8,128)S(1)} all-gather(f32[3,256,4]{2,1,0:T(8,128)S(1)} %reduce_sum.220), channel_id=1, replica_groups=mesh['dp'=8,'tier'=2,'head'=2] {'tier'}, dimensions={1}, use_global_device_ids=true | all-gather | bytes 36864 | tf_op jit(solution)/shard_map/all_gather | solution.py:255
  365.8 21.7 %all-gather.12.cloned.1.call-done = f32[3,512,512]{2,1,0:T(8,128)} async-done(((f32[3,256,512]{2,1,0:T(8,128)}), f32[3,512,512]{2,1,0:T(8,128)}) %all-gather.12.cloned.1.call-update) | async-done | bytes 3145744 | tf_op jit(solution)/shard_map/all_gather | solution.py:254
  387.5 178.5 %while.47 = (s32[]{:T(128)}, bf16[3,512,512]{1,2,0:T(8,128)(2,1)}, bf16[3,512,512]{1,2,0:T(8,128)(2,1)}, bf16[3,512,512]{1,2,0:T(8,128)(2,1)}, bf16[3,512,512]{1...) while((s32[]{:T(128)}, bf16[3,512,512]{1,2,0:T(8,128)(2,1)}, ...), condition=%wide.region_27.28_spmd.clone, body=%wide.region_21.27_spmd.sunk.clone | while | flops 2727873536 | bytes 151760048 | solution.py:319
  406.0 34.9 %conditional.7 = (bf16[1,512,512]{1,2,0:T(8,128)(2,1)}, bf16[1,512,512]{1,2,0:T(8,128)(2,1)}, bf16[1,512,512]{1,2,0:T(8,128)(2,1)S(1)}, bf16[1,512,512]{1,2,0:T(8,128)(2,1)}, bf16[1,512,512]{1,2,0:T(8,128)(2,1)}) conditional(s32[]{:T(128)} %convert_element_type.522, (pred[1,512]{1,0:T(4,128)(4,1)S(1)}, bf16[512,512]{0,1:T(8,128)(2,1)S(1)}, ...), branch_computations={%region_23.24_spmd, %region_25.26_spmd} | conditional | flops 2726820352 | bytes 127982352 | solution.py:316
  411.3 6.0 fusion.59
  423.0 5.3 fusion.43
  428.3 4.9 fusion.42
  465.3 35.0 %conditional.7 = (bf16[1,512,512]{1,2,0:T(8,128)(2,1)}, bf16[1,512,512]{1,2,0:T(8,128)(2,1)}, bf16[1,512,512]{1,2,0:T(8,128)(2,1)S(1)}, bf16[1,512,512]{1,2,0:T(8,128)(2,1)}, bf16[1,512,512]{1,2,0:T(8,128)(2,1)}) conditional(s32[]{:T(128)} %convert_element_type.522, (pred[1,512]{1,0:T(4,128)(4,1)S(1)}, bf16[512,512]{0,1:T(8,128)(2,1)S(1)}, ...), branch_computations={%region_23.24_spmd, %region_25.26_spmd} | conditional | flops 2726820352 | bytes 127982352 | solution.py:316
  470.6 6.0 fusion.59
  482.3 5.3 fusion.43
  487.6 4.9 fusion.42
  524.6 34.9 %conditional.7 = (bf16[1,512,512]{1,2,0:T(8,128)(2,1)}, bf16[1,512,512]{1,2,0:T(8,128)(2,1)}, bf16[1,512,512]{1,2,0:T(8,128)(2,1)S(1)}, bf16[1,512,512]{1,2,0:T(8,128)(2,1)}, bf16[1,512,512]{1,2,0:T(8,128)(2,1)}) conditional(s32[]{:T(128)} %convert_element_type.522, (pred[1,512]{1,0:T(4,128)(4,1)S(1)}, bf16[512,512]{0,1:T(8,128)(2,1)S(1)}, ...), branch_computations={%region_23.24_spmd, %region_25.26_spmd} | conditional | flops 2726820352 | bytes 127982352 | solution.py:316
  529.9 6.0 fusion.59
  541.6 5.3 fusion.43
  547.0 4.9 fusion.42
  567.5 6.1 convolution_bitcast_fusion.2
  573.7 5.5 fusion.163
  579.2 13.1 reduce-scatter.14.cloned.1.call-done
  592.3 4.7 bitcast_add_fusion.1
  597.0 5.5 fusion.164
  602.6 18.0 reduce-scatter.12.cloned.1.call-done
  620.6 4.7 bitcast_add_fusion.2
  625.4 23.6 %reduce-scatter.10.cloned.1.call-done = bf16[3,256,512]{1,2,0:T(8,128)(2,1)} async-done(((bf16[3,512,512]{1,2,0:T(8,128)(2,1)}), bf16[3,256,512]{1,2,0:T(8,128)(2,1)}) %reduce-scatter.10.cloned.1.call-update) | async-done | bytes 786448 | tf_op jit(solution)/shard_map/reduce_scatter | solution.py:338
  653.2 9.5 convolution_bitcast_fusion.1
  662.8 10.3 convolution_bitcast_fusion
  673.2 59.3 %reduce-scatter.22.cloned.1.call-done = f32[512,64]{0,1:T(8,128)} async-done(((f32[512,1024]{0,1:T(8,128)}), f32[512,64]{0,1:T(8,128)}) %reduce-scatter.22.cloned.1.call-update) | async-done | bytes 131088 | tf_op jit(solution)/shard_map/reduce_scatter | solution.py:386
  734.3 9.1 fusion.123
  751.7 61.4 %reduce-scatter.20.cloned.1.call-done = f32[64,512]{1,0:T(8,128)} async-done(((f32[1024,512]{1,0:T(8,128)}), f32[64,512]{1,0:T(8,128)}) %reduce-scatter.20.cloned.1.call-update) | async-done | bytes 131088 | tf_op jit(solution)/shard_map/reduce_scatter | solution.py:385
  814.7 78.5 %reduce-scatter.18.cloned.1.call-done = f32[64,512]{1,0:T(8,128)} async-done(((f32[1024,512]{1,0:T(8,128)}), f32[64,512]{1,0:T(8,128)}) %reduce-scatter.18.cloned.1.call-update) | async-done | bytes 131088 | tf_op jit(solution)/shard_map/reduce_scatter | solution.py:384
  894.8 79.3 %reduce-scatter.16.cloned.1.call-done = f32[64,512]{1,0:T(8,128)} async-done(((f32[1024,512]{1,0:T(8,128)}), f32[64,512]{1,0:T(8,128)}) %reduce-scatter.16.cloned.1.call-update) | async-done | bytes 131088 | tf_op jit(solution)/shard_map/reduce_scatter | solution.py:383
  975.8 176.2 %reduce-scatter.24.cloned.1.call-done = f32[64,2048]{1,0:T(8,128)} async-done(((f32[1024,2048]{1,0:T(8,128)}), f32[64,2048]{1,0:T(8,128)}) %reduce-scatter.24.cloned.1.call-update) | async-done | bytes 524304 | tf_op jit(solution)/shard_map/reduce_scatter | solution.py:389
  1153.8 181.4 %reduce-scatter.26.cloned.1.call-done = f32[2048,64]{0,1:T(8,128)} async-done(((f32[2048,1024]{0,1:T(8,128)}), f32[2048,64]{0,1:T(8,128)}) %reduce-scatter.26.cloned.1.call-update) | async-done | bytes 524304 | tf_op jit(solution)/shard_map/reduce_scatter | solution.py:390
  1340.4 5.2 collective-permute-start
  1349.5 67.0 %collective-permute-done = bf16[3,510,1024]{2,1,0:T(8,128)(2,1)} collective-permute-done((bf16[3,510,1024]{2,1,0:T(8,128)(2,1)}, bf16[3,510,1024]{2,1,0:T(8,128)(2,1)}, u32[]{:S(2)}, u32[]{:S(2)}) %collective-permute-start) | collective-permute-done | bytes 3133472 | tf_op jit(solution)/shard_map/ppermute | solution.py:20
  1419.8 5.7 reshape.408
  1425.5 5.2 dot_general.139
  1430.7 4.6 fusion.162
  1455.1 79.8 %all-reduce.8 = (bf16[1024]{0:T(1024)(128)(2,1)S(1)}, bf16[1024]{0:T(1024)(128)(2,1)S(1)}, bf16[1024]{0:T(1024)(128)(2,1)S(1)}, bf16[1024]{0:T(1024)(128)(2,1)S(1)}) all-reduce(f32[1024]{0:T(1024)S(1)} %convert_add_fusion.2, f32[1024]{0:T(1024)S(1)} %convert_add_fusion.1, ...), channel_id=12, replica_groups=mesh['dp'=8,'tier'=2,'head'=2] {'dp','tier'}, use_global_device_ids=true, to_apply=%region_44.45.clone | all-reduce | flops 4096 | bytes 24576
  1536.0 37.4 %all-reduce.9 = (bf16[1024]{0:T(1024)(128)(2,1)S(1)}, bf16[1024]{0:T(1024)(128)(2,1)S(1)}, bf16[1024]{0:T(1024)(128)(2,1)S(1)}, bf16[1024]{0:T(1024)(128)(2,1)S(1)}) all-reduce(bf16[1024]{0:T(1024)(128)(2,1)S(1)} %dynamic-update-slice, bf16[1024]{0:T(1024)(128)(2,1)S(1)} %dynamic-update-slice.1, ...), channel_id=1, replica_groups=mesh['dp'=8,'tier'=2,'head'=2] {'dp','tier'}, use_global_device_ids=true, to_apply=%add | all-reduce | flops 4096 | bytes 16384
  1575.8 7.0 fusion.107
  1588.5 10.6 all-gather.14.cloned.1.call-done
  1601.9 74.8 %all-gather.22.cloned.1.call-done = bf16[1024,2048]{1,0:T(8,128)(2,1)} async-done(((bf16[64,2048]{1,0:T(8,128)(2,1)}), bf16[1024,2048]{1,0:T(8,128)(2,1)}) %all-gather.22.cloned.1.call-update) | async-done | bytes 4194320 | tf_op jit(solution)/shard_map/all_gather | solution.py:413
  1676.8 6.7 convert_element_type.262
  1683.4 70.7 %all-gather.24.cloned.1.call-done = bf16[2048,1024]{0,1:T(8,128)(2,1)} async-done(((bf16[2048,64]{0,1:T(8,128)(2,1)}), bf16[2048,1024]{0,1:T(8,128)(2,1)}) %all-gather.24.cloned.1.call-update) | async-done | bytes 4194320 | tf_op jit(solution)/shard_map/all_gather | solution.py:416
  1754.1 6.9 copy.308
  1761.0 124.8 %all-reduce.21.cloned.1.call-done = f32[3,1024,256]{2,1,0:T(8,128)} async-done(((f32[3,1024,256]{2,1,0:T(8,128)}), f32[3,1024,256]{2,1,0:T(8,128)}) %all-reduce.21.cloned.1.call-update) | async-done | bytes 3145744 | tf_op jit(solution)/shard_map/psum | solution.py:217
  (553 shorter events, 364.8 us)
Async XLA Ops:
  7.2 1428.1 %copy-start = (bf16[3,1024,256]{2,1,0:T(8,128)(2,1)S(1)}, bf16[3,1024,256]{2,1,0:T(8,128)(2,1)}, u32[]{:S(2)}) copy-start(bf16[3,1024,256]{2,1,0:T(8,128)(2,1)} %param.35) | copy-start | bytes 4718596
  7.2 54.1 %all-gather.10.cloned.1.call-start = ((), (), s32[]{:S(2)}) async-start(), calls=%async_computation.11 | async-start | bytes 4718592 | tf_op jit(solution)/shard_map/all_gather | solution.py:129
  17.5 43.8 %copy-start.61 = (s32[3,1]{0,1:T(1,128)S(1)}, s32[3,1]{0,1:T(1,128)}, u32[]{:S(2)}) copy-start(s32[3,1]{0,1:T(1,128)} %param.28) | copy-start | bytes 40
  17.5 43.8 %copy-start.62 = (s32[3]{0:T(128)S(1)}, s32[3]{0:T(128)}, u32[]{:S(2)}) copy-start(s32[3]{0:T(128)} %param.27) | copy-start | bytes 40
  61.6 6.4 copy-start.22
  104.9 6.4 copy-start.22
  148.2 6.4 copy-start.22
  191.9 17.6 copy-start.33
  197.8 11.7 all-to-all-start.1
  209.5 41.7 %all-to-all-start = ((f32[1,3,512,512]{3,0,1,2:T(1,128)}), f32[1,3,512,512]{3,0,1,2:T(1,128)}, u32[]{:S(2)}, u32[]{:S(2)}) async-start(f32[1,3,512,512]{3,0,1,2:T(1,128)} %copy.273), calls=%async_computation | async-start | bytes 6291456 | tf_op jit(solution)/shard_map/all_to_all | solution.py:180
  214.8 66.7 %all-reduce.17.cloned.1.call-start = ((), (), s32[]{:S(2)}) async-start(), calls=%async_computation.12 | async-start | bytes 3145728 | tf_op jit(solution)/shard_map/psum | solution.py:189
  257.2 24.3 %copy-start.9 = (bf16[3,256,1024]{2,1,0:T(8,128)(2,1)S(1)}, bf16[3,256,1024]{2,1,0:T(8,128)(2,1)}, u32[]{:S(2)}) copy-start(bf16[3,256,1024]{2,1,0:T(8,128)(2,1)} %param.25) | copy-start | bytes 4718596
  260.9 62.7 %all-reduce.19.cloned.1.call-start = ((), (), s32[]{:S(2)}) async-start(), calls=%async_computation.13 | async-start | bytes 3145728 | tf_op jit(solution)/shard_map/psum | solution.py:233
  261.2 66.3 %copy-start.58 = (pred[3,256]{1,0:T(4,128)(4,1)}, pred[3,256]{1,0:T(4,128)(4,1)S(1)}, u32[]{:S(2)}) copy-start(pred[3,256]{1,0:T(4,128)(4,1)S(1)} %broadcast_compare_fusion) | copy-start | bytes 2308
  261.2 23.1 %copy-start.54 = (f32[1024]{0:T(1024)S(1)}, f32[1024]{0:T(1024)}, u32[]{:S(2)}) copy-start(f32[1024]{0:T(1024)} %param.38) | copy-start | bytes 12292
  261.2 23.1 %copy-start.65 = (f32[1024]{0:T(1024)S(1)}, f32[1024]{0:T(1024)}, u32[]{:S(2)}) copy-start(f32[1024]{0:T(1024)} %param.39) | copy-start | bytes 12292
  283.6 44.0 %copy-start.43 = (f32[3,256]{1,0:T(4,128)}, f32[3,256]{1,0:T(4,128)S(1)}, u32[]{:S(2)}) copy-start(f32[3,256]{1,0:T(4,128)S(1)} %broadcast_multiply_fusion.5) | copy-start | bytes 9220
  284.6 42.9 %copy-start.45 = (f32[3,256]{1,0:T(4,128)}, f32[3,256]{1,0:T(4,128)S(1)}, u32[]{:S(2)}) copy-start(f32[3,256]{1,0:T(4,128)S(1)} %add_rsqrt_fusion.1) | copy-start | bytes 9220
  288.4 7.3 copy-start.69
  301.9 85.5 %all-gather.12.cloned.1.call-start = ((), (), s32[]{:S(2)}) async-start(), calls=%async_computation.14 | async-start | bytes 4718592 | tf_op jit(solution)/shard_map/all_gather | solution.py:254
  327.5 5.2 copy-start.50
  327.5 5.2 copy-start.52
  332.8 259.5 %reduce-scatter.14.cloned.1.call-start = ((), (), s32[]{:S(2)}) async-start(), calls=%async_computation.17 | async-start | bytes 2359296 | tf_op jit(solution)/shard_map/reduce_scatter | solution.py:344
  411.3 7.2 copy-start.6
  411.3 7.2 copy-start.7
  423.0 5.3 copy-start.4
  428.3 4.9 copy-start.14
  428.3 4.9 copy-start.15
  470.6 7.2 copy-start.6
  470.6 7.2 copy-start.7
  482.3 5.3 copy-start.4
  487.6 4.9 copy-start.14
  487.6 4.9 copy-start.15
  529.9 7.2 copy-start.6
  529.9 7.2 copy-start.7
  541.6 5.3 copy-start.4
  546.9 4.9 copy-start.14
  546.9 4.9 copy-start.15
  566.1 54.5 %reduce-scatter.12.cloned.1.call-start = ((), (), s32[]{:S(2)}) async-start(), calls=%async_computation.16 | async-start | bytes 2359296 | tf_op jit(solution)/shard_map/reduce_scatter | solution.py:341
  566.6 82.3 %reduce-scatter.10.cloned.1.call-start = ((), (), s32[]{:S(2)}) async-start(), calls=%async_computation.15 | async-start | bytes 2359296 | tf_op jit(solution)/shard_map/reduce_scatter | solution.py:338
  567.4 165.1 %reduce-scatter.22.cloned.1.call-start = ((), (), s32[]{:S(2)}) async-start(), calls=%async_computation.24 | async-start | bytes 2228224 | tf_op jit(solution)/shard_map/reduce_scatter | solution.py:386
  573.7 239.5 %reduce-scatter.20.cloned.1.call-start = ((), (), s32[]{:S(2)}) async-start(), calls=%async_computation.22 | async-start | bytes 2228224 | tf_op jit(solution)/shard_map/reduce_scatter | solution.py:385
  597.0 296.2 %reduce-scatter.18.cloned.1.call-start = ((), (), s32[]{:S(2)}) async-start(), calls=%async_computation.20 | async-start | bytes 2228224 | tf_op jit(solution)/shard_map/reduce_scatter | solution.py:384
  625.3 27.9 %copy-start.66 = (f32[1024]{0:T(1024)S(1)}, f32[1024]{0:T(1024)}, u32[]{:S(2)}) copy-start(f32[1024]{0:T(1024)} %param.39) | copy-start | bytes 12292
  625.3 348.8 %reduce-scatter.16.cloned.1.call-start = ((), (), s32[]{:S(2)}) async-start(), calls=%async_computation.18 | async-start | bytes 2228224 | tf_op jit(solution)/shard_map/reduce_scatter | solution.py:383
  652.9 499.0 %reduce-scatter.24.cloned.1.call-start = ((), (), s32[]{:S(2)}) async-start(), calls=%async_computation.26 | async-start | bytes 8912896 | tf_op jit(solution)/shard_map/reduce_scatter | solution.py:389
  662.7 672.4 %reduce-scatter.26.cloned.1.call-start = ((), (), s32[]{:S(2)}) async-start(), calls=%async_computation.28 | async-start | bytes 8912896 | tf_op jit(solution)/shard_map/reduce_scatter | solution.py:390
  673.1 776.2 %all-gather.20.cloned.1.call-start = ((), (), s32[]{:S(2)}) async-start(), calls=%async_computation.25 | async-start | bytes 1114112 | tf_op jit(solution)/shard_map/all_gather | solution.py:404
  734.0 717.9 %all-reduce.23.cloned.1.call-start = ((), (), s32[]{:S(2)}) async-start(), calls=%async_computation.31 | async-start | bytes 6291456 | tf_op jit(solution)/shard_map/psum | solution.py:197
  734.3 9.1 copy-start.27
  751.6 831.2 %all-gather.18.cloned.1.call-start = ((), (), s32[]{:S(2)}) async-start(), calls=%async_computation.23 | async-start | bytes 1114112 | tf_op jit(solution)/shard_map/all_gather | solution.py:401
  814.7 771.0 %all-gather.16.cloned.1.call-start = ((), (), s32[]{:S(2)}) async-start(), calls=%async_computation.21 | async-start | bytes 1114112 | tf_op jit(solution)/shard_map/all_gather | solution.py:398
  894.8 704.3 %all-gather.14.cloned.1.call-start = ((), (), s32[]{:S(2)}) async-start(), calls=%async_computation.19 | async-start | bytes 1114112 | tf_op jit(solution)/shard_map/all_gather | solution.py:395
  975.7 701.1 %all-gather.22.cloned.1.call-start = ((), (), s32[]{:S(2)}) async-start(), calls=%async_computation.27 | async-start | bytes 4456448 | tf_op jit(solution)/shard_map/all_gather | solution.py:413
  1153.7 600.4 %all-gather.24.cloned.1.call-start = ((), (), s32[]{:S(2)}) async-start(), calls=%async_computation.29 | async-start | bytes 4456448 | tf_op jit(solution)/shard_map/all_gather | solution.py:416
  1337.0 548.7 %all-reduce.21.cloned.1.call-start = ((), (), s32[]{:S(2)}) async-start(), calls=%async_computation.30 | async-start | bytes 6291456 | tf_op jit(solution)/shard_map/psum | solution.py:217
  1337.1 10.5 copy-start.60
  1340.4 76.1 %collective-permute-start = (bf16[3,510,1024]{2,1,0:T(8,128)(2,1)}, bf16[3,510,1024]{2,1,0:T(8,128)(2,1)}, u32[]{:S(2)}, u32[]{:S(2)}) collective-permute-start(bf16[3,510,1024]{2,1,0:T(8,128)(2,1)} %slice_select_fusion), channel_id=1, source_target_pairs={{0,2},{1,3},{4,6},{5,7},{8,10},{9,11},{12,14},{13,15},{16,18},{17,... | collective-permute-start | bytes 9400328 | tf_op jit(solution)/shard_map/ppermute | solution.py:20
  1425.5 5.2 copy-start.31
  1446.8 5.1 copy-start.36
  1446.8 5.1 copy-start.40
  1446.9 5.1 copy-start.42
  1449.3 5.7 copy-start.56
  1449.3 5.7 copy-start.57
  (63 other events, 189.8 us)
Sparse Core Ops, SparseCore 0:
  13.7 47.6 all-gather.9
  261.0 20.4 all-reduce.16
  302.1 21.5 all-reduce.18
  332.9 54.5 all-gather.11
  566.2 26.0 reduce-scatter.13
  594.5 26.0 reduce-scatter.11
  622.8 26.0 reduce-scatter.9
  651.9 80.5 reduce-scatter.21
  735.4 77.6 reduce-scatter.19
  815.9 77.2 reduce-scatter.17
  896.2 77.9 reduce-scatter.15
  977.0 174.8 reduce-scatter.23
  1154.9 180.2 reduce-scatter.25
  1338.2 59.0 all-gather.19
  1400.2 24.7 all-reduce.22
  1427.6 56.5 all-gather.17
  1487.4 54.4 all-gather.15
  1545.1 53.9 all-gather.13
  1601.9 74.8 all-gather.21
  1679.4 74.6 all-gather.23
  1758.3 127.4 all-reduce.20
where the time goes:
time: 1900 us
  waiting for transfers between devices  1170 us (62%)
  matrix products  234 us (12%)
  local copies, waits for them, and re-layouts  200 us (11%)
  blocking collectives  145 us (8%)
  other arithmetic  113 us (6%)
    reduce_scatter x1, waiting for transfers between devices, on_device(): lax.psum_scatter(grad_ffn_out, ('dp', 'tier'), scatter_dimension=1, tiled...  181 us
    reduce_scatter x1, waiting for transfers between devices, on_device(): lax.psum_scatter(grad_ffn_in, ('dp', 'tier'), scatter_dimension=0, tiled=...  176 us
    psum x1, waiting for transfers between devices, on_device(): lax.psum(jnp.einsum('rk,rc->kc', evicted, grad_squeezed, preferred_elemen...  125 us
    unnamed x2, blocking collectives  117 us
    reduce_scatter x1, waiting for transfers between devices, on_device(): lax.psum_scatter(grad_query, ('dp', 'tier'), scatter_dimension=0, tiled=T...  79.3 us
    reduce_scatter x1, waiting for transfers between devices, on_device(): lax.psum_scatter(grad_key, ('dp', 'tier'), scatter_dimension=0, tiled=True)  78.5 us
    all_gather x1, waiting for transfers between devices, on_device(): lax.all_gather(shares[6].astype(jnp.bfloat16), ('dp', 'tier'), axis=0, ti...  74.8 us
    all_gather x1, waiting for transfers between devices, on_device(): lax.all_gather(shares[7].astype(jnp.bfloat16), ('dp', 'tier'), axis=1, ti...  70.7 us
  transfers between devices with their start and end apart: 24, of which 19 were waited for; matrix products, arithmetic and copies ran while one was open for 10% of the time, Pallas kernels for 0%

commit v1 on v0

--- a/solution.py
+++ b/solution.py
@@ -18,6 +18,74 @@
     peers = lax.axis_size(axis)
     pairs = [(i, i + by) for i in range(peers) if 0 <= i + by < peers]
     return lax.ppermute(value, axis, pairs)
+
+
+def bits_of():
+    size = lax.axis_size("dp")
+    bits = [("tier", 1)]
+    step = 1
+    while step < size:
+        bits.append(("dp", step))
+        step *= 2
+    return bits
+
+
+def bit_value(bit):
+    axis, step = bit
+    return (lax.axis_index(axis) // step) % 2
+
+
+def swap(value, bit):
+    axis, step = bit
+    return lax.ppermute(value, axis, [(i, i ^ step) for i in range(lax.axis_size(axis))])
+
+
+def add_low(first, second):
+    total = first.astype(jnp.float32) + second.astype(jnp.float32)
+    return lax.optimization_barrier(total.astype(jnp.bfloat16))
+
+
+def sum_head(value):
+    own = lax.optimization_barrier(value.astype(jnp.bfloat16))
+    other = lax.ppermute(own, "head", [(0, 1), (1, 0)])
+    return own.astype(jnp.float32) + other.astype(jnp.float32)
+
+
+def all_reduce(value, order):
+    held = value
+    scattered = []
+    for place, bit in enumerate(order):
+        half = held.shape[0] // 2
+        if place == len(order) - 1 or half % 16:
+            held = add_low(held, swap(held, bit))
+        else:
+            side = bit_value(bit)
+            sent = lax.dynamic_slice_in_dim(held, (1 - side) * half, half, 0)
+            kept = lax.dynamic_slice_in_dim(held, side * half, half, 0)
+            held = add_low(kept, swap(sent, bit))
+            scattered.append((bit, side))
+    for bit, side in reversed(scattered):
+        other = swap(held, bit)
+        held = jnp.where(
+            side == 0, jnp.concatenate([held, other], 0), jnp.concatenate([other, held], 0)
+        )
+    return held
+
+
+def reduce_parts(value, sizes):
+    tier, *rest = bits_of()
+    orders = (
+        [tier, *rest],
+        [rest[0], rest[1], tier, *rest[2:]],
+        [rest[1], tier, rest[0], *rest[2:]],
+    )
+    low = lax.optimization_barrier(value.astype(jnp.bfloat16))
+    start = 0
+    pieces = []
+    for size, order in zip(sizes, orders):
+        pieces.append(all_reduce(low[start : start + size], order))
+        start += size
+    return jnp.concatenate(pieces, 0).astype(jnp.float32)
 
 
 def norm_stats(values):
@@ -186,17 +254,13 @@
         both_parts.reshape(2, streams, half_rows, heads_here, HD) * mixing[..., None], axis=0
     ).reshape(streams, half_rows, features)
     merged_low = merged.astype(jnp.bfloat16)
-    attended = lax.psum(product(merged_low, w_attn_out).astype(jnp.bfloat16), "head").astype(
-        jnp.float32
-    )
+    attended = sum_head(product(merged_low, w_attn_out))
     hidden = tokens + attended
     normed_second, inverse_second = norm_stats(hidden)
     hidden_low = (normed_second * gain_ffn + bias_ffn).astype(jnp.bfloat16)
     lifted = product(hidden_low, w_ffn_in)
     activated = jax.nn.gelu(lifted).astype(jnp.bfloat16)
-    ffn_result = lax.psum(product(activated, w_ffn_out).astype(jnp.bfloat16), "head").astype(
-        jnp.float32
-    )
+    ffn_result = sum_head(product(activated, w_ffn_out))
     layer_output = jnp.where(row_valid, hidden + ffn_result, 0.0).astype(jnp.bfloat16)
     slot_valid = (jnp.arange(MEM)[None, :] < counts[:, None])[..., None]
     evicted_own = jnp.where(slot_valid, memories[:, 0], jnp.zeros_like(memories[:, 0]))[
@@ -214,9 +278,14 @@
     grad_squeezed = jnp.where(
         squeeze_valid, cotan_compressed, jnp.zeros_like(cotan_compressed)
     ).reshape(streams * COMP, -1)
-    grad_compress = lax.psum(
-        jnp.einsum("rk,rc->kc", evicted, grad_squeezed, preferred_element_type=jnp.float32), "dp"
-    ).reshape(RATE, model_width, -1)
+    grad_compress_low = jnp.einsum(
+        "rk,rc->kc", evicted, grad_squeezed, preferred_element_type=jnp.float32
+    ).astype(jnp.bfloat16)
+    grad_compress = (
+        all_reduce(lax.optimization_barrier(grad_compress_low), bits_of()[1:])
+        .astype(jnp.float32)
+        .reshape(RATE, model_width, -1)
+    )
     grad_out = jnp.where(row_valid, cotan_output.astype(jnp.float32), 0.0)
     grad_ffn_low = grad_out.astype(jnp.bfloat16)
     grad_ffn_out = jnp.einsum(
@@ -230,12 +299,9 @@
     grad_ffn_in = jnp.einsum(
         "srd,srk->dk", hidden_low, grad_lifted, preferred_element_type=jnp.float32
     )
-    grad_hidden_normed = lax.psum(
-        jnp.einsum("srk,dk->srd", grad_lifted, w_ffn_in, preferred_element_type=jnp.float32).astype(
-            jnp.bfloat16
-        ),
-        "head",
-    ).astype(jnp.float32)
+    grad_hidden_normed = sum_head(
+        jnp.einsum("srk,dk->srd", grad_lifted, w_ffn_in, preferred_element_type=jnp.float32)
+    )
     grad_gain_ffn = jnp.sum(grad_hidden_normed * normed_second, axis=(0, 1))
     grad_bias_ffn = jnp.sum(grad_hidden_normed, axis=(0, 1))
     grad_hidden = grad_out + norm_back(grad_hidden_normed, normed_second, inverse_second, gain_ffn)
@@ -369,75 +435,33 @@
     ) + jnp.einsum("smf,df->smd", grad_mem_values, w_value, preferred_element_type=jnp.float32)
     stored_gain_part = jnp.sum(grad_stored_part * stored_normed, axis=(0, 1))
     stored_bias_part = jnp.sum(grad_stored_part, axis=(0, 1))
-    grad_normed, stored_gain, stored_bias = (
-        lax.psum(grad_normed_part.astype(jnp.bfloat16), "head").astype(jnp.float32),
-        lax.psum(stored_gain_part.astype(jnp.bfloat16), "head").astype(jnp.float32),
-        lax.psum(stored_bias_part.astype(jnp.bfloat16), "head").astype(jnp.float32),
-    )
-    grad_gain_attn = jnp.sum(grad_normed * normed_first, axis=(0, 1)) + stored_gain
-    grad_bias_attn = jnp.sum(grad_normed, axis=(0, 1)) + stored_bias
+    grad_normed = sum_head(grad_normed_part)
+    grad_gain_attn = 0.5 * jnp.sum(grad_normed * normed_first, axis=(0, 1)) + stored_gain_part
+    grad_bias_attn = 0.5 * jnp.sum(grad_normed, axis=(0, 1)) + stored_bias_part
     grad_inputs = (
         grad_hidden + norm_back(grad_normed, normed_first, inverse_first, gain_attn)
     ).astype(jnp.bfloat16)
-    shares = (
-        lax.psum_scatter(grad_query, ("dp", "tier"), scatter_dimension=0, tiled=True),
-        lax.psum_scatter(grad_key, ("dp", "tier"), scatter_dimension=0, tiled=True),
-        lax.psum_scatter(grad_value, ("dp", "tier"), scatter_dimension=0, tiled=True),
-        lax.psum_scatter(grad_attn_out, ("dp", "tier"), scatter_dimension=1, tiled=True),
-        lax.psum_scatter(grad_gain_attn, ("dp", "tier"), scatter_dimension=0, tiled=True),
-        lax.psum_scatter(grad_bias_attn, ("dp", "tier"), scatter_dimension=0, tiled=True),
-        lax.psum_scatter(grad_ffn_in, ("dp", "tier"), scatter_dimension=0, tiled=True),
-        lax.psum_scatter(grad_ffn_out, ("dp", "tier"), scatter_dimension=1, tiled=True),
-        lax.psum_scatter(grad_gain_ffn, ("dp", "tier"), scatter_dimension=0, tiled=True),
-        lax.psum_scatter(grad_bias_ffn, ("dp", "tier"), scatter_dimension=0, tiled=True),
-    )
-    gathered = (
-        lax.all_gather(shares[0].astype(jnp.bfloat16), ("dp", "tier"), axis=0, tiled=True).astype(
-            jnp.float32
+    vectors = lax.psum(
+        jnp.stack(
+            [grad_gain_attn, grad_bias_attn, 0.5 * grad_gain_ffn, 0.5 * grad_bias_ffn], axis=0
         ),
-        lax.all_gather(shares[1].astype(jnp.bfloat16), ("dp", "tier"), axis=0, tiled=True).astype(
-            jnp.float32
-        ),
-        lax.all_gather(shares[2].astype(jnp.bfloat16), ("dp", "tier"), axis=0, tiled=True).astype(
-            jnp.float32
-        ),
-        lax.all_gather(shares[3].astype(jnp.bfloat16), ("dp", "tier"), axis=1, tiled=True).astype(
-            jnp.float32
-        ),
-        lax.all_gather(shares[4].astype(jnp.bfloat16), ("dp", "tier"), axis=0, tiled=True).astype(
-            jnp.float32
-        ),
-        lax.all_gather(shares[5].astype(jnp.bfloat16), ("dp", "tier"), axis=0, tiled=True).astype(
-            jnp.float32
-        ),
-        lax.all_gather(shares[6].astype(jnp.bfloat16), ("dp", "tier"), axis=0, tiled=True).astype(
-            jnp.float32
-        ),
-        lax.all_gather(shares[7].astype(jnp.bfloat16), ("dp", "tier"), axis=1, tiled=True).astype(
-            jnp.float32
-        ),
-        lax.all_gather(shares[8].astype(jnp.bfloat16), ("dp", "tier"), axis=0, tiled=True).astype(
-            jnp.float32
-        ),
-        lax.all_gather(shares[9].astype(jnp.bfloat16), ("dp", "tier"), axis=0, tiled=True).astype(
-            jnp.float32
-        ),
+        ("dp", "tier", "head"),
     )
     return (
         layer_output,
         compressed,
         grad_inputs,
-        gathered[0],
-        gathered[1],
-        gathered[2],
-        gathered[3],
-        gathered[6],
-        gathered[7],
+        reduce_parts(grad_query, (256, 384, 384)),
+        reduce_parts(grad_key, (256, 384, 384)),
+        reduce_parts(grad_value, (256, 384, 384)),
+        reduce_parts(grad_attn_out, (128, 192, 192)),
+        reduce_parts(grad_ffn_in, (256, 384, 384)),
+        reduce_parts(grad_ffn_out, (512, 768, 768)),
         grad_compress,
-        gathered[4],
-        gathered[5],
-        gathered[8],
-        gathered[9],
+        vectors[0],
+        vectors[1],
+        vectors[2],
+        vectors[3],
     )
 
 

time: 1900 us -> 1150 us (0.61)
  waiting for transfers between devices: 1170 us -> 400 us
  starting transfers between devices: 15.2 us -> 163 us
  blocking collectives: 145 us -> 57.1 us
  local copies, waits for them, and re-layouts: 200 us -> 164 us
  matrix products: 234 us -> 201 us
  other arithmetic: 113 us -> 134 us
    reduce_scatter x6 -> x0, waiting for transfers between devices: 636 us -> none  [the longest x1 181 us: on_device(): lax.psum_scatter(grad_ffn_out, ('dp', 'tier'), scatter_dimension=1, tiled...]
    ppermute x0 -> x133, waiting for transfers between devices: none -> 295 us  [the longest x129 295 us: swap(): lax.ppermute(value, axis, [(i, i ^ step) for i in range(lax.axis_size(axi...]
    psum x4 -> x0, waiting for transfers between devices: 167 us -> none  [the longest x1 125 us: on_device(): lax.psum(jnp.einsum('rk,rc->kc', evicted, grad_squeezed, preferred_elemen...]
    all_gather x6 -> x0, waiting for transfers between devices: 156 us -> none  [the longest x1 74.8 us: on_device(): lax.all_gather(shares[6].astype(jnp.bfloat16), ('dp', 'tier'), axis=0, ti...]
    ppermute x0 -> x133, starting transfers between devices: none -> 148 us  [the longest x129 147 us: swap(): lax.ppermute(value, axis, [(i, i ^ step) for i in range(lax.axis_size(axi...]
    unnamed x2 -> x0, blocking collectives: 117 us -> none
    all_gather x1, waiting for transfers between devices: 41.4 us -> 0.01 us  [on_device(): normed_full = lax.all_gather(normed_own, 'tier', axis=1, tiled=True)]
    psum x1, blocking collectives: 2.47 us -> 39.4 us  [on_device(): lax.psum(jnp.stack([grad_gain_attn, grad_bias_attn, 0.5 * grad_gain_ffn,...]
  transfers between devices with their start and end apart: 24 -> 141, of which waited for: 19 -> 81; matrix products, arithmetic and copies ran while one was open for 10% -> 38% of each run, Pallas kernels for 0% -> 0%
where the time goes in v1:
time: 1150 us; the launch traced here: 1140 us
  waiting for transfers between devices  400 us (35%)
  matrix products  201 us (17%)
  local copies, waits for them, and re-layouts  164 us (14%)
  starting transfers between devices  163 us (14%)
  other arithmetic  134 us (12%)
  blocking collectives  57.1 us (5%)
  between operations  16.4 us (1%)
    ppermute x129, waiting for transfers between devices, swap(): lax.ppermute(value, axis, [(i, i ^ step) for i in range(lax.axis_size(axi...  295 us
    ppermute x129, starting transfers between devices, swap(): lax.ppermute(value, axis, [(i, i ^ step) for i in range(lax.axis_size(axi...  147 us
    ppermute x1, waiting for transfers between devices, from_behind(): return lax.ppermute(value, axis, pairs)  89 us
    dot_general x19, matrix products, product(): jnp.dot(first_operand, second_operand, preferred_element_type=jnp.float32)  60.4 us
    psum x1, blocking collectives, on_device(): lax.psum(jnp.stack([grad_gain_attn, grad_bias_attn, 0.5 * grad_gain_ffn,...  39.4 us
    dynamic_update_slice x24, local copies, waits for them, and re-layouts, on_device(): lax.map(attend, (normed_full, stored_low, seg_len, counts))  34.4 us
    dynamic_slice x30, local copies, waits for them, and re-layouts, on_device(): lax.map(attend_back, (queries, memory_keys, memory_values, segment_keys,...  27.1 us
    dot_general x6, matrix products, scores_of(): jnp.einsum('hqd,hkd->hqk', queries, key_heads, preferred_element_type=jnp...  25.8 us
  transfers between devices with their start and end apart: 141, of which 81 were waited for; matrix products, arithmetic and copies ran while one was open for 38% of the time, Pallas kernels for 0%

profile of v1, /device:TPU:0, one launch (start us, length us, event | category | flops | bytes accessed | tf_op | source)
XLA Modules:
  0.0 1137.3 jit_solution(12069305968141670605)
XLA Ops:
  11.5 6.7 collective-permute-start.2
  28.8 89.0 %collective-permute-done.2 = bf16[3,510,1024]{2,1,0:T(8,128)(2,1)} collective-permute-done((bf16[3,510,1024]{2,1,0:T(8,128)(2,1)}, bf16[3,510,1024]{2,1,0:T(8,128)(2,1)}, u32[]{:S(2)}, u32[]{:S(2)}) %collective-permute-start.2) | collective-permute-done | bytes 3133472 | tf_op jit(solution)/shard_map/ppermute | solution.py:20
  119.8 5.2 reshape.464
  131.6 132.0 %while.46 = (s32[]{:T(128)}, f32[3,512,512]{1,2,0:T(8,128)}, f32[3,512,4]{1,2,0:T(4,128)}, bf16[3,512,512]{2,1,0:T(8,128)(2,1)}, bf16[3,512,512]{2,1,0:T(8,128)(...) while((s32[]{:T(128)}, f32[3,512,512]{1,2,0:T(8,128)}, ...), condition=%wide.region_11.12_spmd.clone, body=%wide.region_4.11_spmd.sunk.clone | while | flops 3787736064 | bytes 121763872 | solution.py:245
  144.6 24.6 %conditional.6 = (f32[1,512,512]{1,2,0:T(8,128)}, f32[1,512,4]{1,2,0:T(4,128)S(1)}, bf16[1,512,512]{2,1,0:T(8,128)(2,1)}, bf16[1,512,512]{2,1,0:T(8,128)(2,1)}) conditional(s32[]{:T(128)} %convert_element_type.1581, (pred[1,512]{1,0:T(4,128)(4,1)S(1)}, bf16[512,512]{1,0:T(8,128)(2,1)}, bf16[512,512]{1,0:T(8,128)(2,1)}, ...), branch_computations={%region_5.7_spmd, %region_8.10_spmd} | conditional | flops 2176336384 | bytes 89234136 | solution.py:231
  162.1 7.1 fusion.15
  188.4 24.6 %conditional.6 = (f32[1,512,512]{1,2,0:T(8,128)}, f32[1,512,4]{1,2,0:T(4,128)S(1)}, bf16[1,512,512]{2,1,0:T(8,128)(2,1)}, bf16[1,512,512]{2,1,0:T(8,128)(2,1)}) conditional(s32[]{:T(128)} %convert_element_type.1581, (pred[1,512]{1,0:T(4,128)(4,1)S(1)}, bf16[512,512]{1,0:T(8,128)(2,1)}, bf16[512,512]{1,0:T(8,128)(2,1)}, ...), branch_computations={%region_5.7_spmd, %region_8.10_spmd} | conditional | flops 2176336384 | bytes 89234136 | solution.py:231
  206.0 7.1 fusion.15
  232.3 24.6 %conditional.6 = (f32[1,512,512]{1,2,0:T(8,128)}, f32[1,512,4]{1,2,0:T(4,128)S(1)}, bf16[1,512,512]{2,1,0:T(8,128)(2,1)}, bf16[1,512,512]{2,1,0:T(8,128)(2,1)}) conditional(s32[]{:T(128)} %convert_element_type.1581, (pred[1,512]{1,0:T(4,128)(4,1)S(1)}, bf16[512,512]{1,0:T(8,128)(2,1)}, bf16[512,512]{1,0:T(8,128)(2,1)}, ...), branch_computations={%region_5.7_spmd, %region_8.10_spmd} | conditional | flops 2176336384 | bytes 89234136 | solution.py:231
  249.9 7.1 fusion.15
  273.8 8.5 copy.261
  282.3 5.3 all-to-all-start
  307.2 5.0 mul.527
  312.3 7.0 collective-permute-done.131
  334.1 5.2 dot_general.139
  342.9 4.9 all-gather
  347.8 5.9 collective-permute-done.133
  365.0 4.0 fusion.121
  369.0 7.3 fusion.83
  376.3 4.4 bitcast_convert_fusion
  384.6 4.6 bitcast_convert_fusion.1
  393.1 11.8 %collective-permute-done.108 = bf16[256,1024]{1,0:T(8,128)(2,1)S(1)} collective-permute-done((bf16[256,1024]{1,0:T(8,128)(2,1)S(1)}, bf16[256,1024]{1,0:T(8,128)(2,1)S(1)}, u32[]{:S(2)}, u32[]{:S(2)}) %collective-permute-start.108) | collective-permute-done | bytes 524320 | tf_op jit(solution)/shard_map/ppermute | solution.py:40
  406.7 8.5 collective-permute-done.87
  415.9 6.8 collective-permute-done.109
  425.2 20.9 %collective-permute-done.88 = bf16[64,2048]{1,0:T(8,128)(2,1)S(1)} collective-permute-done((bf16[64,2048]{1,0:T(8,128)(2,1)S(1)}, bf16[64,2048]{1,0:T(8,128)(2,1)S(1)}, u32[]{:S(2)}, u32[]{:S(2)}) %collective-permute-start.88) | collective-permute-done | bytes 262176 | tf_op jit(solution)/shard_map/ppermute | solution.py:40
  450.6 16.0 %collective-permute-done.101 = bf16[192,2048]{1,0:T(8,128)(2,1)S(1)} collective-permute-done((bf16[192,2048]{1,0:T(8,128)(2,1)S(1)}, bf16[192,2048]{1,0:T(8,128)(2,1)S(1)}, u32[]{:S(2)}, u32[]{:S(2)}) %collective-permute-start.101) | collective-permute-done | bytes 786464 | tf_op jit(solution)/shard_map/ppermute | solution.py:40
  471.0 6.0 collective-permute-done.89
  480.6 7.0 collective-permute-done.111
  487.6 7.2 collective-permute-done.90
  495.2 8.8 collective-permute-done.95
  505.0 4.5 collective-permute-done.112
  516.3 5.4 collective-permute-done.96
  522.4 5.7 collective-permute-done.103
  554.3 12.7 %all_gather.15 = f32[3,512,4]{2,1,0:T(8,128)S(1)} all-gather(f32[3,256,4]{2,1,0:T(8,128)S(1)} %reduce_sum.220), channel_id=1, replica_groups=mesh['dp'=8,'tier'=2,'head'=2] {'tier'}, dimensions={1}, use_global_device_ids=true | all-gather | bytes 36864 | tf_op jit(solution)/shard_map/all_gather | solution.py:321
  579.6 11.6 %collective-permute-done.68 = bf16[64,1024]{1,0:T(8,128)(2,1)S(1)} collective-permute-done((bf16[64,1024]{1,0:T(8,128)(2,1)S(1)}, bf16[64,1024]{1,0:T(8,128)(2,1)S(1)}, u32[]{:S(2)}, u32[]{:S(2)}) %collective-permute-start.68) | collective-permute-done | bytes 131104 | tf_op jit(solution)/shard_map/ppermute | solution.py:40
  600.2 5.2 collective-permute-done.98
  609.1 10.1 all-gather.6.cloned.1.call-done
  619.1 147.9 %while.47 = (s32[]{:T(128)}, bf16[3,512,512]{1,2,0:T(8,128)(2,1)}, bf16[3,512,512]{1,2,0:T(8,128)(2,1)}, bf16[3,512,512]{1,2,0:T(8,128)(2,1)}, bf16[3,512,512]{1...) while((s32[]{:T(128)}, bf16[3,512,512]{1,2,0:T(8,128)(2,1)}, ...), condition=%wide.region_24.25_spmd.clone, body=%wide.region_18.24_spmd.sunk.clone | while | flops 2727873536 | bytes 145370224 | solution.py:385
  630.5 32.9 %conditional.7 = (bf16[1,512,512]{1,2,0:T(8,128)(2,1)S(1)}, bf16[1,512,512]{1,2,0:T(8,128)(2,1)}, bf16[1,512,512]{1,2,0:T(8,128)(2,1)S(1)}, bf16[1,512,512]{1,2,0:T(8,128)(2,1)}, bf16[1,512,512]{1,2,0:T(8,128)(2,1)S(1)}) conditional(s32[]{:T(128)} %convert_element_type.1583, (pred[1,512]{1,0:T(4,128)(4,1)S(1)}, bf16[512,512]{0,1:T(8,128)(2,1)S(1)}, ...), branch_computations={%region_20.21_spmd, %region_22.23_spmd} | conditional | flops 2726820352 | bytes 121690848 | solution.py:382
  635.8 5.9 fusion.59
  645.3 6.2 fusion.43
  651.5 4.9 fusion.42
  679.6 32.9 %conditional.7 = (bf16[1,512,512]{1,2,0:T(8,128)(2,1)S(1)}, bf16[1,512,512]{1,2,0:T(8,128)(2,1)}, bf16[1,512,512]{1,2,0:T(8,128)(2,1)S(1)}, bf16[1,512,512]{1,2,0:T(8,128)(2,1)}, bf16[1,512,512]{1,2,0:T(8,128)(2,1)S(1)}) conditional(s32[]{:T(128)} %convert_element_type.1583, (pred[1,512]{1,0:T(4,128)(4,1)S(1)}, bf16[512,512]{0,1:T(8,128)(2,1)S(1)}, ...), branch_computations={%region_20.21_spmd, %region_22.23_spmd} | conditional | flops 2726820352 | bytes 121690848 | solution.py:382
  684.8 5.9 fusion.59
  694.4 6.2 fusion.43
  700.6 4.9 fusion.42
  728.7 32.9 %conditional.7 = (bf16[1,512,512]{1,2,0:T(8,128)(2,1)S(1)}, bf16[1,512,512]{1,2,0:T(8,128)(2,1)}, bf16[1,512,512]{1,2,0:T(8,128)(2,1)S(1)}, bf16[1,512,512]{1,2,0:T(8,128)(2,1)}, bf16[1,512,512]{1,2,0:T(8,128)(2,1)S(1)}) conditional(s32[]{:T(128)} %convert_element_type.1583, (pred[1,512]{1,0:T(4,128)(4,1)S(1)}, bf16[512,512]{0,1:T(8,128)(2,1)S(1)}, ...), branch_computations={%region_20.21_spmd, %region_22.23_spmd} | conditional | flops 2726820352 | bytes 121690848 | solution.py:382
  733.9 5.9 fusion.59
  743.5 6.2 fusion.43
  749.7 4.9 fusion.42
  784.0 4.8 collective-permute-done.82
  802.8 4.1 collective-permute-done.83
  819.6 5.3 collective-permute-done.84
  832.6 4.5 collective-permute-done.79
  839.2 4.8 collective-permute-done.85
  854.9 9.0 collective-permute-done.121
  866.4 5.9 collective-permute-done.100
  874.7 3.9 maximum_convert_fusion.1
  878.6 3.9 maximum_convert_fusion
  892.1 4.8 fusion.75
  934.5 4.4 collective-permute-done.48
  1032.2 6.7 collective-permute-done.58
  1085.9 39.4 %psum.7 = f32[4,1024]{1,0:T(4,128)S(1)} all-reduce(f32[4,1024]{1,0:T(4,128)S(1)} %pad_maximum_fusion.1), channel_id=1, replica_groups=mesh['dp'=8,'tier'=2,'head'=2] {'dp','tier','head'}, use_global_device_ids=true, to_apply=%region_36.37 | all-reduce | flops 4096 | bytes 32768 | tf_op jit(solution)/shard_map/psum | solution.py:444
  1126.0 4.5 fusion.104
  (937 shorter events, 629.7 us)
Async XLA Ops:
  7.2 124.4 %all-gather.4.cloned.1.call-start = ((), (), s32[]{:S(2)}) async-start(), calls=%async_computation.5 | async-start | bytes 4718592 | tf_op jit(solution)/shard_map/all_gather | solution.py:197
  11.5 106.3 %collective-permute-start.2 = (bf16[3,510,1024]{2,1,0:T(8,128)(2,1)}, bf16[3,510,1024]{2,1,0:T(8,128)(2,1)}, u32[]{:S(2)}, u32[]{:S(2)}) collective-permute-start(bf16[3,510,1024]{2,1,0:T(8,128)(2,1)} %slice_select_fusion), channel_id=1, source_target_pairs={{0,2},{1,3},{4,6},{5,7},{8,10},{9,11},{12,14},{13,15},{16,18},{17,... | collective-permute-start | bytes 9400328 | tf_op jit(solution)/shard_map/ppermute | solution.py:20
  130.1 157.5 %collective-permute-start.129 = (bf16[1536,256]{1,0:T(8,128)(2,1)}, bf16[1536,256]{1,0:T(8,128)(2,1)}, u32[]{:S(2)}, u32[]{:S(2)}) collective-permute-start(bf16[1536,256]{1,0:T(8,128)(2,1)} %constant_dynamic-slice_fusion.8), channel_id=1, source_target_pairs={{0,4},{4,0},{8,12},{12,8},{16,20},{20,16},{24,28},{28,24},{1,5},{5... | collective-permute-start | bytes 2359304 | tf_op jit(solution)/shard_map/ppermute | solution.py:40
  270.5 11.8 %all-to-all-start.1 = ((f32[2,1,3072]{2,1,0:T(1,128)}), f32[2,1,3072]{2,1,0:T(1,128)S(1)}, u32[]{:S(2)}, u32[]{:S(2)}) async-start(f32[2,1,3072]{2,1,0:T(1,128)} %reshape.494), calls=%async_computation.1 | async-start | bytes 49152 | tf_op jit(solution)/shard_map/all_to_all | solution.py:249
  282.3 40.6 %all-to-all-start = ((f32[1,3,512,512]{3,0,1,2:T(1,128)}), f32[1,3,512,512]{3,0,1,2:T(1,128)}, u32[]{:S(2)}, u32[]{:S(2)}) async-start(f32[1,3,512,512]{3,0,1,2:T(1,128)} %copy.261), calls=%async_computation | async-start | bytes 6291456 | tf_op jit(solution)/shard_map/all_to_all | solution.py:248
  287.5 331.6 %all-gather.6.cloned.1.call-start = ((), (), s32[]{:S(2)}) async-start(), calls=%async_computation.6 | async-start | bytes 4718592 | tf_op jit(solution)/shard_map/all_gather | solution.py:320
  289.9 10.0 collective-permute-start.130
  301.1 18.2 %collective-permute-start.131 = (bf16[768,256]{1,0:T(8,128)(2,1)S(1)}, bf16[768,256]{1,0:T(8,128)(2,1)S(1)}, u32[]{:S(2)}, u32[]{:S(2)}) collective-permute-start(bf16[768,256]{1,0:T(8,128)(2,1)S(1)} %add_convert_fusion.10), channel_id=1, source_target_pairs={{0,16},{4,20},{8,24},{12,28},{16,0},{20,4},{24,8},{28,12},{1,17},{... | collective-permute-start | bytes 1179656 | tf_op jit(solution)/shard_map/ppermute | solution.py:40
  319.3 11.9 %collective-permute-start.132 = (bf16[768,256]{1,0:T(8,128)(2,1)S(1)}, bf16[768,256]{1,0:T(8,128)(2,1)}, u32[]{:S(2)}, u32[]{:S(2)}) collective-permute-start(bf16[768,256]{1,0:T(8,128)(2,1)S(1)} %add_convert_fusion.9), channel_id=1, source_target_pairs={{0,8},{4,12},{8,0},{12,4},{16,24},{20,28},{24,16},{28,20},{1,9},{5... | collective-permute-start | bytes 1179656 | tf_op jit(solution)/shard_map/ppermute | solution.py:40
  331.2 26.7 %collective-permute-start = (bf16[3,256,1024]{2,1,0:T(8,128)(2,1)}, bf16[3,256,1024]{2,1,0:T(8,128)(2,1)}, u32[]{:S(2)}, u32[]{:S(2)}) collective-permute-start(bf16[3,256,1024]{2,1,0:T(8,128)(2,1)} %convolution_convert_fusion.6), channel_id=1, source_target_pairs={{0,1},{1,0},{2,3},{3,2},{4,5},{5,4},{6,7},{7,6},{8,9},{9,8},{10,11... | collective-permute-start | bytes 4718600 | tf_op jit(solution)/shard_map/ppermute | solution.py:50
  333.5 20.3 %collective-permute-start.133 = (bf16[1536,256]{1,0:T(8,128)(2,1)}, bf16[1536,256]{1,0:T(8,128)(2,1)}, u32[]{:S(2)}, u32[]{:S(2)}) collective-permute-start(bf16[1536,256]{1,0:T(8,128)(2,1)} %maximum_select_fusion.11), channel_id=1, source_target_pairs={{0,4},{4,0},{8,12},{12,8},{16,20},{20,16},{24,28},{28,24},{1,5},{5... | collective-permute-start | bytes 2359304 | tf_op jit(solution)/shard_map/ppermute | solution.py:40
  389.4 152.2 %collective-permute-start.3 = (bf16[3,256,1024]{2,1,0:T(8,128)(2,1)S(1)}, bf16[3,256,1024]{2,1,0:T(8,128)(2,1)S(1)}, u32[]{:S(2)}, u32[]{:S(2)}) collective-permute-start(bf16[3,256,1024]{2,1,0:T(8,128)(2,1)S(1)} %fusion.118), channel_id=1, source_target_pairs={{0,1},{1,0},{2,3},{3,2},{4,5},{5,4},{6,7},{7,6},{8,9},{9,8},{10,11... | collective-permute-start | bytes 4718600 | tf_op jit(solution)/shard_map/ppermute | solution.py:50
  389.5 154.5 %collective-permute-start.1 = (bf16[3,256,1024]{2,1,0:T(8,128)(2,1)S(1)}, bf16[3,256,1024]{2,1,0:T(8,128)(2,1)S(1)}, u32[]{:S(2)}, u32[]{:S(2)}) collective-permute-start(bf16[3,256,1024]{2,1,0:T(8,128)(2,1)S(1)} %fusion.121), channel_id=1, source_target_pairs={{0,1},{1,0},{2,3},{3,2},{4,5},{5,4},{6,7},{7,6},{8,9},{9,8},{10,11... | collective-permute-start | bytes 4718600 | tf_op jit(solution)/shard_map/ppermute | solution.py:50
  390.0 14.8 %collective-permute-start.108 = (bf16[256,1024]{1,0:T(8,128)(2,1)S(1)}, bf16[256,1024]{1,0:T(8,128)(2,1)S(1)}, u32[]{:S(2)}, u32[]{:S(2)}) collective-permute-start(bf16[256,1024]{1,0:T(8,128)(2,1)S(1)} %constant_dynamic-slice_fusion.17), channel_id=1, source_target_pairs={{0,2},{2,0},{1,3},{3,1},{4,6},{6,4},{5,7},{7,5},{8,10},{10,8},{9,1... | collective-permute-start | bytes 1572872 | tf_op jit(solution)/shard_map/ppermute | solution.py:40
  390.5 32.9 %collective-permute-start.115 = (bf16[384,1024]{1,0:T(8,128)(2,1)S(1)}, bf16[384,1024]{1,0:T(8,128)(2,1)S(1)}, u32[]{:S(2)}, u32[]{:S(2)}) collective-permute-start(bf16[384,1024]{1,0:T(8,128)(2,1)S(1)} %constant_dynamic-slice_fusion.14), channel_id=1, source_target_pairs={{0,4},{4,0},{8,12},{12,8},{16,20},{20,16},{24,28},{28,24},{1,5},{5... | collective-permute-start | bytes 2359304 | tf_op jit(solution)/shard_map/ppermute | solution.py:40
  391.1 24.2 %collective-permute-start.87 = (bf16[128,2048]{1,0:T(8,128)(2,1)S(1)}, bf16[128,2048]{1,0:T(8,128)(2,1)S(1)}, u32[]{:S(2)}, u32[]{:S(2)}) collective-permute-start(bf16[128,2048]{1,0:T(8,128)(2,1)S(1)} %constant_dynamic-slice_fusion.26), channel_id=1, source_target_pairs={{0,2},{2,0},{1,3},{3,1},{4,6},{6,4},{5,7},{7,5},{8,10},{10,8},{9,1... | collective-permute-start | bytes 1572872 | tf_op jit(solution)/shard_map/ppermute | solution.py:40
  404.9 42.8 %collective-permute-start.122 = (bf16[384,1024]{1,0:T(8,128)(2,1)S(1)}, bf16[384,1024]{1,0:T(8,128)(2,1)S(1)}, u32[]{:S(2)}, u32[]{:S(2)}) collective-permute-start(bf16[384,1024]{1,0:T(8,128)(2,1)S(1)} %constant_dynamic-slice_fusion.11), channel_id=1, source_target_pairs={{0,8},{4,12},{8,0},{12,4},{16,24},{20,28},{24,16},{28,20},{1,9},{5... | collective-permute-start | bytes 2359304 | tf_op jit(solution)/shard_map/ppermute | solution.py:40
  422.7 25.9 %collective-permute-start.94 = (bf16[192,2048]{1,0:T(8,128)(2,1)S(1)}, bf16[192,2048]{1,0:T(8,128)(2,1)S(1)}, u32[]{:S(2)}, u32[]{:S(2)}) collective-permute-start(bf16[192,2048]{1,0:T(8,128)(2,1)S(1)} %constant_dynamic-slice_fusion.23), channel_id=1, source_target_pairs={{0,4},{4,0},{8,12},{12,8},{16,20},{20,16},{24,28},{28,24},{1,5},{5... | collective-permute-start | bytes 2359304 | tf_op jit(solution)/shard_map/ppermute | solution.py:40
  423.3 22.8 %collective-permute-start.88 = (bf16[64,2048]{1,0:T(8,128)(2,1)S(1)}, bf16[64,2048]{1,0:T(8,128)(2,1)S(1)}, u32[]{:S(2)}, u32[]{:S(2)}) collective-permute-start(bf16[64,2048]{1,0:T(8,128)(2,1)S(1)} %constant_dynamic-slice_fusion.25), channel_id=1, source_target_pairs={{0,4},{4,0},{8,12},{12,8},{16,20},{20,16},{24,28},{28,24},{1,5},{5... | collective-permute-start | bytes 786440 | tf_op jit(solution)/shard_map/ppermute | solution.py:40
  446.1 20.5 %collective-permute-start.101 = (bf16[192,2048]{1,0:T(8,128)(2,1)S(1)}, bf16[192,2048]{1,0:T(8,128)(2,1)S(1)}, u32[]{:S(2)}, u32[]{:S(2)}) collective-permute-start(bf16[192,2048]{1,0:T(8,128)(2,1)S(1)} %constant_dynamic-slice_fusion.20), channel_id=1, source_target_pairs={{0,8},{4,12},{8,0},{12,4},{16,24},{20,28},{24,16},{28,20},{1,9},{5... | collective-permute-start | bytes 2359304 | tf_op jit(solution)/shard_map/ppermute | solution.py:40
  447.7 21.6 %collective-permute-start.110 = (bf16[64,1024]{1,0:T(8,128)(2,1)S(1)}, bf16[64,1024]{1,0:T(8,128)(2,1)S(1)}, u32[]{:S(2)}, u32[]{:S(2)}) collective-permute-start(bf16[64,1024]{1,0:T(8,128)(2,1)S(1)} %constant_dynamic-slice_fusion.15), channel_id=1, source_target_pairs={{0,8},{4,12},{8,0},{12,4},{16,24},{20,28},{24,16},{28,20},{1,9},{5... | collective-permute-start | bytes 393224 | tf_op jit(solution)/shard_map/ppermute | solution.py:40
  448.6 55.8 %collective-permute-start.116 = (bf16[192,1024]{1,0:T(8,128)(2,1)S(1)}, bf16[192,1024]{1,0:T(8,128)(2,1)S(1)}, u32[]{:S(2)}, u32[]{:S(2)}) collective-permute-start(bf16[192,1024]{1,0:T(8,128)(2,1)S(1)} %constant_dynamic-slice_fusion.13), channel_id=1, source_target_pairs={{0,8},{4,12},{8,0},{12,4},{16,24},{20,28},{24,16},{28,20},{1,9},{5... | collective-permute-start | bytes 1179656 | tf_op jit(solution)/shard_map/ppermute | solution.py:40
  466.6 43.3 %collective-permute-start.123 = (bf16[192,1024]{1,0:T(8,128)(2,1)S(1)}, bf16[192,1024]{1,0:T(8,128)(2,1)S(1)}, u32[]{:S(2)}, u32[]{:S(2)}) collective-permute-start(bf16[192,1024]{1,0:T(8,128)(2,1)S(1)} %constant_dynamic-slice_fusion.10), channel_id=1, source_target_pairs={{0,2},{2,0},{1,3},{3,1},{4,6},{6,4},{5,7},{7,5},{8,10},{10,8},{9,1... | collective-permute-start | bytes 1179656 | tf_op jit(solution)/shard_map/ppermute | solution.py:40
  477.0 10.6 collective-permute-start.111
  509.9 26.9 %collective-permute-start.113 = (bf16[128,1024]{1,0:T(8,128)(2,1)S(1)}, bf16[128,1024]{1,0:T(8,128)(2,1)S(1)}, u32[]{:S(2)}, u32[]{:S(2)}) collective-permute-start(bf16[128,1024]{1,0:T(8,128)(2,1)S(1)} %maximum_select_fusion.31), channel_id=1, source_target_pairs={{0,4},{4,0},{8,12},{12,8},{16,20},{20,16},{24,28},{28,24},{1,5},{5... | collective-permute-start | bytes 786440 | tf_op jit(solution)/shard_map/ppermute | solution.py:40
  513.9 14.8 %collective-permute-start.117 = (bf16[96,1024]{1,0:T(8,128)(2,1)S(1)}, bf16[96,1024]{1,0:T(8,128)(2,1)S(1)}, u32[]{:S(2)}, u32[]{:S(2)}) collective-permute-start(bf16[96,1024]{1,0:T(8,128)(2,1)S(1)} %constant_dynamic-slice_fusion.12), channel_id=1, source_target_pairs={{0,2},{2,0},{1,3},{3,1},{4,6},{6,4},{5,7},{7,5},{8,10},{10,8},{9,1... | collective-permute-start | bytes 589832 | tf_op jit(solution)/shard_map/ppermute | solution.py:40
  533.8 34.2 %collective-permute-start.118 = (bf16[96,1024]{1,0:T(8,128)(2,1)}, bf16[96,1024]{1,0:T(8,128)(2,1)}, u32[]{:S(2)}, u32[]{:S(2)}) collective-permute-start(bf16[96,1024]{1,0:T(8,128)(2,1)} %add_convert_fusion.20), channel_id=1, source_target_pairs={{0,16},{4,20},{8,24},{12,28},{16,0},{20,4},{24,8},{28,12},{1,17},{... | collective-permute-start | bytes 589832 | tf_op jit(solution)/shard_map/ppermute | solution.py:40
  536.8 35.5 %collective-permute-start.125 = (bf16[96,1024]{1,0:T(8,128)(2,1)}, bf16[96,1024]{1,0:T(8,128)(2,1)}, u32[]{:S(2)}, u32[]{:S(2)}) collective-permute-start(bf16[96,1024]{1,0:T(8,128)(2,1)} %add_convert_fusion.18), channel_id=1, source_target_pairs={{0,16},{4,20},{8,24},{12,28},{16,0},{20,4},{24,8},{28,12},{1,17},{... | collective-permute-start | bytes 589832 | tf_op jit(solution)/shard_map/ppermute | solution.py:40
  538.4 39.2 %collective-permute-start.97 = (bf16[48,2048]{1,0:T(8,128)(2,1)S(1)}, bf16[48,2048]{1,0:T(8,128)(2,1)}, u32[]{:S(2)}, u32[]{:S(2)}) collective-permute-start(bf16[48,2048]{1,0:T(8,128)(2,1)S(1)} %add_convert_fusion.24), channel_id=1, source_target_pairs={{0,16},{4,20},{8,24},{12,28},{16,0},{20,4},{24,8},{28,12},{1,17},{... | collective-permute-start | bytes 589832 | tf_op jit(solution)/shard_map/ppermute | solution.py:40
  541.6 33.8 %collective-permute-start.104 = (bf16[48,2048]{1,0:T(8,128)(2,1)S(1)}, bf16[48,2048]{1,0:T(8,128)(2,1)}, u32[]{:S(2)}, u32[]{:S(2)}) collective-permute-start(bf16[48,2048]{1,0:T(8,128)(2,1)S(1)} %add_convert_fusion.22), channel_id=1, source_target_pairs={{0,16},{4,20},{8,24},{12,28},{16,0},{20,4},{24,8},{28,12},{1,17},{... | collective-permute-start | bytes 589832 | tf_op jit(solution)/shard_map/ppermute | solution.py:40
  544.1 268.6 %collective-permute-start.114 = (bf16[256,1024]{1,0:T(8,128)(2,1)}, bf16[256,1024]{1,0:T(8,128)(2,1)}, u32[]{:S(2)}, u32[]{:S(2)}) collective-permute-start(bf16[256,1024]{1,0:T(8,128)(2,1)} %maximum_select_fusion.13), channel_id=1, source_target_pairs={{0,2},{2,0},{1,3},{3,1},{4,6},{6,4},{5,7},{7,5},{8,10},{10,8},{9,1... | collective-permute-start | bytes 1572872 | tf_op jit(solution)/shard_map/ppermute | solution.py:40
  567.9 329.1 %reduce-scatter.8.cloned.1.call-start = ((), (), s32[]{:S(2)}) async-start(), calls=%async_computation.9 | async-start | bytes 2359296 | tf_op jit(solution)/shard_map/reduce_scatter | solution.py:410
  568.0 240.7 %collective-permute-start.93 = (bf16[128,2048]{1,0:T(8,128)(2,1)}, bf16[128,2048]{1,0:T(8,128)(2,1)}, u32[]{:S(2)}, u32[]{:S(2)}) collective-permute-start(bf16[128,2048]{1,0:T(8,128)(2,1)} %maximum_select_fusion.12), channel_id=1, source_target_pairs={{0,2},{2,0},{1,3},{3,1},{4,6},{6,4},{5,7},{7,5},{8,10},{10,8},{9,1... | collective-permute-start | bytes 1572872 | tf_op jit(solution)/shard_map/ppermute | solution.py:40
  572.3 25.0 %collective-permute-start.119 = (bf16[96,1024]{1,0:T(8,128)(2,1)S(1)}, bf16[96,1024]{1,0:T(8,128)(2,1)S(1)}, u32[]{:S(2)}, u32[]{:S(2)}) collective-permute-start(bf16[96,1024]{1,0:T(8,128)(2,1)S(1)} %add_convert_fusion.19), channel_id=1, source_target_pairs={{0,2},{2,0},{1,3},{3,1},{4,6},{6,4},{5,7},{7,5},{8,10},{10,8},{9,1... | collective-permute-start | bytes 589832 | tf_op jit(solution)/shard_map/ppermute | solution.py:40
  575.5 20.3 %collective-permute-start.126 = (bf16[96,1024]{1,0:T(8,128)(2,1)S(1)}, bf16[96,1024]{1,0:T(8,128)(2,1)S(1)}, u32[]{:S(2)}, u32[]{:S(2)}) collective-permute-start(bf16[96,1024]{1,0:T(8,128)(2,1)S(1)} %add_convert_fusion.17), channel_id=1, source_target_pairs={{0,4},{4,0},{8,12},{12,8},{16,20},{20,16},{24,28},{28,24},{1,5},{5... | collective-permute-start | bytes 589832 | tf_op jit(solution)/shard_map/ppermute | solution.py:40
  577.6 13.5 %collective-permute-start.68 = (bf16[64,1024]{1,0:T(8,128)(2,1)S(1)}, bf16[64,1024]{1,0:T(8,128)(2,1)S(1)}, u32[]{:S(2)}, u32[]{:S(2)}) collective-permute-start(bf16[64,1024]{1,0:T(8,128)(2,1)S(1)} %constant_dynamic-slice_fusion.33), channel_id=1, source_target_pairs={{0,2},{2,0},{1,3},{3,1},{4,6},{6,4},{5,7},{7,5},{8,10},{10,8},{9,1... | collective-permute-start | bytes 393224 | tf_op jit(solution)/shard_map/ppermute | solution.py:40
  595.8 12.3 %collective-permute-start.105 = (bf16[48,2048]{1,0:T(8,128)(2,1)S(1)}, bf16[48,2048]{1,0:T(8,128)(2,1)S(1)}, u32[]{:S(2)}, u32[]{:S(2)}) collective-permute-start(bf16[48,2048]{1,0:T(8,128)(2,1)S(1)} %add_convert_fusion.21), channel_id=1, source_target_pairs={{0,4},{4,0},{8,12},{12,8},{16,20},{20,16},{24,28},{28,24},{1,5},{5... | collective-permute-start | bytes 589832 | tf_op jit(solution)/shard_map/ppermute | solution.py:40
  597.3 169.8 %collective-permute-start.75 = (bf16[96,1024]{1,0:T(8,128)(2,1)}, bf16[96,1024]{1,0:T(8,128)(2,1)}, u32[]{:S(2)}, u32[]{:S(2)}) collective-permute-start(bf16[96,1024]{1,0:T(8,128)(2,1)} %constant_dynamic-slice_fusion.30), channel_id=1, source_target_pairs={{0,4},{4,0},{8,12},{12,8},{16,20},{20,16},{24,28},{28,24},{1,5},{5... | collective-permute-start | bytes 589832 | tf_op jit(solution)/shard_map/ppermute | solution.py:40
  605.4 163.0 %collective-permute-start.81 = (bf16[96,1024]{1,0:T(8,128)(2,1)}, bf16[96,1024]{1,0:T(8,128)(2,1)}, u32[]{:S(2)}, u32[]{:S(2)}) collective-permute-start(bf16[96,1024]{1,0:T(8,128)(2,1)} %constant_dynamic-slice_fusion.28), channel_id=1, source_target_pairs={{0,8},{4,12},{8,0},{12,4},{16,24},{20,28},{24,16},{28,20},{1,9},{5... | collective-permute-start | bytes 589832 | tf_op jit(solution)/shard_map/ppermute | solution.py:40
  608.1 236.9 %collective-permute-start.120 = (bf16[192,1024]{1,0:T(8,128)(2,1)}, bf16[192,1024]{1,0:T(8,128)(2,1)}, u32[]{:S(2)}, u32[]{:S(2)}) collective-permute-start(bf16[192,1024]{1,0:T(8,128)(2,1)} %maximum_select_fusion.24), channel_id=1, source_target_pairs={{0,8},{4,12},{8,0},{12,4},{16,24},{20,28},{24,16},{28,20},{1,9},{5... | collective-permute-start | bytes 1179656 | tf_op jit(solution)/shard_map/ppermute | solution.py:40
  767.1 134.5 %reduce-scatter.6.cloned.1.call-start = ((), (), s32[]{:S(2)}) async-start(), calls=%async_computation.8 | async-start | bytes 2359296 | tf_op jit(solution)/shard_map/reduce_scatter | solution.py:407
  767.2 79.7 %collective-permute-start.127 = (bf16[192,1024]{1,0:T(8,128)(2,1)}, bf16[192,1024]{1,0:T(8,128)(2,1)S(1)}, u32[]{:S(2)}, u32[]{:S(2)}) collective-permute-start(bf16[192,1024]{1,0:T(8,128)(2,1)} %maximum_select_fusion.25), channel_id=1, source_target_pairs={{0,2},{2,0},{1,3},{3,1},{4,6},{6,4},{5,7},{7,5},{8,10},{10,8},{9,1... | collective-permute-start | bytes 1179656 | tf_op jit(solution)/shard_map/ppermute | solution.py:40
  806.9 42.4 %collective-permute-start.99 = (bf16[96,2048]{1,0:T(8,128)(2,1)S(1)}, bf16[96,2048]{1,0:T(8,128)(2,1)S(1)}, u32[]{:S(2)}, u32[]{:S(2)}) collective-permute-start(bf16[96,2048]{1,0:T(8,128)(2,1)S(1)} %copy-done.31), channel_id=1, source_target_pairs={{0,8},{4,12},{8,0},{12,4},{16,24},{20,28},{24,16},{28,20},{1,9},{5... | collective-permute-start | bytes 1179656 | tf_op jit(solution)/shard_map/ppermute | solution.py:40
  808.7 42.8 %collective-permute-start.106 = (bf16[96,2048]{1,0:T(8,128)(2,1)S(1)}, bf16[96,2048]{1,0:T(8,128)(2,1)}, u32[]{:S(2)}, u32[]{:S(2)}) collective-permute-start(bf16[96,2048]{1,0:T(8,128)(2,1)S(1)} %copy-done.32), channel_id=1, source_target_pairs={{0,2},{2,0},{1,3},{3,1},{4,6},{6,4},{5,7},{7,5},{8,10},{10,8},{9,1... | collective-permute-start | bytes 1179656 | tf_op jit(solution)/shard_map/ppermute | solution.py:40
  827.6 79.8 %reduce-scatter.4.cloned.1.call-start = ((), (), s32[]{:S(2)}) async-start(), calls=%async_computation.7 | async-start | bytes 2359296 | tf_op jit(solution)/shard_map/reduce_scatter | solution.py:404
  846.9 16.9 %collective-permute-start.121 = (bf16[384,1024]{1,0:T(8,128)(2,1)S(1)}, bf16[384,1024]{1,0:T(8,128)(2,1)S(1)}, u32[]{:S(2)}, u32[]{:S(2)}) collective-permute-start(bf16[384,1024]{1,0:T(8,128)(2,1)S(1)} %maximum_select_fusion.9), channel_id=1, source_target_pairs={{0,4},{4,0},{8,12},{12,8},{16,20},{20,16},{24,28},{28,24},{1,5},{5... | collective-permute-start | bytes 2359304 | tf_op jit(solution)/shard_map/ppermute | solution.py:40
  849.3 16.3 %collective-permute-start.128 = (bf16[384,1024]{1,0:T(8,128)(2,1)S(1)}, bf16[384,1024]{1,0:T(8,128)(2,1)S(1)}, u32[]{:S(2)}, u32[]{:S(2)}) collective-permute-start(bf16[384,1024]{1,0:T(8,128)(2,1)S(1)} %maximum_select_fusion.10), channel_id=1, source_target_pairs={{0,8},{4,12},{8,0},{12,4},{16,24},{20,28},{24,16},{28,20},{1,9},{5... | collective-permute-start | bytes 2359304 | tf_op jit(solution)/shard_map/ppermute | solution.py:40
  851.5 20.8 %collective-permute-start.100 = (bf16[192,2048]{1,0:T(8,128)(2,1)S(1)}, bf16[192,2048]{1,0:T(8,128)(2,1)S(1)}, u32[]{:S(2)}, u32[]{:S(2)}) collective-permute-start(bf16[192,2048]{1,0:T(8,128)(2,1)S(1)} %maximum_select_fusion.7), channel_id=1, source_target_pairs={{0,4},{4,0},{8,12},{12,8},{16,20},{20,16},{24,28},{28,24},{1,5},{5... | collective-permute-start | bytes 2359304 | tf_op jit(solution)/shard_map/ppermute | solution.py:40
  853.0 21.1 %collective-permute-start.107 = (bf16[192,2048]{1,0:T(8,128)(2,1)S(1)}, bf16[192,2048]{1,0:T(8,128)(2,1)S(1)}, u32[]{:S(2)}, u32[]{:S(2)}) collective-permute-start(bf16[192,2048]{1,0:T(8,128)(2,1)S(1)} %maximum_select_fusion.8), channel_id=1, source_target_pairs={{0,8},{4,12},{8,0},{12,4},{16,24},{20,28},{24,16},{28,20},{1,9},{5... | collective-permute-start | bytes 2359304 | tf_op jit(solution)/shard_map/ppermute | solution.py:40
  916.8 167.2 %collective-permute-start.4 = (bf16[3,256,1024]{2,1,0:T(8,128)(2,1)S(1)}, bf16[3,256,1024]{2,1,0:T(8,128)(2,1)S(1)}, u32[]{:S(2)}, u32[]{:S(2)}) collective-permute-start(bf16[3,256,1024]{2,1,0:T(8,128)(2,1)S(1)} %add_convert_fusion), channel_id=1, source_target_pairs={{0,1},{1,0},{2,3},{3,2},{4,5},{5,4},{6,7},{7,6},{8,9},{9,8},{10,11... | collective-permute-start | bytes 4718600 | tf_op jit(solution)/shard_map/ppermute | solution.py:50
  917.3 14.9 %collective-permute-start.54 = (bf16[192,512]{1,0:T(8,128)(2,1)S(1)}, bf16[192,512]{1,0:T(8,128)(2,1)S(1)}, u32[]{:S(2)}, u32[]{:S(2)}) collective-permute-start(bf16[192,512]{1,0:T(8,128)(2,1)S(1)} %constant_dynamic-slice_fusion.39), channel_id=1, source_target_pairs={{0,4},{4,0},{8,12},{12,8},{16,20},{20,16},{24,28},{28,24},{1,5},{5... | collective-permute-start | bytes 589832 | tf_op jit(solution)/shard_map/ppermute | solution.py:40
  919.1 14.8 %collective-permute-start.61 = (bf16[192,512]{1,0:T(8,128)(2,1)S(1)}, bf16[192,512]{1,0:T(8,128)(2,1)S(1)}, u32[]{:S(2)}, u32[]{:S(2)}) collective-permute-start(bf16[192,512]{1,0:T(8,128)(2,1)S(1)} %constant_dynamic-slice_fusion.36), channel_id=1, source_target_pairs={{0,8},{4,12},{8,0},{12,4},{16,24},{20,28},{24,16},{28,20},{1,9},{5... | collective-permute-start | bytes 589832 | tf_op jit(solution)/shard_map/ppermute | solution.py:40
  922.8 20.9 %collective-permute-start.33 = (bf16[192,512]{1,0:T(8,128)(2,1)S(1)}, bf16[192,512]{1,0:T(8,128)(2,1)S(1)}, u32[]{:S(2)}, u32[]{:S(2)}) collective-permute-start(bf16[192,512]{1,0:T(8,128)(2,1)S(1)} %constant_dynamic-slice_fusion.48), channel_id=1, source_target_pairs={{0,4},{4,0},{8,12},{12,8},{16,20},{20,16},{24,28},{28,24},{1,5},{5... | collective-permute-start | bytes 589832 | tf_op jit(solution)/shard_map/ppermute | solution.py:40
  930.7 14.9 %collective-permute-start.40 = (bf16[192,512]{1,0:T(8,128)(2,1)S(1)}, bf16[192,512]{1,0:T(8,128)(2,1)S(1)}, u32[]{:S(2)}, u32[]{:S(2)}) collective-permute-start(bf16[192,512]{1,0:T(8,128)(2,1)S(1)} %constant_dynamic-slice_fusion.45), channel_id=1, source_target_pairs={{0,8},{4,12},{8,0},{12,4},{16,24},{20,28},{24,16},{28,20},{1,9},{5... | collective-permute-start | bytes 589832 | tf_op jit(solution)/shard_map/ppermute | solution.py:40
  932.2 18.0 %collective-permute-start.12 = (bf16[192,512]{1,0:T(8,128)(2,1)S(1)}, bf16[192,512]{1,0:T(8,128)(2,1)S(1)}, u32[]{:S(2)}, u32[]{:S(2)}) collective-permute-start(bf16[192,512]{1,0:T(8,128)(2,1)S(1)} %constant_dynamic-slice_fusion.57), channel_id=1, source_target_pairs={{0,4},{4,0},{8,12},{12,8},{16,20},{20,16},{24,28},{28,24},{1,5},{5... | collective-permute-start | bytes 589832 | tf_op jit(solution)/shard_map/ppermute | solution.py:40
  948.0 38.9 %collective-permute-start.55 = (bf16[96,512]{1,0:T(8,128)(2,1)S(1)}, bf16[96,512]{1,0:T(8,128)(2,1)S(1)}, u32[]{:S(2)}, u32[]{:S(2)}) collective-permute-start(bf16[96,512]{1,0:T(8,128)(2,1)S(1)} %constant_dynamic-slice_fusion.38), channel_id=1, source_target_pairs={{0,8},{4,12},{8,0},{12,4},{16,24},{20,28},{24,16},{28,20},{1,9},{5... | collective-permute-start | bytes 294920 | tf_op jit(solution)/shard_map/ppermute | solution.py:40
  950.1 37.1 %collective-permute-start.62 = (bf16[96,512]{1,0:T(8,128)(2,1)S(1)}, bf16[96,512]{1,0:T(8,128)(2,1)S(1)}, u32[]{:S(2)}, u32[]{:S(2)}) collective-permute-start(bf16[96,512]{1,0:T(8,128)(2,1)S(1)} %constant_dynamic-slice_fusion.35), channel_id=1, source_target_pairs={{0,2},{2,0},{1,3},{3,1},{4,6},{6,4},{5,7},{7,5},{8,10},{10,8},{9,1... | collective-permute-start | bytes 294920 | tf_op jit(solution)/shard_map/ppermute | solution.py:40
  952.5 36.3 %collective-permute-start.34 = (bf16[96,512]{1,0:T(8,128)(2,1)S(1)}, bf16[96,512]{1,0:T(8,128)(2,1)S(1)}, u32[]{:S(2)}, u32[]{:S(2)}) collective-permute-start(bf16[96,512]{1,0:T(8,128)(2,1)S(1)} %constant_dynamic-slice_fusion.47), channel_id=1, source_target_pairs={{0,8},{4,12},{8,0},{12,4},{16,24},{20,28},{24,16},{28,20},{1,9},{5... | collective-permute-start | bytes 294920 | tf_op jit(solution)/shard_map/ppermute | solution.py:40
  988.8 31.3 %collective-permute-start.52 = (bf16[64,512]{1,0:T(8,128)(2,1)S(1)}, bf16[64,512]{1,0:T(8,128)(2,1)S(1)}, u32[]{:S(2)}, u32[]{:S(2)}) collective-permute-start(bf16[64,512]{1,0:T(8,128)(2,1)S(1)} %maximum_select_fusion.52), channel_id=1, source_target_pairs={{0,4},{4,0},{8,12},{12,8},{16,20},{20,16},{24,28},{28,24},{1,5},{5... | collective-permute-start | bytes 196616 | tf_op jit(solution)/shard_map/ppermute | solution.py:40
  990.4 30.7 %collective-permute-start.31 = (bf16[64,512]{1,0:T(8,128)(2,1)S(1)}, bf16[64,512]{1,0:T(8,128)(2,1)S(1)}, u32[]{:S(2)}, u32[]{:S(2)}) collective-permute-start(bf16[64,512]{1,0:T(8,128)(2,1)S(1)} %maximum_select_fusion.51), channel_id=1, source_target_pairs={{0,4},{4,0},{8,12},{12,8},{16,20},{20,16},{24,28},{28,24},{1,5},{5... | collective-permute-start | bytes 196616 | tf_op jit(solution)/shard_map/ppermute | solution.py:40
  992.0 31.2 %collective-permute-start.10 = (bf16[64,512]{1,0:T(8,128)(2,1)S(1)}, bf16[64,512]{1,0:T(8,128)(2,1)S(1)}, u32[]{:S(2)}, u32[]{:S(2)}) collective-permute-start(bf16[64,512]{1,0:T(8,128)(2,1)S(1)} %maximum_select_fusion.50), channel_id=1, source_target_pairs={{0,4},{4,0},{8,12},{12,8},{16,20},{20,16},{24,28},{28,24},{1,5},{5... | collective-permute-start | bytes 196616 | tf_op jit(solution)/shard_map/ppermute | solution.py:40
  1027.4 33.3 %collective-permute-start.53 = (bf16[128,512]{1,0:T(8,128)(2,1)S(1)}, bf16[128,512]{1,0:T(8,128)(2,1)S(1)}, u32[]{:S(2)}, u32[]{:S(2)}) collective-permute-start(bf16[128,512]{1,0:T(8,128)(2,1)S(1)} %maximum_select_fusion.42), channel_id=1, source_target_pairs={{0,2},{2,0},{1,3},{3,1},{4,6},{6,4},{5,7},{7,5},{8,10},{10,8},{9,1... | collective-permute-start | bytes 393224 | tf_op jit(solution)/shard_map/ppermute | solution.py:40
  1028.8 33.2 %collective-permute-start.32 = (bf16[128,512]{1,0:T(8,128)(2,1)S(1)}, bf16[128,512]{1,0:T(8,128)(2,1)S(1)}, u32[]{:S(2)}, u32[]{:S(2)}) collective-permute-start(bf16[128,512]{1,0:T(8,128)(2,1)S(1)} %maximum_select_fusion.41), channel_id=1, source_target_pairs={{0,2},{2,0},{1,3},{3,1},{4,6},{6,4},{5,7},{7,5},{8,10},{10,8},{9,1... | collective-permute-start | bytes 393224 | tf_op jit(solution)/shard_map/ppermute | solution.py:40
  1029.8 33.1 %collective-permute-start.11 = (bf16[128,512]{1,0:T(8,128)(2,1)S(1)}, bf16[128,512]{1,0:T(8,128)(2,1)S(1)}, u32[]{:S(2)}, u32[]{:S(2)}) collective-permute-start(bf16[128,512]{1,0:T(8,128)(2,1)S(1)} %maximum_select_fusion.40), channel_id=1, source_target_pairs={{0,2},{2,0},{1,3},{3,1},{4,6},{6,4},{5,7},{7,5},{8,10},{10,8},{9,1... | collective-permute-start | bytes 393224 | tf_op jit(solution)/shard_map/ppermute | solution.py:40
  (176 other events, 1649.0 us)
Sparse Core Ops, SparseCore 0:
  21.6 76.7 all-gather.3
  568.1 51.0 all-gather.5
  767.2 32.1 reduce-scatter.7
  827.7 24.5 reduce-scatter.5
  882.7 24.7 reduce-scatter.3

commit v2 on v1

v2 whole, which is shorter than its diff:
```python
import functools

import jax
import jax.numpy as jnp
from jax import lax
from jax.experimental import pallas as pl
from jax.experimental.pallas import tpu as pltpu
from jax.sharding import PartitionSpec as P

HD = 128
RATE = 3
EPS = 1e-05
NEG = -1000000000.0
LOG2E = 1.4426950408889634
SCALE = HD ** (-0.5)
GELU_ROOT = 0.7978845608028654
GELU_CUBE = 0.044715

LOW = jnp.bfloat16
WIDE = jnp.float32
NN = (((1,), (0,)), ((), ()))
NT = (((1,), (1,)), ((), ()))
TN = (((0,), (0,)), ((), ()))


def dot(first, second, dims=NN):
    return lax.dot_general(first, second, dims, preferred_element_type=WIDE)


def norm_stats(values):
    centre = values - jnp.mean(values, axis=-1, keepdims=True)
    inverse = lax.rsqrt(jnp.mean(centre * centre, axis=-1, keepdims=True) + EPS)
    return (centre * inverse, inverse)


def norm_back(grad_normed, normed, inverse, gain_vector):
    scaled = grad_normed * gain_vector
    return inverse * (
        scaled
        - jnp.mean(scaled, axis=-1, keepdims=True)
        - normed * jnp.mean(scaled * normed, axis=-1, keepdims=True)
    )


def per_stream(array_shape):
    block = (1,) + tuple(array_shape[1:])
    zeros = (0,) * (len(block) - 1)
    return pl.BlockSpec(block, lambda s: (s,) + zeros)


def whole(array_shape):
    zeros = (0,) * len(array_shape)
    return pl.BlockSpec(tuple(array_shape), lambda *_: zeros)


def scalars():
    return pl.BlockSpec(memory_space=pltpu.SMEM)


def shaped(shape, dtype=LOW):
    return jax.ShapeDtypeStruct(tuple(shape), dtype)


def call(kernel, grid, in_specs, out_specs, out_shape, scratch=(), flops=0, moved=0, vmem=48):
    return pl.pallas_call(
        kernel,
        grid=grid,
        in_specs=in_specs,
        out_specs=out_specs,
        out_shape=out_shape,
        scratch_shapes=list(scratch),
        compiler_params=pltpu.CompilerParams(vmem_limit_bytes=vmem * 1024 * 1024),
        cost_estimate=pl.CostEstimate(flops=flops, bytes_accessed=moved, transcendentals=0),
    )


def project_kernel(x_ref, gain_ref, bias_ref, *refs):
    count = (len(refs) - 1) // 2
    weights, unit_ref, outs = refs[:count], refs[count], refs[count + 1 :]
    rows = x_ref.shape[-2]
    normed, _ = norm_stats(x_ref[...].reshape(rows, -1).astype(WIDE))
    unit_ref[0] = normed.astype(LOW)
    low = (normed * gain_ref[...] + bias_ref[...]).astype(LOW)
    for weight_ref, out_ref in zip(weights, outs):
        out_ref[0] = dot(low, weight_ref[...]).astype(LOW)


def project(rows, gain, bias, weights):
    streams, count, width = rows.shape[0], rows.shape[-2], rows.shape[-1]
    features = weights[0].shape[1]
    outs = [shaped((streams, count, width))] + [
        shaped((streams, count, features)) for _ in weights
    ]
    return call(
        project_kernel,
        (streams,),
        [per_stream(rows.shape), whole(gain.shape), whole(bias.shape)]
        + [whole(w.shape) for w in weights],
        [per_stream(o.shape) for o in outs],
        outs,
        flops=2 * streams * count * width * features * len(weights),
        moved=4 * streams * count * width,
    )(rows, gain, bias, *weights)


def slot_masks(own, meta_ref, stream, streams, slots, rows):
    tier = meta_ref[0]
    length = meta_ref[1 + stream]
    filled = meta_ref[1 + streams + stream]
    memory_ok = lax.broadcasted_iota(jnp.int32, (slots, rows), 0) < filled
    key_row = lax.broadcasted_iota(jnp.int32, (rows, rows), 0)
    segment_ok = (tier * rows + key_row) < length
    if own:
        query_row = lax.broadcasted_iota(jnp.int32, (rows, rows), 1)
        segment_ok = segment_ok & (key_row <= query_row)
    return memory_ok, segment_ok


def by_tier(own, meta_ref, body):
    if own:
        body(True)
        return

    @pl.when(meta_ref[0] == 0)
    def _():
        body(True)

    @pl.when(meta_ref[0] != 0)
    def _():
        body(False)


def attend_kernel(own, meta_ref, q_ref, km_ref, vm_ref, ks_ref, vs_ref, out_ref, total_ref):
    streams = pl.num_programs(0)
    stream = pl.program_id(0)
    slots, rows = km_ref.shape[1], q_ref.shape[1]
    heads = q_ref.shape[2] // HD

    def body(with_segment):
        memory_ok, segment_ok = slot_masks(own, meta_ref, stream, streams, slots, rows)
        for head in range(heads):
            cols = slice(head * HD, (head + 1) * HD)
            query = q_ref[0, :, cols]
            scores = jnp.where(
                memory_ok, dot(km_ref[0, :, cols], query, NT) * (SCALE * LOG2E), NEG
            )
            top = jnp.max(scores, axis=0, keepdims=True)
            if with_segment:
                near = jnp.where(
                    segment_ok, dot(ks_ref[0, :, cols], query, NT) * (SCALE * LOG2E), NEG
                )
                top = jnp.maximum(top, jnp.max(near, axis=0, keepdims=True))
            raw = jnp.exp2(scores - top)
            spent = jnp.sum(raw, axis=0, keepdims=True)
            mixed = dot(vm_ref[0, :, cols], raw.astype(LOW), TN)
            if with_segment:
                raw_near = jnp.exp2(near - top)
                spent = spent + jnp.sum(raw_near, axis=0, keepdims=True)
                mixed = mixed + dot(vs_ref[0, :, cols], raw_near.astype(LOW), TN)
            out_ref[0, :, cols] = (mixed / spent).T.astype(LOW)
            total_ref[0, head : head + 1, :] = top + jnp.log2(spent)

    by_tier(own, meta_ref, body)


def attend(own, meta, q, km, vm, ks, vs):
    streams, rows, features = q.shape
    heads = features // HD
    outs = [shaped(q.shape), shaped((streams, heads, rows), WIDE)]
    return call(
        functools.partial(attend_kernel, own),
        (streams,),
        [scalars()] + [per_stream(a.shape) for a in (q, km, vm, ks, vs)],
        [per_stream(o.shape) for o in outs],
        outs,
        flops=8 * streams * rows * features * (km.shape[1] + rows),
        moved=4 * km.size + 8 * q.size,
    )(meta, q, km, vm, ks, vs)


def merge_kernel(own_ref, own_total_ref, other_ref, other_total_ref, w_ref, low_ref, total_ref, part_ref):
    first, second = own_total_ref[0], other_total_ref[0]
    top = jnp.maximum(first, second)
    total = top + jnp.log2(jnp.exp2(first - top) + jnp.exp2(second - top))
    total_ref[0] = total
    share_own, share_other = jnp.exp2(first - total), jnp.exp2(second - total)
    rows = own_ref.shape[1]
    for head in range(own_ref.shape[2] // HD):
        cols = slice(head * HD, (head + 1) * HD)
        column_own = jnp.broadcast_to(share_own[head : head + 1], (HD, rows)).T
        column_other = jnp.broadcast_to(share_other[head : head + 1], (HD, rows)).T
        merged = (
            own_ref[0, :, cols].astype(WIDE) * column_own
            + other_ref[0, :, cols].astype(WIDE) * column_other
        )
        low_ref[0, :, cols] = merged.astype(LOW)
    part_ref[0] = dot(low_ref[0], w_ref[...]).astype(LOW)


def merge(own, own_total, other, other_total, w_attn_out):
    streams, rows, features = own.shape
    outs = [
        shaped(own.shape),
        shaped(own_total.shape, WIDE),
        shaped((streams, rows, w_attn_out.shape[1])),
    ]
    return call(
        merge_kernel,
        (streams,),
        [per_stream(a.shape) for a in (own, own_total, other, other_total)]
        + [whole(w_attn_out.shape)],
        [per_stream(o.shape) for o in outs],
        outs,
        flops=2 * own.size * w_attn_out.shape[1],
        moved=6 * own.size + w_attn_out.size * 2,
    )(own, own_total, other, other_total, w_attn_out)


def valid_rows(meta_ref, streams, rows):
    place = lax.broadcasted_iota(jnp.int32, (streams * rows, 1), 0)
    ok = None
    for stream in range(streams):
        inside = (place >= stream * rows) & (
            place < stream * rows + meta_ref[1 + stream] - meta_ref[0] * rows
        ) & (place < (stream + 1) * rows)
        ok = inside if ok is None else ok | inside
    return ok


def ffn_kernel(first, streams, meta_ref, x_ref, a_ref, b_ref, cot_ref, gain_ref, bias_ref, wi_ref, wo_ref, *refs):
    if first:
        grads_ref, ffn_ref, back_ref, low_ref, grad_ref, ffn_acc, back_acc = refs
    else:
        ffn_in, back_in, grads_ref, ffn_ref, back_ref, low_ref, grad_ref, ffn_acc, back_acc = refs
    step = pl.program_id(0)
    units = wi_ref.shape[1]

    @pl.when(step == 0)
    def _():
        hidden = x_ref[...].astype(WIDE) + (a_ref[...].astype(WIDE) + b_ref[...].astype(WIDE))
        normed, _ = norm_stats(hidden)
        low_ref[...] = (normed * gain_ref[...] + bias_ref[...]).astype(LOW)
        ok = valid_rows(meta_ref, streams, x_ref.shape[0] // streams)
        grad_ref[...] = jnp.where(ok, cot_ref[...].astype(WIDE), 0.0).astype(LOW)
        if first:
            ffn_acc[...] = jnp.zeros_like(ffn_acc)
            back_acc[...] = jnp.zeros_like(back_acc)
        else:
            ffn_acc[...] = ffn_in[...]
            back_acc[...] = back_in[...]

    lifted = dot(low_ref[...], wi_ref[...])
    square = lifted * lifted
    bent = jnp.tanh(GELU_ROOT * lifted * (1.0 + GELU_CUBE * square))
    half = 0.5 * (1.0 + bent)
    activated = (lifted * half).astype(LOW)
    slope = half + 0.5 * lifted * (1.0 - bent * bent) * (
        GELU_ROOT * (1.0 + 3.0 * GELU_CUBE * square)
    )
    place = pl.multiple_of(step * units, units)
    grads_ref[0, pl.ds(place, units), :] = dot(activated, grad_ref[...], TN).astype(LOW)
    grad_activated = dot(grad_ref[...], wo_ref[...], NT)
    grad_lifted = (slope * grad_activated).astype(LOW)
    grads_ref[1, :, pl.ds(place, units)] = dot(low_ref[...], grad_lifted, TN).astype(LOW)
    ffn_acc[...] += dot(activated, wo_ref[...])
    back_acc[...] += dot(grad_lifted, wi_ref[...], NT)

    @pl.when(step == pl.num_programs(0) - 1)
    def _():
        ffn_ref[...] = ffn_acc[...].astype(ffn_ref.dtype)
        back_ref[...] = back_acc[...].astype(back_ref.dtype)


def ffn_half(part, streams, meta, x, a, b, cot, gain, bias, w_in, w_out, carried=()):
    rows, width = x.shape
    units = w_in.shape[1] // 2
    block = units // 2
    base = part * 2
    first = not carried
    kind = WIDE if first else LOW
    outs = [shaped((2, width, units)), shaped(x.shape, kind), shaped(x.shape, kind)]
    return call(
        functools.partial(ffn_kernel, first, streams),
        (2,),
        [scalars()]
        + [whole(v.shape) for v in (x, a, b, cot, gain, bias)]
        + [
            pl.BlockSpec((width, block), lambda j: (0, base + j)),
            pl.BlockSpec((block, width), lambda j: (base + j, 0)),
        ]
        + [whole(v.shape) for v in carried],
        [whole(o.shape) for o in outs],
        outs,
        scratch=[
            pltpu.VMEM(x.shape, LOW),
            pltpu.VMEM(x.shape, LOW),
            pltpu.VMEM(x.shape, WIDE),
            pltpu.VMEM(x.shape, WIDE),
        ],
        flops=12 * rows * width * units,
        moved=8 * rows * width + 8 * units * width,
        vmem=60,
    )(meta, x, a, b, cot, gain, bias, w_in, w_out, *carried)


def hidden_back_kernel(
    meta_ref,
    x_ref,
    a_ref,
    b_ref,
    back_ref,
    back_other_ref,
    ffn_ref,
    ffn_other_ref,
    cot_ref,
    merged_ref,
    total_ref,
    w_ref,
    gain_ref,
    out_ref,
    grad_hidden_ref,
    grad_merged_ref,
    stats_ref,
    grad_w_ref,
    vector_ref,
    w_acc,
):
    stream = pl.program_id(0)
    rows = x_ref.shape[1]
    hidden = x_ref[0].astype(WIDE) + (a_ref[0].astype(WIDE) + b_ref[0].astype(WIDE))
    normed, inverse = norm_stats(hidden)
    place = meta_ref[0] * rows + lax.broadcasted_iota(jnp.int32, (rows, 1), 0)
    ok = place < meta_ref[1 + stream]
    result = hidden + (ffn_ref[0].astype(WIDE) + ffn_other_ref[0].astype(WIDE))
    out_ref[0] = jnp.where(ok, result, 0.0).astype(LOW)
    back = back_ref[0].astype(WIDE) + back_other_ref[0].astype(WIDE)
    grad_out = jnp.where(ok, cot_ref[0].astype(WIDE), 0.0)
    grad_hidden = grad_out + norm_back(back, normed, inverse, gain_ref[...])
    grad_hidden_ref[0] = grad_hidden
    low = grad_hidden.astype(LOW)
    merged = merged_ref[0]
    grad_merged = dot(low, w_ref[...], NT).astype(LOW)
    grad_merged_ref[0] = grad_merged
    heads = merged.shape[1] // HD
    stats_ref[0, :heads, :] = total_ref[0]
    product = grad_merged.astype(WIDE) * merged.astype(WIDE)
    for head in range(heads):
        turned = product[:, head * HD : (head + 1) * HD].T
        stats_ref[0, heads + head : heads + head + 1, :] = jnp.sum(turned, axis=0, keepdims=True)
    grad_w = dot(merged, low, TN)
    gain_part = jnp.sum(back * normed, axis=0, keepdims=True)
    bias_part = jnp.sum(back, axis=0, keepdims=True)

    @pl.when(stream == 0)
    def _():
        w_acc[...] = grad_w
        vector_ref[0:1, :] = gain_part
        vector_ref[1:2, :] = bias_part

    @pl.when(stream != 0)
    def _():
        w_acc[...] += grad_w
        vector_ref[0:1, :] += gain_part
        vector_ref[1:2, :] += bias_part

    @pl.when(stream == pl.num_programs(0) - 1)
    def _():
        grad_w_ref[...] = w_acc[...].astype(LOW)


def hidden_back(meta, x, a, b, back, back_other, ffn, ffn_other, cot, merged, total, w, gain):
    streams, rows, width = x.shape
    heads = merged.shape[2] // HD
    outs = [
        shaped(x.shape),
        shaped(x.shape, WIDE),
        shaped(merged.shape),
        shaped((streams, 2 * heads, rows), WIDE),
        shaped(w.shape),
        shaped((2, width), WIDE),
    ]
    streamed = (x, a, b, back, back_other, ffn, ffn_other, cot, merged, total)
    return call(
        hidden_back_kernel,
        (streams,),
        [scalars()] + [per_stream(v.shape) for v in streamed] + [whole(w.shape), whole(gain.shape)],
        [per_stream(o.shape) for o in outs[:4]] + [whole(o.shape) for o in outs[4:]],
        outs,
        scratch=[pltpu.VMEM(w.shape, WIDE)],
        flops=4 * streams * rows * w.size,
        moved=24 * x.size,
    )(meta, *streamed, w, gain)


def attend_back_kernel(own, meta_ref, q_ref, gm_ref, stats_ref, km_ref, vm_ref, ks_ref, vs_ref, *refs):
    if own:
        gq_ref, gkm_ref, gvm_ref, gks_ref, gvs_ref = refs
        before = None
    else:
        before, (gq_ref, gkm_ref, gvm_ref, gks_ref, gvs_ref) = refs[:4], refs[4:]
    streams = pl.num_programs(0)
    stream = pl.program_id(0)
    slots, rows = km_ref.shape[1], q_ref.shape[1]
    heads = q_ref.shape[2] // HD

    def put(ref, index, cols, value):
        if before is not None:
            value = value + before[index][0, :, cols]
        ref[0, :, cols] = value.astype(ref.dtype)

    def body(with_segment):
        memory_ok, segment_ok = slot_masks(own, meta_ref, stream, streams, slots, rows)
        for head in range(heads):
            cols = slice(head * HD, (head + 1) * HD)
            query = q_ref[0, :, cols]
            grad = gm_ref[0, :, cols]
            total = stats_ref[0, head : head + 1, :]
            delta = stats_ref[0, heads + head : heads + head + 1, :]

            def tier(key, value, ok):
                scores = jnp.where(ok, dot(key, query, NT) * (SCALE * LOG2E), NEG)
                weights = jnp.exp2(scores - total)
                grad_scores = (weights * (dot(value, grad, NT) - delta)).astype(LOW)
                return (
                    dot(key, grad_scores, TN),
                    dot(grad_scores, query) * SCALE,
                    dot(weights.astype(LOW), grad),
                )

            turned, grad_key, grad_value = tier(km_ref[0, :, cols], vm_ref[0, :, cols], memory_ok)
            put(gkm_ref, 0, cols, grad_key)
            put(gvm_ref, 1, cols, grad_value)
            if with_segment:
                more, grad_key, grad_value = tier(
                    ks_ref[0, :, cols], vs_ref[0, :, cols], segment_ok
                )
                turned = turned + more
                put(gks_ref, 2, cols, grad_key)
                put(gvs_ref, 3, cols, grad_value)
            else:
                gks_ref[0, :, cols] = before[2][0, :, cols].astype(gks_ref.dtype)
                gvs_ref[0, :, cols] = before[3][0, :, cols].astype(gvs_ref.dtype)
            gq_ref[0, :, cols] = (turned * SCALE).T.astype(LOW)

    by_tier(own, meta_ref, body)


def attend_back(own, meta, q, gm, stats, km, vm, ks, vs, before=()):
    streams, rows, features = q.shape
    kind = WIDE if own else LOW
    outs = [shaped(q.shape)] + [shaped(a.shape, kind) for a in (km, vm, ks, vs)]
    return call(
        functools.partial(attend_back_kernel, own),
        (streams,),
        [scalars()] + [per_stream(a.shape) for a in (q, gm, stats, km, vm, ks, vs, *before)],
        [per_stream(o.shape) for o in outs],
        outs,
        flops=20 * streams * rows * features * (km.shape[1] + rows),
        moved=12 * km.size + 12 * q.size,
    )(meta, q, gm, stats, km, vm, ks, vs, *before)


def key_value_grads_kernel(
    unit_ref, stored_ref, gks_ref, gvs_ref, gkm_ref, gvm_ref, wk_ref, wv_ref, gain_ref, bias_ref,
    grads_ref, part_ref, column_ref, k_acc, v_acc, sums
):
    stream = pl.program_id(0)

    @pl.when(stream == 0)
    def _():
        k_acc[...] = jnp.zeros_like(k_acc)
        v_acc[...] = jnp.zeros_like(v_acc)
        sums[...] = jnp.zeros_like(sums)

    unit, stored = unit_ref[0], stored_ref[0]
    gks, gvs, gkm, gvm = gks_ref[0], gvs_ref[0], gkm_ref[0], gvm_ref[0]
    k_acc[...] += dot(unit, gks, TN) + dot(stored, gkm, TN)
    v_acc[...] += dot(unit, gvs, TN) + dot(stored, gvm, TN)
    for place, pair in enumerate(((gks, gkm), (gvs, gvm))):
        for piece in pair:
            sums[place : place + 1, :] += jnp.sum(piece.astype(WIDE), axis=0, keepdims=True)
    part_ref[0] = dot(gks, wk_ref[...], NT) + dot(gvs, wv_ref[...], NT)

    @pl.when(stream == pl.num_programs(0) - 1)
    def _():
        features = wk_ref.shape[1]
        gain, bias = gain_ref[...], bias_ref[...]
        grads_ref[:, :features] = (gain * k_acc[...] + bias * sums[0:1, :]).astype(LOW)
        grads_ref[:, features:] = (gain * v_acc[...] + bias * sums[1:2, :]).astype(LOW)
        wk, wv = wk_ref[...].astype(WIDE), wv_ref[...].astype(WIDE)
        column_ref[:, 0:1] = jnp.sum(wk * k_acc[...] + wv * v_acc[...], axis=1, keepdims=True)
        column_ref[:, 1:2] = jnp.sum(wk * sums[0:1, :] + wv * sums[1:2, :], axis=1, keepdims=True)


def key_value_grads(unit, stored, gks, gvs, gkm, gvm, wk, wv, gain, bias):
    width, features = wk.shape
    outs = [shaped((width, 2 * features)), shaped(unit.shape, WIDE), shaped((width, 2), WIDE)]
    streamed = (unit, stored, gks, gvs, gkm, gvm)
    fixed = (wk, wv, gain, bias)
    return call(
        key_value_grads_kernel,
        (unit.shape[0],),
        [per_stream(v.shape) for v in streamed] + [whole(v.shape) for v in fixed],
        [whole(outs[0].shape), per_stream(outs[1].shape), whole(outs[2].shape)],
        outs,
        scratch=[
            pltpu.VMEM(wk.shape, WIDE),
            pltpu.VMEM(wk.shape, WIDE),
            pltpu.VMEM((2, features), WIDE),
        ],
        flops=4 * (unit.size * 2 + stored.size) * features,
        moved=2 * (unit.size * 3 + stored.size) + 8 * wk.size,
    )(*streamed, *fixed)


def query_grads_kernel(
    unit_ref, own_ref, other_ref, part_ref, wq_ref, gain_ref, bias_ref, column_in_ref,
    grads_ref, normed_ref, column_ref, q_acc, sums
):
    stream = pl.program_id(0)

    @pl.when(stream == 0)
    def _():
        q_acc[...] = jnp.zeros_like(q_acc)
        sums[...] = jnp.zeros_like(sums)

    wide = own_ref[0].astype(WIDE) + other_ref[0].astype(WIDE)
    grad = wide.astype(LOW)
    q_acc[...] += dot(unit_ref[0], grad, TN)
    sums[...] += jnp.sum(grad.astype(WIDE), axis=0, keepdims=True)
    normed_ref[0] = (part_ref[0] + dot(grad, wq_ref[...], NT)).astype(LOW)

    @pl.when(stream == pl.num_programs(0) - 1)
    def _():
        grads_ref[...] = (gain_ref[...] * q_acc[...] + bias_ref[...] * sums[...]).astype(LOW)
        wq = wq_ref[...].astype(WIDE)
        column_ref[:, 0:1] = column_in_ref[:, 0:1] + jnp.sum(
            wq * q_acc[...], axis=1, keepdims=True
        )
        column_ref[:, 1:2] = column_in_ref[:, 1:2] + jnp.sum(
            wq * sums[...], axis=1, keepdims=True
        )


def query_grads(unit, own, other, part, wq, gain, bias, column):
    outs = [shaped(wq.shape), shaped(unit.shape), shaped(column.shape, WIDE)]
    streamed = (unit, own, other, part)
    fixed = (wq, gain, bias, column)
    return call(
        query_grads_kernel,
        (unit.shape[0],),
        [per_stream(v.shape) for v in streamed] + [whole(v.shape) for v in fixed],
        [whole(outs[0].shape), per_stream(outs[1].shape), whole(outs[2].shape)],
        outs,
        scratch=[pltpu.VMEM(wq.shape, WIDE), pltpu.VMEM((1, wq.shape[1]), WIDE)],
        flops=4 * unit.size * wq.shape[1],
        moved=10 * unit.size + 8 * wq.size,
    )(*streamed, *fixed)


def input_back_kernel(x_ref, own_ref, other_ref, hidden_ref, gain_ref, out_ref):
    normed, inverse = norm_stats(x_ref[0].astype(WIDE))
    grad = own_ref[0].astype(WIDE) + other_ref[0].astype(WIDE)
    out_ref[0] = (hidden_ref[0] + norm_back(grad, normed, inverse, gain_ref[...])).astype(LOW)


def input_back(x, own, other, grad_hidden, gain):
    streamed = (x, own, other, grad_hidden)
    return call(
        input_back_kernel,
        (x.shape[0],),
        [per_stream(v.shape) for v in streamed] + [whole(gain.shape)],
        per_stream(x.shape),
        shaped(x.shape),
        flops=30 * x.size,
        moved=12 * x.size,
    )(*streamed, gain)


def compress_kernel(meta_ref, own_ref, other_ref, w_ref, cot_ref, out_ref, grad_ref, acc):
    stream = pl.program_id(0)
    streams = pl.num_programs(0)
    head = meta_ref[1 + 2 * streams]
    slots, part = own_ref.shape[1], own_ref.shape[2]
    count = out_ref.shape[1]
    place = lax.broadcasted_iota(jnp.int32, (count, slots), 0)
    slot = lax.broadcasted_iota(jnp.int32, (count, slots), 1)
    ok = lax.broadcasted_iota(jnp.int32, (count, 1), 0) < meta_ref[1 + stream] // RATE
    cot = jnp.where(ok, cot_ref[0].astype(WIDE), 0.0).astype(LOW)

    @pl.when(stream == 0)
    def _():
        acc[...] = jnp.zeros_like(acc)

    result = jnp.zeros(out_ref.shape[1:], WIDE)
    for shift in range(RATE):
        pick = jnp.where(slot == place * RATE + shift, 1.0, 0.0).astype(LOW)
        for ref, side in ((own_ref, head), (other_ref, 1 - head)):
            rows = dot(pick, ref[0]).astype(LOW)
            start = pl.multiple_of(side * part, part)
            result = result + dot(rows, w_ref[shift, pl.ds(start, part), :])
            acc[shift, pl.ds(start, part), :] += dot(rows, cot, TN)
    out_ref[0] = jnp.where(ok, result, 0.0).astype(LOW)

    @pl.when(stream == streams - 1)
    def _():
        grad_ref[...] = acc[...].astype(LOW)


def compress(meta, own, other, w, cot):
    streams = own.shape[0]
    outs = [shaped(cot.shape), shaped(w.shape)]
    return call(
        compress_kernel,
        (streams,),
        [scalars(), per_stream(own.shape), per_stream(other.shape), whole(w.shape), per_stream(cot.shape)],
        [per_stream(cot.shape), whole(w.shape)],
        outs,
        scratch=[pltpu.VMEM(w.shape, WIDE)],
        flops=4 * cot.shape[0] * cot.shape[1] * w.size,
        moved=4 * own.size + 4 * w.size,
    )(meta, own, other, w, cot)


def bits_of():
    size = lax.axis_size("dp")
    bits = [("tier", 1)]
    step = 1
    while step < size:
        bits.append(("dp", step))
        step *= 2
    return bits


def bit_value(bit):
    axis, step = bit
    return (lax.axis_index(axis) // step) % 2


def swap(value, bit):
    axis, step = bit
    return lax.ppermute(value, axis, [(i, i ^ step) for i in range(lax.axis_size(axis))])


def swap_head(value):
    return swap(value, ("head", 1))


def swap_tier(value):
    return swap(value, ("tier", 1))


def add_low(first, second):
    total = first.astype(WIDE) + second.astype(WIDE)
    return lax.optimization_barrier(total.astype(LOW))


def all_reduce(value, order):
    held = value
    scattered = []
    for place, bit in enumerate(order):
        half = held.shape[0] // 2
        if place == len(order) - 1 or half % 16:
            held = add_low(held, swap(held, bit))
        else:
            side = bit_value(bit)
            sent = lax.dynamic_slice_in_dim(held, (1 - side) * half, half, 0)
            kept = lax.dynamic_slice_in_dim(held, side * half, half, 0)
            held = add_low(kept, swap(sent, bit))
            scattered.append((bit, side))
    for bit, side in reversed(scattered):
        other = swap(held, bit)
        held = jnp.where(
            side == 0, jnp.concatenate([held, other], 0), jnp.concatenate([other, held], 0)
        )
    return held


def reduce_parts(low, sizes):
    tier, *rest = bits_of()
    orders = (
        [tier, *rest],
        [rest[0], rest[1], tier, *rest[2:]],
        [rest[1], tier, rest[0], *rest[2:]],
    )
    start = 0
    pieces = []
    for size, order in zip(sizes, orders):
        pieces.append(all_reduce(low[start : start + size], order))
        start += size
    return jnp.concatenate(pieces, 0)


def on_device(
    inputs,
    memories,
    seg_len,
    mem_count,
    w_query,
    w_key,
    w_value,
    w_attn_out,
    w_ffn_in,
    w_ffn_out,
    w_compress,
    gain_attn,
    bias_attn,
    gain_ffn,
    bias_ffn,
    cotan_output,
    cotan_compressed,
):
    tier_index = lax.axis_index("tier")
    head_index = lax.axis_index("head")
    streams, rows, width = inputs.shape
    features = w_query.shape[1]
    counts = mem_count[:, 0]
    meta = jnp.concatenate(
        [tier_index[None], seg_len, counts, head_index[None]], 0
    ).astype(jnp.int32)
    gain_row, bias_row = gain_attn[None], bias_attn[None]
    gain_second, bias_second = gain_ffn[None], bias_ffn[None]

    unit, queries, keys, values = project(inputs, gain_row, bias_row, (w_query, w_key, w_value))
    queries_other = swap_tier(queries)
    stored, memory_keys, memory_values = project(memories, gain_row, bias_row, (w_key, w_value))
    tiers = (memory_keys, memory_values, keys, values)
    part_other, part_other_total = attend(False, meta, queries_other, *tiers)
    came, came_total = swap_tier(part_other), swap_tier(part_other_total)
    part_own, part_own_total = attend(True, meta, queries, *tiers)
    merged, totals, attended = merge(part_own, part_own_total, came, came_total, w_attn_out)
    attended_other = swap_head(attended)

    flat = (streams * rows, width)
    ffn_args = (
        inputs.reshape(flat),
        attended.reshape(flat),
        attended_other.reshape(flat),
        cotan_output.reshape(flat),
        gain_second,
        bias_second,
        w_ffn_in,
        w_ffn_out,
    )
    grads_first, ffn_wide, back_wide = ffn_half(0, streams, meta, *ffn_args)
    grads_second, ffn_part, back_part = ffn_half(
        1, streams, meta, *ffn_args, carried=(ffn_wide, back_wide)
    )
    ffn_part, back_part = ffn_part.reshape(inputs.shape), back_part.reshape(inputs.shape)
    back_other = swap_head(back_part)
    ffn_other = swap_head(ffn_part)

    layer_output, grad_hidden, grad_merged, stats, grad_attn_out, vectors_ffn = hidden_back(
        meta,
        inputs,
        attended,
        attended_other,
        back_part,
        back_other,
        ffn_part,
        ffn_other,
        cotan_output,
        merged,
        totals,
        w_attn_out,
        gain_second,
    )
    grad_merged_other, stats_other = swap_tier(grad_merged), swap_tier(stats)
    own_query, *sums = attend_back(True, meta, queries, grad_merged, stats, *tiers)
    other_query, grad_km, grad_vm, grad_ks, grad_vs = attend_back(
        False, meta, queries_other, grad_merged_other, stats_other, *tiers, before=tuple(sums)
    )
    came_query = swap_tier(other_query)
    grad_key_value, normed_part, column = key_value_grads(
        unit, stored, grad_ks, grad_vs, grad_km, grad_vm, w_key, w_value,
        gain_attn[:, None], bias_attn[:, None],
    )
    grad_query, normed_low, column = query_grads(
        unit, own_query, came_query, normed_part, w_query,
        gain_attn[:, None], bias_attn[:, None], column,
    )
    grad_inputs = input_back(inputs, normed_low, swap_head(normed_low), grad_hidden, gain_row)

    slots = memories.shape[2]
    slot_valid = (jnp.arange(slots)[None, :] < counts[:, None])[..., None]
    half = width // 2
    evicted = lax.dynamic_slice_in_dim(memories[:, 0], head_index * half, half, 2)
    evicted = jnp.where(slot_valid, evicted, jnp.zeros_like(evicted))
    evicted_came = lax.ppermute(evicted, "tier", [(0, 1)])
    evicted = jnp.where(tier_index == 0, evicted, evicted_came)
    compressed, grad_compress_low = compress(
        meta, evicted, swap_head(evicted), w_compress, cotan_compressed
    )
    grad_compress = all_reduce(
        grad_compress_low.reshape(RATE * width, -1), bits_of()[1:]
    )

    first = reduce_parts(grads_first.reshape(2 * width, -1), (512, 768, 768))
    second = reduce_parts(grads_second.reshape(2 * width, -1), (512, 768, 768))
    third = reduce_parts(
        jnp.concatenate([grad_key_value, grad_attn_out], 0), (512, 512, 512)
    )
    fourth = reduce_parts(grad_query, (256, 384, 384))
    grad_ffn_out = jnp.concatenate([first[:width], second[:width]], 0).astype(WIDE)
    grad_ffn_in = jnp.concatenate([first[width:], second[width:]], 1).astype(WIDE)
    vectors = lax.psum(
        jnp.concatenate([column.T, 0.5 * vectors_ffn], axis=0), ("dp", "tier", "head")
    )
    return (
        layer_output,
        compressed,
        grad_inputs,
        fourth.astype(WIDE),
        third[:width, :features].astype(WIDE),
        third[:width, features:].astype(WIDE),
        third[width:].astype(WIDE),
        grad_ffn_in,
        grad_ffn_out,
        grad_compress.astype(WIDE).reshape(RATE, width, -1),
        vectors[0],
        vectors[1],
        vectors[2],
        vectors[3],
    )


def solution(mesh):
    return jax.shard_map(
        on_device,
        mesh=mesh,
        in_specs=(
            P("dp", "tier", None),
            P("dp", "tier", None, None),
            P("dp"),
            P("dp", "tier"),
            P(None, "head"),
            P(None, "head"),
            P(None, "head"),
            P("head", None),
            P(None, "head"),
            P("head", None),
            P(None, None, ("tier", "head")),
            P(),
            P(),
            P(),
            P(),
            P("dp", "tier", None),
            P("dp", None, ("tier", "head")),
        ),
        out_specs=(
            P("dp", "tier", None),
            P("dp", None, ("tier", "head")),
            P("dp", "tier", None),
            P(None, "head"),
            P(None, "head"),
            P(None, "head"),
            P("head", None),
            P(None, "head"),
            P("head", None),
            P(None, None, ("tier", "head")),
            P(),
            P(),
            P(),
            P(),
        ),
        check_vma=False,
    )
```

time: 1150 us -> 670 us (0.58)
  matrix products: 201 us -> 0 us
  Pallas kernels: 0 us -> 141 us
  local copies, waits for them, and re-layouts: 164 us -> 29.6 us
  waiting for transfers between devices: 400 us -> 278 us
  other arithmetic: 134 us -> 60 us
  starting transfers between devices: 163 us -> 112 us
  blocking collectives: 57.1 us -> 39.5 us
  between operations: 16.4 us -> 3.04 us
    dot_general x57 -> x0, matrix products: 201 us -> none  [the longest x19 60.4 us: product(): jnp.dot(first_operand, second_operand, preferred_element_type=jnp.float32)]
    pallas_call x0 -> x14, Pallas kernels: none -> 141 us  [the longest x2 43.7 us: ffn_half(): call(functools.partial(ffn_kernel, first, streams), (2,), [scalars()] + [...]
    ppermute x5 -> x1, waiting for transfers between devices: 89 us -> 0.01 us  [on_device(): evicted_came = lax.ppermute(evicted, 'tier', [(0, 1)])]
    ppermute x129 -> x100, starting transfers between devices: 147 us -> 108 us  [swap(): lax.ppermute(value, axis, [(i, i ^ step) for i in range(lax.axis_size(axi...]
    dynamic_slice x42 -> x0, local copies, waits for them, and re-layouts: 34.6 us -> none  [the longest x30 27.1 us: on_device(): lax.map(attend_back, (queries, memory_keys, memory_values, segment_keys,...]
    dynamic_update_slice x24 -> x0, local copies, waits for them, and re-layouts: 34.4 us -> none  [on_device(): lax.map(attend, (normed_full, stored_low, seg_len, counts))]
    convert_element_type x88 -> x54, other arithmetic: 55 us -> 33.6 us  [the longest x48 13.7 us: add_low(): return lax.optimization_barrier(total.astype(LOW))]
    reduce_sum x16 -> x0, other arithmetic: 19.1 us -> none  [the longest x3 5.56 us: forward_part(): totals = jax.nn.logsumexp(scores, axis=-1, keepdims=True)]
  transfers between devices with their start and end apart: 141 -> 101, of which waited for: 81 -> 53; matrix products, arithmetic and copies ran while one was open for 38% -> 12% of each run, Pallas kernels for 0% -> 18%
where the time goes in v2:
time: 670 us; the launch traced here: 664 us
  waiting for transfers between devices  278 us (41%)
  Pallas kernels  141 us (21%)
  starting transfers between devices  112 us (17%)
  other arithmetic  60 us (9%)
  blocking collectives  39.5 us (6%)
  local copies, waits for them, and re-layouts  29.6 us (4%)
    ppermute x100, waiting for transfers between devices, swap(): lax.ppermute(value, axis, [(i, i ^ step) for i in range(lax.axis_size(axi...  278 us
    ppermute x100, starting transfers between devices, swap(): lax.ppermute(value, axis, [(i, i ^ step) for i in range(lax.axis_size(axi...  108 us
    pallas_call x2, Pallas kernels, ffn_half(): call(functools.partial(ffn_kernel, first, streams), (2,), [scalars()] + [...  43.7 us
    psum x1, blocking collectives, on_device(): lax.psum(jnp.concatenate([column.T, 0.5 * vectors_ffn], axis=0), ('dp', '...  39.5 us
    pallas_call x2, Pallas kernels, attend_back(): call(functools.partial(attend_back_kernel, own), (streams,), [scalars()]...  23.2 us
    select_n x37, other arithmetic, all_reduce(): jnp.where(side == 0, jnp.concatenate([held, other], 0), jnp.concatenate([...  18 us
    pallas_call x2, Pallas kernels, attend(): call(functools.partial(attend_kernel, own), (streams,), [scalars()] + [pe...  15.1 us
    convert_element_type x48, other arithmetic, add_low(): return lax.optimization_barrier(total.astype(LOW))  13.7 us
  transfers between devices with their start and end apart: 101, of which 53 were waited for; matrix products, arithmetic and copies ran while one was open for 12% of the time, Pallas kernels for 18%

profile of v2, /device:TPU:0, one launch (start us, length us, event | category | flops | bytes accessed | tf_op | source)
XLA Modules:
  0.0 663.7 jit_solution(15002747445735724500)
XLA Ops:
  5.7 5.6 shard_map.272
  13.2 2.9 collective-permute-start
  16.2 6.7 %shard_map.273 = (bf16[3,512,1024]{2,1,0:T(8,128)(2,1)}, bf16[3,512,512]{2,1,0:T(8,128)(2,1)S(1)}, bf16[3,512,512]{2,1,0:T(8,128)(2,1)S(1)}) custom-call(bf16[3,1,512,1024]{3,2,1,0:T(8,128)(2,1)} %x_ref.5, f32[1,1024]{1,0:T(1,128)S(1)} %bitcast.37, f32[1,1024]{1,0:T(1,128)S(1)} %bitcast.41, bf16[1024,512]{1,0:T(8,128)(2,1)S(1)} %copy-done.16, ...), custom_call_target="tpu_custom_call" | custom-call | flops 3221225472 | bytes 6291456 | tf_op jit(solution)/shard_map/pallas_call | solution.py:94
  24.0 9.8 %collective-permute-done.q_ref = bf16[3,256,512]{2,1,0:T(8,128)(2,1)S(1)} collective-permute-done((bf16[3,256,512]{2,1,0:T(8,128)(2,1)}, bf16[3,256,512]{2,1,0:T(8,128)(2,1)S(1)}, u32[]{:S(2)}, u32[]{:S(2)}) %collective-permute-start) | collective-permute-done | bytes 786464 | tf_op jit(solution)/shard_map/ppermute | solution.py:642
  33.9 7.7 %shard_map.275 = (bf16[3,256,512]{2,1,0:T(8,128)(2,1)S(1)}, f32[3,4,256]{2,1,0:T(4,128)S(1)}) custom-call(s32[8]{0:T(128)S(1)} %pad_add_fusion.meta_ref, bf16[3,256,512]{2,1,0:T(8,128)(2,1)S(1)} %collective-permute-done.q_ref, bf16[3,512,512]{2,1,0:T(8,128)(2,1)S(1)} %get-tuple-element.59.km_ref, bf16[3,512,512]{2,1,0:T(8,128)(2,1)} %copy-done.26, ...), custom_call_target="tpu_custom_call" | custom-call | flops 2415919104 | bytes 6291456 | tf_op jit(solution)/shard_map/pallas_call | solution.py:170
  42.8 3.1 bitcast_select_fusion
  45.9 4.2 collective-permute-start.6
  50.3 7.3 %shard_map.274 = (bf16[3,256,512]{2,1,0:T(8,128)(2,1)S(1)}, f32[3,4,256]{2,1,0:T(4,128)S(1)}) custom-call(s32[8]{0:T(128)S(1)} %pad_add_fusion.meta_ref, bf16[3,256,512]{2,1,0:T(8,128)(2,1)} %get-tuple-element.58.q_ref, bf16[3,512,512]{2,1,0:T(8,128)(2,1)S(1)} %copy-done.25, bf16[3,512,512]{2,1,0:T(8,128)(2,1)} %copy-done.26, ...), custom_call_target="tpu_custom_call" | custom-call | flops 2415919104 | bytes 6291456 | tf_op jit(solution)/shard_map/pallas_call | solution.py:170
  57.6 35.0 %collective-permute-done.2.other_total_ref = f32[3,4,256]{2,1,0:T(4,128)S(1)} collective-permute-done((f32[3,4,256]{2,1,0:T(4,128)S(1)}, f32[3,4,256]{2,1,0:T(4,128)S(1)}, u32[]{:S(2)}, u32[]{:S(2)}) %collective-permute-start.2) | collective-permute-done | bytes 12320 | tf_op jit(solution)/shard_map/ppermute | solution.py:642
  95.9 3.1 broadcast_select_fusion.own_ref
  99.3 21.4 %shard_map.277 = (bf16[2,1024,1024]{2,1,0:T(8,128)(2,1)}, f32[768,1024]{1,0:T(8,128)}, f32[768,1024]{1,0:T(8,128)}) custom-call(s32[8]{0:T(128)} %copy-done.13, bf16[768,1024]{1,0:T(8,128)(2,1)} %bitcast.29, bf16[768,1024]{1,0:T(8,128)(2,1)} %bitcast.31, bf16[768,1024]{1,0:T(8,128)(2,1)} %bitcast.7.b_ref, bf16[768,1024]{1,0:T(8,128)(2,1)} %bitcast.51, ...), custom_call_target="tpu_custom_call" | custom-call | flops 9663676416 | bytes 14680064 | tf_op jit(solution)/shard_map/pallas_call | solution.py:282
  120.7 22.3 %shard_map.278 = (bf16[2,1024,1024]{2,1,0:T(8,128)(2,1)}, bf16[768,1024]{1,0:T(8,128)(2,1)}, bf16[768,1024]{1,0:T(8,128)(2,1)}) custom-call(s32[8]{0:T(128)} %copy-done.13, bf16[768,1024]{1,0:T(8,128)(2,1)} %bitcast.30, bf16[768,1024]{1,0:T(8,128)(2,1)} %bitcast.32, bf16[768,1024]{1,0:T(8,128)(2,1)} %bitcast.7.b_ref, bf16[768,1024]{1,0:T(8,128)(2,1)} %bitcast.52, ...), custom_call_target="tpu_custom_call" | custom-call | flops 9663676416 | bytes 14680064 | tf_op jit(solution)/shard_map/pallas_call | solution.py:282
  144.6 2.4 fusion.11
  152.1 2.9 collective-permute-start.89
  155.9 10.0 %shard_map.280 = (bf16[3,170,256]{2,1,0:T(8,128)(2,1)}, bf16[3,1024,256]{2,1,0:T(8,128)(2,1)S(1)}) custom-call(s32[8]{0:T(128)S(1)} %copy-done.14, bf16[3,512,512]{2,1,0:T(8,128)(2,1)} %broadcast_select_fusion.own_ref, bf16[3,512,512]{2,1,0:T(8,128)(2,1)} %collective-permute-done.7.other_ref, bf16[3,1024,256]{2,1,0:T(8,128)(2,1)} %w_ref.5, ...), custom_call_target="tpu_custom_call" | custom-call | flops 1604321280 | bytes 6291456 | tf_op jit(solution)/shard_map/pallas_call | solution.py:613
  171.6 6.8 %collective-permute-done.82 = bf16[256,1024]{1,0:T(8,128)(2,1)} collective-permute-done((bf16[256,1024]{1,0:T(8,128)(2,1)}, bf16[256,1024]{1,0:T(8,128)(2,1)}, u32[]{:S(2)}, u32[]{:S(2)}) %collective-permute-start.82) | collective-permute-done | bytes 524320 | tf_op jit(solution)/shard_map/ppermute | solution.py:642
  191.1 15.1 %collective-permute-done.54 = bf16[384,1024]{1,0:T(8,128)(2,1)S(1)} collective-permute-done((bf16[384,1024]{1,0:T(8,128)(2,1)S(1)}, bf16[384,1024]{1,0:T(8,128)(2,1)S(1)}, u32[]{:S(2)}, u32[]{:S(2)}) %collective-permute-start.54) | collective-permute-done | bytes 786464 | tf_op jit(solution)/shard_map/ppermute | solution.py:642
  208.6 20.0 %collective-permute-done.90 = bf16[128,1024]{1,0:T(8,128)(2,1)S(1)} collective-permute-done((bf16[128,1024]{1,0:T(8,128)(2,1)S(1)}, bf16[128,1024]{1,0:T(8,128)(2,1)S(1)}, u32[]{:S(2)}, u32[]{:S(2)}) %collective-permute-start.90) | collective-permute-done | bytes 262176 | tf_op jit(solution)/shard_map/ppermute | solution.py:642
  234.1 9.4 %collective-permute-done.91 = bf16[64,1024]{1,0:T(8,128)(2,1)S(1)} collective-permute-done((bf16[64,1024]{1,0:T(8,128)(2,1)S(1)}, bf16[64,1024]{1,0:T(8,128)(2,1)S(1)}, u32[]{:S(2)}, u32[]{:S(2)}) %collective-permute-start.91) | collective-permute-done | bytes 131104 | tf_op jit(solution)/shard_map/ppermute | solution.py:642
  245.1 4.7 collective-permute-done.84
  251.6 7.3 %collective-permute-done.92 = bf16[64,1024]{1,0:T(8,128)(2,1)S(1)} collective-permute-done((bf16[64,1024]{1,0:T(8,128)(2,1)S(1)}, bf16[64,1024]{1,0:T(8,128)(2,1)S(1)}, u32[]{:S(2)}, u32[]{:S(2)}) %collective-permute-start.92) | collective-permute-done | bytes 131104 | tf_op jit(solution)/shard_map/ppermute | solution.py:642
  258.9 6.8 %collective-permute-done.85 = bf16[64,1024]{1,0:T(8,128)(2,1)S(1)} collective-permute-done((bf16[64,1024]{1,0:T(8,128)(2,1)S(1)}, bf16[64,1024]{1,0:T(8,128)(2,1)S(1)}, u32[]{:S(2)}, u32[]{:S(2)}) %collective-permute-start.85) | collective-permute-done | bytes 131104 | tf_op jit(solution)/shard_map/ppermute | solution.py:642
  269.8 6.9 %collective-permute-done.55 = bf16[192,1024]{1,0:T(8,128)(2,1)S(1)} collective-permute-done((bf16[192,1024]{1,0:T(8,128)(2,1)S(1)}, bf16[192,1024]{1,0:T(8,128)(2,1)S(1)}, u32[]{:S(2)}, u32[]{:S(2)}) %collective-permute-start.55) | collective-permute-done | bytes 393248 | tf_op jit(solution)/shard_map/ppermute | solution.py:642
  279.1 5.7 collective-permute-done.97
  289.0 2.3 collective-permute-done.77
  298.9 2.9 collective-permute-done.94
  301.9 2.3 collective-permute-start.78
  304.7 2.3 collective-permute-start.71
  307.8 2.3 collective-permute-start.57
  310.2 10.1 %shard_map.279 = (bf16[3,256,1024]{2,1,0:T(8,128)(2,1)}, f32[3,256,1024]{2,1,0:T(8,128)}, bf16[3,256,512]{2,1,0:T(8,128)(2,1)S(1)}, f32[3,8,256]{2,1,0:T(8,128)S...) custom-call(s32[8]{0:T(128)S(1)} %copy-done.14, bf16[3,256,1024]{2,1,0:T(8,128)(2,1)S(1)} %copy-done, ...), custom_call_target="tpu_custom_call" | custom-call | flops 1610612736 | bytes 18874368 | tf_op jit(solution)/shard_map/pallas_call | solution.py:383
  320.3 11.4 %shard_map.281 = (bf16[3,256,512]{2,1,0:T(8,128)(2,1)S(1)}, f32[3,512,512]{2,1,0:T(8,128)}, f32[3,512,512]{2,1,0:T(8,128)}, f32[3,256,512]{2,1,0:T(8,128)S(1)}, f32[3,256,512]{2,1,0:T(8,128)}) custom-call(s32[8]{0:T(128)S(1)} %copy-done.14, bf16[3,256,512]{2,1,0:T(8,128)(2,1)} %get-tuple-element.58.q_ref, bf16[3,256,512]{2,1,0:T(8,128)(2,1)S(1)} %get-tuple-element.77.gm_ref, ...), custom_call_target="tpu_custom_call" | custom-call | flops 6039797760 | bytes 14155776 | tf_op jit(solution)/shard_map/pallas_call | solution.py:452
  335.0 7.8 %collective-permute-done.64 = bf16[96,1024]{1,0:T(8,128)(2,1)S(1)} collective-permute-done((bf16[96,1024]{1,0:T(8,128)(2,1)S(1)}, bf16[96,1024]{1,0:T(8,128)(2,1)S(1)}, u32[]{:S(2)}, u32[]{:S(2)}) %collective-permute-start.64) | collective-permute-done | bytes 196640 | tf_op jit(solution)/shard_map/ppermute | solution.py:642
  347.4 3.5 collective-permute-done.79
  353.6 26.1 %collective-permute-done.72 = bf16[96,1024]{1,0:T(8,128)(2,1)S(1)} collective-permute-done((bf16[96,1024]{1,0:T(8,128)(2,1)S(1)}, bf16[96,1024]{1,0:T(8,128)(2,1)S(1)}, u32[]{:S(2)}, u32[]{:S(2)}) %collective-permute-start.72) | collective-permute-done | bytes 196640 | tf_op jit(solution)/shard_map/ppermute | solution.py:642
  385.3 8.5 %collective-permute-done.99 = bf16[768,256]{1,0:T(8,128)(2,1)S(1)} collective-permute-done((bf16[768,256]{1,0:T(8,128)(2,1)S(1)}, bf16[768,256]{1,0:T(8,128)(2,1)S(1)}, u32[]{:S(2)}, u32[]{:S(2)}) %collective-permute-start.99) | collective-permute-done | bytes 393248 | tf_op jit(solution)/shard_map/ppermute | solution.py:642
  395.0 10.0 %collective-permute-done.47 = bf16[256,1024]{1,0:T(8,128)(2,1)S(1)} collective-permute-done((bf16[256,1024]{1,0:T(8,128)(2,1)S(1)}, bf16[256,1024]{1,0:T(8,128)(2,1)S(1)}, u32[]{:S(2)}, u32[]{:S(2)}) %collective-permute-start.47) | collective-permute-done | bytes 524320 | tf_op jit(solution)/shard_map/ppermute | solution.py:642
  406.0 7.5 %collective-permute-done.73 = bf16[192,1024]{1,0:T(8,128)(2,1)S(1)} collective-permute-done((bf16[192,1024]{1,0:T(8,128)(2,1)S(1)}, bf16[192,1024]{1,0:T(8,128)(2,1)S(1)}, u32[]{:S(2)}, u32[]{:S(2)}) %collective-permute-start.73) | collective-permute-done | bytes 393248 | tf_op jit(solution)/shard_map/ppermute | solution.py:642
  424.2 11.8 %shard_map.282 = (bf16[3,256,512]{2,1,0:T(8,128)(2,1)S(1)}, bf16[3,512,512]{2,1,0:T(8,128)(2,1)}, bf16[3,512,512]{2,1,0:T(8,128)(2,1)}, bf16[3,256,512]{2,1,0:T(8,128)(2,1)S(1)}, bf16[3,256,512]{2,1,0:T(8,128)(2,1)S(1)}) custom-call(s32[8]{0:T(128)S(1)} %copy-done.14, bf16[3,256,512]{2,1,0:T(8,128)(2,1)S(1)} %copy-done.22, ...), custom_call_target="tpu_custom_call" | custom-call | flops 6039797760 | bytes 14155776 | tf_op jit(solution)/shard_map/pallas_call | solution.py:452
  436.0 12.8 %shard_map.283 = (bf16[1024,1024]{1,0:T(8,128)(2,1)}, f32[3,256,1024]{2,1,0:T(8,128)}, f32[1024,2]{1,0:T(8,128)S(1)}) custom-call(bf16[3,256,1024]{2,1,0:T(8,128)(2,1)} %get-tuple-element.76.unit_ref, bf16[3,512,1024]{2,1,0:T(8,128)(2,1)} %get-tuple-element.85.stored_ref, bf16[3,256,512]{2,1,0:T(8,128)(2,1)S(1)} %get-tuple-element.86.gks_ref, ...), custom_call_target="tpu_custom_call" | custom-call | flops 6442450944 | bytes 12058624 | tf_op jit(solution)/shard_map/pallas_call | solution.py:500
  450.6 5.5 collective-permute-done.50
  458.4 3.6 collective-permute-done.51
  466.3 6.9 %collective-permute-done.40 = bf16[256,1024]{1,0:T(8,128)(2,1)S(1)} collective-permute-done((bf16[256,1024]{1,0:T(8,128)(2,1)S(1)}, bf16[256,1024]{1,0:T(8,128)(2,1)S(1)}, u32[]{:S(2)}, u32[]{:S(2)}) %collective-permute-start.40) | collective-permute-done | bytes 524320 | tf_op jit(solution)/shard_map/ppermute | solution.py:642
  474.3 2.7 collective-permute-done.33
  480.7 2.8 maximum_select_fusion.2
  483.6 4.0 collective-permute-done.60
  488.3 3.9 fusion.3
  495.8 6.6 fusion.5
  505.4 6.7 %shard_map.284 = (bf16[1024,512]{1,0:T(8,128)(2,1)S(1)}, bf16[3,256,1024]{2,1,0:T(8,128)(2,1)}, f32[1024,2]{1,0:T(8,128)S(1)}) custom-call(bf16[3,256,1024]{2,1,0:T(8,128)(2,1)} %get-tuple-element.76.unit_ref, bf16[3,256,512]{2,1,0:T(8,128)(2,1)S(1)} %get-tuple-element.79.own_ref, bf16[3,256,512]{2,1,0:T(8,128)(2,1)S(1)} %collective-permute-done.10.other_ref, ...), custom_call_target="tpu_custom_call" | custom-call | flops 1610612736 | bytes 12058624 | tf_op jit(solution)/shard_map/pallas_call | solution.py:549
  522.2 39.5 %psum.7 = f32[4,1024]{1,0:T(4,128)} all-reduce(f32[4,1024]{1,0:T(4,128)} %pad_maximum_fusion.4), channel_id=1, replica_groups=mesh['dp'=8,'tier'=2,'head'=2] {'dp','tier','head'}, use_global_device_ids=true, to_apply=%region_0.1 | all-reduce | flops 4096 | bytes 32768 | tf_op jit(solution)/shard_map/psum | solution.py:806
  563.2 2.3 collective-permute-start.12
  570.5 3.0 collective-permute-done.42
  574.0 4.5 collective-permute-done.35
  578.5 3.3 collective-permute-start.13
  587.2 2.9 collective-permute-done.14
  591.6 3.4 collective-permute-done.15
  599.0 3.4 collective-permute-done.16
  603.6 2.7 collective-permute-start.28
  617.5 4.2 collective-permute-done.29
  623.1 3.7 collective-permute-done.22
  632.8 3.4 fusion.9
  638.9 2.4 collective-permute-done.31
  650.5 4.0 collective-permute-done.46
  655.5 2.5 fusion.8
  658.0 5.3 shard_map.285
  (399 shorter events, 178.4 us)
Async XLA Ops:
  13.2 20.7 %collective-permute-start = (bf16[3,256,512]{2,1,0:T(8,128)(2,1)}, bf16[3,256,512]{2,1,0:T(8,128)(2,1)S(1)}, u32[]{:S(2)}, u32[]{:S(2)}) collective-permute-start(bf16[3,256,512]{2,1,0:T(8,128)(2,1)} %get-tuple-element.58.q_ref), channel_id=1, source_target_pairs={{0,2},{2,0},{1,3},{3,1},{4,6},{6,4},{5,7},{7,5},{8,10},{10,8},{9,1... | collective-permute-start | bytes 2359304 | tf_op jit(solution)/shard_map/ppermute | solution.py:642
  41.6 51.0 %collective-permute-start.1 = (bf16[3,256,512]{2,1,0:T(8,128)(2,1)S(1)}, bf16[3,256,512]{2,1,0:T(8,128)(2,1)S(1)}, u32[]{:S(2)}, u32[]{:S(2)}) collective-permute-start(bf16[3,256,512]{2,1,0:T(8,128)(2,1)S(1)} %get-tuple-element.65), channel_id=1, source_target_pairs={{0,2},{2,0},{1,3},{3,1},{4,6},{6,4},{5,7},{7,5},{8,10},{10,8},{9,1... | collective-permute-start | bytes 2359304 | tf_op jit(solution)/shard_map/ppermute | solution.py:642
  45.9 50.0 %collective-permute-start.6 = (bf16[3,512,512]{2,1,0:T(8,128)(2,1)}, bf16[3,512,512]{2,1,0:T(8,128)(2,1)}, u32[]{:S(2)}, u32[]{:S(2)}) collective-permute-start(bf16[3,512,512]{2,1,0:T(8,128)(2,1)} %bitcast_select_fusion), channel_id=1, source_target_pairs={{0,2},{1,3},{4,6},{5,7},{8,10},{9,11},{12,14},{13,15},{16,18},{17,... | collective-permute-start | bytes 4718600 | tf_op jit(solution)/shard_map/ppermute | solution.py:789
  50.1 42.5 %collective-permute-start.2 = (f32[3,4,256]{2,1,0:T(4,128)S(1)}, f32[3,4,256]{2,1,0:T(4,128)S(1)}, u32[]{:S(2)}, u32[]{:S(2)}) collective-permute-start(f32[3,4,256]{2,1,0:T(4,128)S(1)} %get-tuple-element.66), channel_id=1, source_target_pairs={{0,2},{2,0},{1,3},{3,1},{4,6},{6,4},{5,7},{7,5},{8,10},{10,8},{9,1... | collective-permute-start | bytes 36872 | tf_op jit(solution)/shard_map/ppermute | solution.py:642
  99.0 56.9 %collective-permute-start.7 = (bf16[3,512,512]{2,1,0:T(8,128)(2,1)}, bf16[3,512,512]{2,1,0:T(8,128)(2,1)}, u32[]{:S(2)}, u32[]{:S(2)}) collective-permute-start(bf16[3,512,512]{2,1,0:T(8,128)(2,1)} %broadcast_select_fusion.own_ref), channel_id=1, source_target_pairs={{0,1},{1,0},{2,3},{3,2},{4,5},{5,4},{6,7},{7,6},{8,9},{9,8},{10,11... | collective-permute-start | bytes 4718600 | tf_op jit(solution)/shard_map/ppermute | solution.py:642
  143.0 164.2 %collective-permute-start.4 = (bf16[3,256,1024]{2,1,0:T(8,128)(2,1)}, bf16[3,256,1024]{2,1,0:T(8,128)(2,1)}, u32[]{:S(2)}, u32[]{:S(2)}) collective-permute-start(bf16[3,256,1024]{2,1,0:T(8,128)(2,1)} %bitcast.55), channel_id=1, source_target_pairs={{0,1},{1,0},{2,3},{3,2},{4,5},{5,4},{6,7},{7,6},{8,9},{9,8},{10,11... | collective-permute-start | bytes 4718600 | tf_op jit(solution)/shard_map/ppermute | solution.py:642
  147.9 33.4 %collective-permute-start.75 = (bf16[384,1024]{1,0:T(8,128)(2,1)}, bf16[384,1024]{1,0:T(8,128)(2,1)S(1)}, u32[]{:S(2)}, u32[]{:S(2)}) collective-permute-start(bf16[384,1024]{1,0:T(8,128)(2,1)} %constant_dynamic-slice_fusion.10), channel_id=1, source_target_pairs={{0,8},{4,12},{8,0},{12,4},{16,24},{20,28},{24,16},{28,20},{1,9},{5... | collective-permute-start | bytes 2359304 | tf_op jit(solution)/shard_map/ppermute | solution.py:642
  150.8 33.9 %collective-permute-start.61 = (bf16[384,1024]{1,0:T(8,128)(2,1)}, bf16[384,1024]{1,0:T(8,128)(2,1)}, u32[]{:S(2)}, u32[]{:S(2)}) collective-permute-start(bf16[384,1024]{1,0:T(8,128)(2,1)} %constant_dynamic-slice_fusion.16), channel_id=1, source_target_pairs={{0,8},{4,12},{8,0},{12,4},{16,24},{20,28},{24,16},{28,20},{1,9},{5... | collective-permute-start | bytes 2359304 | tf_op jit(solution)/shard_map/ppermute | solution.py:642
  152.1 15.9 %collective-permute-start.89 = (bf16[256,1024]{1,0:T(8,128)(2,1)}, bf16[256,1024]{1,0:T(8,128)(2,1)S(1)}, u32[]{:S(2)}, u32[]{:S(2)}) collective-permute-start(bf16[256,1024]{1,0:T(8,128)(2,1)} %constant_dynamic-slice_fusion.4), channel_id=1, source_target_pairs={{0,2},{2,0},{1,3},{3,1},{4,6},{6,4},{5,7},{7,5},{8,10},{10,8},{9,1... | collective-permute-start | bytes 1572872 | tf_op jit(solution)/shard_map/ppermute | solution.py:642
  155.9 22.5 %collective-permute-start.82 = (bf16[256,1024]{1,0:T(8,128)(2,1)}, bf16[256,1024]{1,0:T(8,128)(2,1)}, u32[]{:S(2)}, u32[]{:S(2)}) collective-permute-start(bf16[256,1024]{1,0:T(8,128)(2,1)} %constant_dynamic-slice_fusion.7), channel_id=1, source_target_pairs={{0,2},{2,0},{1,3},{3,1},{4,6},{6,4},{5,7},{7,5},{8,10},{10,8},{9,1... | collective-permute-start | bytes 1572872 | tf_op jit(solution)/shard_map/ppermute | solution.py:642
  168.8 20.5 %collective-permute-start.68 = (bf16[384,1024]{1,0:T(8,128)(2,1)S(1)}, bf16[384,1024]{1,0:T(8,128)(2,1)S(1)}, u32[]{:S(2)}, u32[]{:S(2)}) collective-permute-start(bf16[384,1024]{1,0:T(8,128)(2,1)S(1)} %constant_dynamic-slice_fusion.13), channel_id=1, source_target_pairs={{0,4},{4,0},{8,12},{12,8},{16,20},{20,16},{24,28},{28,24},{1,5},{5... | collective-permute-start | bytes 2359304 | tf_op jit(solution)/shard_map/ppermute | solution.py:642
  178.4 27.7 %collective-permute-start.54 = (bf16[384,1024]{1,0:T(8,128)(2,1)S(1)}, bf16[384,1024]{1,0:T(8,128)(2,1)S(1)}, u32[]{:S(2)}, u32[]{:S(2)}) collective-permute-start(bf16[384,1024]{1,0:T(8,128)(2,1)S(1)} %constant_dynamic-slice_fusion.19), channel_id=1, source_target_pairs={{0,4},{4,0},{8,12},{12,8},{16,20},{20,16},{24,28},{28,24},{1,5},{5... | collective-permute-start | bytes 2359304 | tf_op jit(solution)/shard_map/ppermute | solution.py:642
  182.1 51.1 %collective-permute-start.96 = (bf16[1536,256]{1,0:T(8,128)(2,1)S(1)}, bf16[1536,256]{1,0:T(8,128)(2,1)S(1)}, u32[]{:S(2)}, u32[]{:S(2)}) collective-permute-start(bf16[1536,256]{1,0:T(8,128)(2,1)S(1)} %constant_dynamic-slice_fusion.1), channel_id=1, source_target_pairs={{0,4},{4,0},{8,12},{12,8},{16,20},{20,16},{24,28},{28,24},{1,5},{5... | collective-permute-start | bytes 2359304 | tf_op jit(solution)/shard_map/ppermute | solution.py:642
  184.7 43.9 %collective-permute-start.90 = (bf16[128,1024]{1,0:T(8,128)(2,1)S(1)}, bf16[128,1024]{1,0:T(8,128)(2,1)S(1)}, u32[]{:S(2)}, u32[]{:S(2)}) collective-permute-start(bf16[128,1024]{1,0:T(8,128)(2,1)S(1)} %constant_dynamic-slice_fusion.3), channel_id=1, source_target_pairs={{0,4},{4,0},{8,12},{12,8},{16,20},{20,16},{24,28},{28,24},{1,5},{5... | collective-permute-start | bytes 786440 | tf_op jit(solution)/shard_map/ppermute | solution.py:642
  189.3 42.1 %collective-permute-start.83 = (bf16[128,1024]{1,0:T(8,128)(2,1)S(1)}, bf16[128,1024]{1,0:T(8,128)(2,1)S(1)}, u32[]{:S(2)}, u32[]{:S(2)}) collective-permute-start(bf16[128,1024]{1,0:T(8,128)(2,1)S(1)} %constant_dynamic-slice_fusion.6), channel_id=1, source_target_pairs={{0,4},{4,0},{8,12},{12,8},{16,20},{20,16},{24,28},{28,24},{1,5},{5... | collective-permute-start | bytes 786440 | tf_op jit(solution)/shard_map/ppermute | solution.py:642
  206.2 61.0 %collective-permute-start.76 = (bf16[192,1024]{1,0:T(8,128)(2,1)S(1)}, bf16[192,1024]{1,0:T(8,128)(2,1)S(1)}, u32[]{:S(2)}, u32[]{:S(2)}) collective-permute-start(bf16[192,1024]{1,0:T(8,128)(2,1)S(1)} %constant_dynamic-slice_fusion.9), channel_id=1, source_target_pairs={{0,2},{2,0},{1,3},{3,1},{4,6},{6,4},{5,7},{7,5},{8,10},{10,8},{9,1... | collective-permute-start | bytes 1179656 | tf_op jit(solution)/shard_map/ppermute | solution.py:642
  228.6 38.7 %collective-permute-start.62 = (bf16[192,1024]{1,0:T(8,128)(2,1)S(1)}, bf16[192,1024]{1,0:T(8,128)(2,1)S(1)}, u32[]{:S(2)}, u32[]{:S(2)}) collective-permute-start(bf16[192,1024]{1,0:T(8,128)(2,1)S(1)} %constant_dynamic-slice_fusion.15), channel_id=1, source_target_pairs={{0,2},{2,0},{1,3},{3,1},{4,6},{6,4},{5,7},{7,5},{8,10},{10,8},{9,1... | collective-permute-start | bytes 1179656 | tf_op jit(solution)/shard_map/ppermute | solution.py:642
  231.4 36.9 %collective-permute-start.69 = (bf16[192,1024]{1,0:T(8,128)(2,1)S(1)}, bf16[192,1024]{1,0:T(8,128)(2,1)S(1)}, u32[]{:S(2)}, u32[]{:S(2)}) collective-permute-start(bf16[192,1024]{1,0:T(8,128)(2,1)S(1)} %constant_dynamic-slice_fusion.12), channel_id=1, source_target_pairs={{0,8},{4,12},{8,0},{12,4},{16,24},{20,28},{24,16},{28,20},{1,9},{5... | collective-permute-start | bytes 1179656 | tf_op jit(solution)/shard_map/ppermute | solution.py:642
  233.3 10.2 %collective-permute-start.91 = (bf16[64,1024]{1,0:T(8,128)(2,1)S(1)}, bf16[64,1024]{1,0:T(8,128)(2,1)S(1)}, u32[]{:S(2)}, u32[]{:S(2)}) collective-permute-start(bf16[64,1024]{1,0:T(8,128)(2,1)S(1)} %constant_dynamic-slice_fusion.2), channel_id=1, source_target_pairs={{0,8},{4,12},{8,0},{12,4},{16,24},{20,28},{24,16},{28,20},{1,9},{5... | collective-permute-start | bytes 393224 | tf_op jit(solution)/shard_map/ppermute | solution.py:642
  265.8 10.9 %collective-permute-start.55 = (bf16[192,1024]{1,0:T(8,128)(2,1)S(1)}, bf16[192,1024]{1,0:T(8,128)(2,1)S(1)}, u32[]{:S(2)}, u32[]{:S(2)}) collective-permute-start(bf16[192,1024]{1,0:T(8,128)(2,1)S(1)} %constant_dynamic-slice_fusion.18), channel_id=1, source_target_pairs={{0,8},{4,12},{8,0},{12,4},{16,24},{20,28},{24,16},{28,20},{1,9},{5... | collective-permute-start | bytes 1179656 | tf_op jit(solution)/shard_map/ppermute | solution.py:642
  267.2 40.6 %collective-permute-start.5 = (bf16[3,256,1024]{2,1,0:T(8,128)(2,1)S(1)}, bf16[3,256,1024]{2,1,0:T(8,128)(2,1)S(1)}, u32[]{:S(2)}, u32[]{:S(2)}) collective-permute-start(bf16[3,256,1024]{2,1,0:T(8,128)(2,1)S(1)} %bitcast.54), channel_id=1, source_target_pairs={{0,1},{1,0},{2,3},{3,2},{4,5},{5,4},{6,7},{7,6},{8,9},{9,8},{10,11... | collective-permute-start | bytes 4718600 | tf_op jit(solution)/shard_map/ppermute | solution.py:642
  267.3 17.5 %collective-permute-start.97 = (bf16[768,256]{1,0:T(8,128)(2,1)S(1)}, bf16[768,256]{1,0:T(8,128)(2,1)S(1)}, u32[]{:S(2)}, u32[]{:S(2)}) collective-permute-start(bf16[768,256]{1,0:T(8,128)(2,1)S(1)} %constant_dynamic-slice_fusion), channel_id=1, source_target_pairs={{0,8},{4,12},{8,0},{12,4},{16,24},{20,28},{24,16},{28,20},{1,9},{5... | collective-permute-start | bytes 1179656 | tf_op jit(solution)/shard_map/ppermute | solution.py:642
  268.3 17.9 %collective-permute-start.93 = (bf16[64,1024]{1,0:T(8,128)(2,1)S(1)}, bf16[64,1024]{1,0:T(8,128)(2,1)S(1)}, u32[]{:S(2)}, u32[]{:S(2)}) collective-permute-start(bf16[64,1024]{1,0:T(8,128)(2,1)S(1)} %add_convert_fusion.31), channel_id=1, source_target_pairs={{0,8},{4,12},{8,0},{12,4},{16,24},{20,28},{24,16},{28,20},{1,9},{5... | collective-permute-start | bytes 393224 | tf_op jit(solution)/shard_map/ppermute | solution.py:642
  276.7 10.9 %collective-permute-start.86 = (bf16[64,1024]{1,0:T(8,128)(2,1)S(1)}, bf16[64,1024]{1,0:T(8,128)(2,1)S(1)}, u32[]{:S(2)}, u32[]{:S(2)}) collective-permute-start(bf16[64,1024]{1,0:T(8,128)(2,1)S(1)} %add_convert_fusion.33), channel_id=1, source_target_pairs={{0,8},{4,12},{8,0},{12,4},{16,24},{20,28},{24,16},{28,20},{1,9},{5... | collective-permute-start | bytes 393224 | tf_op jit(solution)/shard_map/ppermute | solution.py:642
  297.0 46.4 %collective-permute-start.98 = (bf16[768,256]{1,0:T(8,128)(2,1)S(1)}, bf16[768,256]{1,0:T(8,128)(2,1)S(1)}, u32[]{:S(2)}, u32[]{:S(2)}) collective-permute-start(bf16[768,256]{1,0:T(8,128)(2,1)S(1)} %add_convert_fusion.11), channel_id=1, source_target_pairs={{0,16},{4,20},{8,24},{12,28},{16,0},{20,4},{24,8},{28,12},{1,17},{... | collective-permute-start | bytes 1179656 | tf_op jit(solution)/shard_map/ppermute | solution.py:642
  301.9 32.5 %collective-permute-start.78 = (bf16[96,1024]{1,0:T(8,128)(2,1)S(1)}, bf16[96,1024]{1,0:T(8,128)(2,1)S(1)}, u32[]{:S(2)}, u32[]{:S(2)}) collective-permute-start(bf16[96,1024]{1,0:T(8,128)(2,1)S(1)} %add_convert_fusion.22), channel_id=1, source_target_pairs={{0,16},{4,20},{8,24},{12,28},{16,0},{20,4},{24,8},{28,12},{1,17},{... | collective-permute-start | bytes 589832 | tf_op jit(solution)/shard_map/ppermute | solution.py:642
  304.7 40.4 %collective-permute-start.71 = (bf16[96,1024]{1,0:T(8,128)(2,1)S(1)}, bf16[96,1024]{1,0:T(8,128)(2,1)S(1)}, u32[]{:S(2)}, u32[]{:S(2)}) collective-permute-start(bf16[96,1024]{1,0:T(8,128)(2,1)S(1)} %add_convert_fusion.24), channel_id=1, source_target_pairs={{0,16},{4,20},{8,24},{12,28},{16,0},{20,4},{24,8},{28,12},{1,17},{... | collective-permute-start | bytes 589832 | tf_op jit(solution)/shard_map/ppermute | solution.py:642
  307.2 35.6 %collective-permute-start.64 = (bf16[96,1024]{1,0:T(8,128)(2,1)S(1)}, bf16[96,1024]{1,0:T(8,128)(2,1)S(1)}, u32[]{:S(2)}, u32[]{:S(2)}) collective-permute-start(bf16[96,1024]{1,0:T(8,128)(2,1)S(1)} %add_convert_fusion.26), channel_id=1, source_target_pairs={{0,16},{4,20},{8,24},{12,28},{16,0},{20,4},{24,8},{28,12},{1,17},{... | collective-permute-start | bytes 589832 | tf_op jit(solution)/shard_map/ppermute | solution.py:642
  307.8 38.5 %collective-permute-start.57 = (bf16[96,1024]{1,0:T(8,128)(2,1)S(1)}, bf16[96,1024]{1,0:T(8,128)(2,1)S(1)}, u32[]{:S(2)}, u32[]{:S(2)}) collective-permute-start(bf16[96,1024]{1,0:T(8,128)(2,1)S(1)} %add_convert_fusion.28), channel_id=1, source_target_pairs={{0,16},{4,20},{8,24},{12,28},{16,0},{20,4},{24,8},{28,12},{1,17},{... | collective-permute-start | bytes 589832 | tf_op jit(solution)/shard_map/ppermute | solution.py:642
  334.4 47.5 %collective-permute-start.95 = (bf16[256,1024]{1,0:T(8,128)(2,1)S(1)}, bf16[256,1024]{1,0:T(8,128)(2,1)S(1)}, u32[]{:S(2)}, u32[]{:S(2)}) collective-permute-start(bf16[256,1024]{1,0:T(8,128)(2,1)S(1)} %maximum_select_fusion.19), channel_id=1, source_target_pairs={{0,2},{2,0},{1,3},{3,1},{4,6},{6,4},{5,7},{7,5},{8,10},{10,8},{9,1... | collective-permute-start | bytes 1572872 | tf_op jit(solution)/shard_map/ppermute | solution.py:642
  342.8 41.6 %collective-permute-start.88 = (bf16[256,1024]{1,0:T(8,128)(2,1)S(1)}, bf16[256,1024]{1,0:T(8,128)(2,1)S(1)}, u32[]{:S(2)}, u32[]{:S(2)}) collective-permute-start(bf16[256,1024]{1,0:T(8,128)(2,1)S(1)} %maximum_select_fusion.18), channel_id=1, source_target_pairs={{0,2},{2,0},{1,3},{3,1},{4,6},{6,4},{5,7},{7,5},{8,10},{10,8},{9,1... | collective-permute-start | bytes 1572872 | tf_op jit(solution)/shard_map/ppermute | solution.py:642
  343.5 80.7 %collective-permute-start.8 = (bf16[3,256,512]{2,1,0:T(8,128)(2,1)S(1)}, bf16[3,256,512]{2,1,0:T(8,128)(2,1)S(1)}, u32[]{:S(2)}, u32[]{:S(2)}) collective-permute-start(bf16[3,256,512]{2,1,0:T(8,128)(2,1)S(1)} %get-tuple-element.77.gm_ref), channel_id=1, source_target_pairs={{0,2},{2,0},{1,3},{3,1},{4,6},{6,4},{5,7},{7,5},{8,10},{10,8},{9,1... | collective-permute-start | bytes 2359304 | tf_op jit(solution)/shard_map/ppermute | solution.py:642
  350.8 28.8 %collective-permute-start.72 = (bf16[96,1024]{1,0:T(8,128)(2,1)S(1)}, bf16[96,1024]{1,0:T(8,128)(2,1)S(1)}, u32[]{:S(2)}, u32[]{:S(2)}) collective-permute-start(bf16[96,1024]{1,0:T(8,128)(2,1)S(1)} %add_convert_fusion.23), channel_id=1, source_target_pairs={{0,2},{2,0},{1,3},{3,1},{4,6},{6,4},{5,7},{7,5},{8,10},{10,8},{9,1... | collective-permute-start | bytes 589832 | tf_op jit(solution)/shard_map/ppermute | solution.py:642
  352.9 28.8 %collective-permute-start.58 = (bf16[96,1024]{1,0:T(8,128)(2,1)S(1)}, bf16[96,1024]{1,0:T(8,128)(2,1)S(1)}, u32[]{:S(2)}, u32[]{:S(2)}) collective-permute-start(bf16[96,1024]{1,0:T(8,128)(2,1)S(1)} %add_convert_fusion.27), channel_id=1, source_target_pairs={{0,2},{2,0},{1,3},{3,1},{4,6},{6,4},{5,7},{7,5},{8,10},{10,8},{9,1... | collective-permute-start | bytes 589832 | tf_op jit(solution)/shard_map/ppermute | solution.py:642
  379.7 43.6 %collective-permute-start.9 = (f32[3,8,256]{2,1,0:T(8,128)S(1)}, f32[3,8,256]{2,1,0:T(8,128)S(1)}, u32[]{:S(2)}, u32[]{:S(2)}) collective-permute-start(f32[3,8,256]{2,1,0:T(8,128)S(1)} %get-tuple-element.78.stats_ref), channel_id=1, source_target_pairs={{0,2},{2,0},{1,3},{3,1},{4,6},{6,4},{5,7},{7,5},{8,10},{10,8},{9,1... | collective-permute-start | bytes 73736 | tf_op jit(solution)/shard_map/ppermute | solution.py:642
  381.8 12.1 %collective-permute-start.99 = (bf16[768,256]{1,0:T(8,128)(2,1)S(1)}, bf16[768,256]{1,0:T(8,128)(2,1)S(1)}, u32[]{:S(2)}, u32[]{:S(2)}) collective-permute-start(bf16[768,256]{1,0:T(8,128)(2,1)S(1)} %add_convert_fusion.10), channel_id=1, source_target_pairs={{0,8},{4,12},{8,0},{12,4},{16,24},{20,28},{24,16},{28,20},{1,9},{5... | collective-permute-start | bytes 1179656 | tf_op jit(solution)/shard_map/ppermute | solution.py:642
  381.9 23.2 %collective-permute-start.47 = (bf16[256,1024]{1,0:T(8,128)(2,1)S(1)}, bf16[256,1024]{1,0:T(8,128)(2,1)S(1)}, u32[]{:S(2)}, u32[]{:S(2)}) collective-permute-start(bf16[256,1024]{1,0:T(8,128)(2,1)S(1)} %constant_dynamic-slice_fusion.22), channel_id=1, source_target_pairs={{0,8},{4,12},{8,0},{12,4},{16,24},{20,28},{24,16},{28,20},{1,9},{5... | collective-permute-start | bytes 1572872 | tf_op jit(solution)/shard_map/ppermute | solution.py:642
  384.5 21.1 %collective-permute-start.80 = (bf16[192,1024]{1,0:T(8,128)(2,1)S(1)}, bf16[192,1024]{1,0:T(8,128)(2,1)S(1)}, u32[]{:S(2)}, u32[]{:S(2)}) collective-permute-start(bf16[192,1024]{1,0:T(8,128)(2,1)S(1)} %maximum_select_fusion.25), channel_id=1, source_target_pairs={{0,2},{2,0},{1,3},{3,1},{4,6},{6,4},{5,7},{7,5},{8,10},{10,8},{9,1... | collective-permute-start | bytes 1179656 | tf_op jit(solution)/shard_map/ppermute | solution.py:642
  393.8 19.7 %collective-permute-start.73 = (bf16[192,1024]{1,0:T(8,128)(2,1)S(1)}, bf16[192,1024]{1,0:T(8,128)(2,1)S(1)}, u32[]{:S(2)}, u32[]{:S(2)}) collective-permute-start(bf16[192,1024]{1,0:T(8,128)(2,1)S(1)} %maximum_select_fusion.24), channel_id=1, source_target_pairs={{0,8},{4,12},{8,0},{12,4},{16,24},{20,28},{24,16},{28,20},{1,9},{5... | collective-permute-start | bytes 1179656 | tf_op jit(solution)/shard_map/ppermute | solution.py:642
  405.1 10.5 %collective-permute-start.66 = (bf16[192,1024]{1,0:T(8,128)(2,1)S(1)}, bf16[192,1024]{1,0:T(8,128)(2,1)S(1)}, u32[]{:S(2)}, u32[]{:S(2)}) collective-permute-start(bf16[192,1024]{1,0:T(8,128)(2,1)S(1)} %maximum_select_fusion.23), channel_id=1, source_target_pairs={{0,2},{2,0},{1,3},{3,1},{4,6},{6,4},{5,7},{7,5},{8,10},{10,8},{9,1... | collective-permute-start | bytes 1179656 | tf_op jit(solution)/shard_map/ppermute | solution.py:642
  405.6 13.5 %collective-permute-start.59 = (bf16[192,1024]{1,0:T(8,128)(2,1)S(1)}, bf16[192,1024]{1,0:T(8,128)(2,1)S(1)}, u32[]{:S(2)}, u32[]{:S(2)}) collective-permute-start(bf16[192,1024]{1,0:T(8,128)(2,1)S(1)} %maximum_select_fusion.22), channel_id=1, source_target_pairs={{0,8},{4,12},{8,0},{12,4},{16,24},{20,28},{24,16},{28,20},{1,9},{5... | collective-permute-start | bytes 1179656 | tf_op jit(solution)/shard_map/ppermute | solution.py:642
  413.5 48.5 %collective-permute-start.100 = (bf16[1536,256]{1,0:T(8,128)(2,1)}, bf16[1536,256]{1,0:T(8,128)(2,1)}, u32[]{:S(2)}, u32[]{:S(2)}) collective-permute-start(bf16[1536,256]{1,0:T(8,128)(2,1)} %maximum_select_fusion.14), channel_id=1, source_target_pairs={{0,4},{4,0},{8,12},{12,8},{16,20},{20,16},{24,28},{28,24},{1,5},{5... | collective-permute-start | bytes 2359304 | tf_op jit(solution)/shard_map/ppermute | solution.py:642
  419.2 73.1 %collective-permute-start.81 = (bf16[384,1024]{1,0:T(8,128)(2,1)S(1)}, bf16[384,1024]{1,0:T(8,128)(2,1)}, u32[]{:S(2)}, u32[]{:S(2)}) collective-permute-start(bf16[384,1024]{1,0:T(8,128)(2,1)S(1)} %maximum_select_fusion.13), channel_id=1, source_target_pairs={{0,8},{4,12},{8,0},{12,4},{16,24},{20,28},{24,16},{28,20},{1,9},{5... | collective-permute-start | bytes 2359304 | tf_op jit(solution)/shard_map/ppermute | solution.py:642
  421.9 56.8 %collective-permute-start.74 = (bf16[384,1024]{1,0:T(8,128)(2,1)}, bf16[384,1024]{1,0:T(8,128)(2,1)}, u32[]{:S(2)}, u32[]{:S(2)}) collective-permute-start(bf16[384,1024]{1,0:T(8,128)(2,1)} %maximum_select_fusion.12), channel_id=1, source_target_pairs={{0,4},{4,0},{8,12},{12,8},{16,20},{20,16},{24,28},{28,24},{1,5},{5... | collective-permute-start | bytes 2359304 | tf_op jit(solution)/shard_map/ppermute | solution.py:642
  423.3 25.5 %collective-permute-start.49 = (bf16[64,1024]{1,0:T(8,128)(2,1)S(1)}, bf16[64,1024]{1,0:T(8,128)(2,1)S(1)}, u32[]{:S(2)}, u32[]{:S(2)}) collective-permute-start(bf16[64,1024]{1,0:T(8,128)(2,1)S(1)} %constant_dynamic-slice_fusion.20), channel_id=1, source_target_pairs={{0,4},{4,0},{8,12},{12,8},{16,20},{20,16},{24,28},{28,24},{1,5},{5... | collective-permute-start | bytes 393224 | tf_op jit(solution)/shard_map/ppermute | solution.py:642
  457.0 16.2 %collective-permute-start.40 = (bf16[256,1024]{1,0:T(8,128)(2,1)S(1)}, bf16[256,1024]{1,0:T(8,128)(2,1)S(1)}, u32[]{:S(2)}, u32[]{:S(2)}) collective-permute-start(bf16[256,1024]{1,0:T(8,128)(2,1)S(1)} %constant_dynamic-slice_fusion.25), channel_id=1, source_target_pairs={{0,4},{4,0},{8,12},{12,8},{16,20},{20,16},{24,28},{28,24},{1,5},{5... | collective-permute-start | bytes 1572872 | tf_op jit(solution)/shard_map/ppermute | solution.py:642
  462.0 33.1 %collective-permute-start.67 = (bf16[384,1024]{1,0:T(8,128)(2,1)S(1)}, bf16[384,1024]{1,0:T(8,128)(2,1)S(1)}, u32[]{:S(2)}, u32[]{:S(2)}) collective-permute-start(bf16[384,1024]{1,0:T(8,128)(2,1)S(1)} %copy-done.37), channel_id=1, source_target_pairs={{0,8},{4,12},{8,0},{12,4},{16,24},{20,28},{24,16},{28,20},{1,9},{5... | collective-permute-start | bytes 2359304 | tf_op jit(solution)/shard_map/ppermute | solution.py:642
  462.1 14.9 %collective-permute-start.33 = (bf16[256,1024]{1,0:T(8,128)(2,1)S(1)}, bf16[256,1024]{1,0:T(8,128)(2,1)S(1)}, u32[]{:S(2)}, u32[]{:S(2)}) collective-permute-start(bf16[256,1024]{1,0:T(8,128)(2,1)S(1)} %constant_dynamic-slice_fusion.28), channel_id=1, source_target_pairs={{0,2},{2,0},{1,3},{3,1},{4,6},{6,4},{5,7},{7,5},{8,10},{10,8},{9,1... | collective-permute-start | bytes 1572872 | tf_op jit(solution)/shard_map/ppermute | solution.py:642
  473.2 14.4 %collective-permute-start.60 = (bf16[384,1024]{1,0:T(8,128)(2,1)S(1)}, bf16[384,1024]{1,0:T(8,128)(2,1)S(1)}, u32[]{:S(2)}, u32[]{:S(2)}) collective-permute-start(bf16[384,1024]{1,0:T(8,128)(2,1)S(1)} %copy-done.38), channel_id=1, source_target_pairs={{0,4},{4,0},{8,12},{12,8},{16,20},{20,16},{24,28},{28,24},{1,5},{5... | collective-permute-start | bytes 2359304 | tf_op jit(solution)/shard_map/ppermute | solution.py:642
  477.0 28.4 %collective-permute-start.10 = (bf16[3,256,512]{2,1,0:T(8,128)(2,1)S(1)}, bf16[3,256,512]{2,1,0:T(8,128)(2,1)S(1)}, u32[]{:S(2)}, u32[]{:S(2)}) collective-permute-start(bf16[3,256,512]{2,1,0:T(8,128)(2,1)S(1)} %get-tuple-element.84), channel_id=1, source_target_pairs={{0,2},{2,0},{1,3},{3,1},{4,6},{6,4},{5,7},{7,5},{8,10},{10,8},{9,1... | collective-permute-start | bytes 2359304 | tf_op jit(solution)/shard_map/ppermute | solution.py:642
  478.7 23.7 %collective-permute-start.52 = (bf16[128,1024]{1,0:T(8,128)(2,1)S(1)}, bf16[128,1024]{1,0:T(8,128)(2,1)S(1)}, u32[]{:S(2)}, u32[]{:S(2)}) collective-permute-start(bf16[128,1024]{1,0:T(8,128)(2,1)S(1)} %maximum_select_fusion.29), channel_id=1, source_target_pairs={{0,2},{2,0},{1,3},{3,1},{4,6},{6,4},{5,7},{7,5},{8,10},{10,8},{9,1... | collective-permute-start | bytes 786440 | tf_op jit(solution)/shard_map/ppermute | solution.py:642
  487.6 75.6 %collective-permute-start.41 = (bf16[128,1024]{1,0:T(8,128)(2,1)}, bf16[128,1024]{1,0:T(8,128)(2,1)}, u32[]{:S(2)}, u32[]{:S(2)}) collective-permute-start(bf16[128,1024]{1,0:T(8,128)(2,1)} %constant_dynamic-slice_fusion.24), channel_id=1, source_target_pairs={{0,8},{4,12},{8,0},{12,4},{16,24},{20,28},{24,16},{28,20},{1,9},{5... | collective-permute-start | bytes 786440 | tf_op jit(solution)/shard_map/ppermute | solution.py:642
  492.2 25.6 %collective-permute-start.34 = (bf16[128,1024]{1,0:T(8,128)(2,1)}, bf16[128,1024]{1,0:T(8,128)(2,1)}, u32[]{:S(2)}, u32[]{:S(2)}) collective-permute-start(bf16[128,1024]{1,0:T(8,128)(2,1)} %constant_dynamic-slice_fusion.27), channel_id=1, source_target_pairs={{0,4},{4,0},{8,12},{12,8},{16,20},{20,16},{24,28},{28,24},{1,5},{5... | collective-permute-start | bytes 786440 | tf_op jit(solution)/shard_map/ppermute | solution.py:642
  503.3 127.8 %collective-permute-start.53 = (bf16[256,1024]{1,0:T(8,128)(2,1)}, bf16[256,1024]{1,0:T(8,128)(2,1)}, u32[]{:S(2)}, u32[]{:S(2)}) collective-permute-start(bf16[256,1024]{1,0:T(8,128)(2,1)} %maximum_select_fusion.17), channel_id=1, source_target_pairs={{0,8},{4,12},{8,0},{12,4},{16,24},{20,28},{24,16},{28,20},{1,9},{5... | collective-permute-start | bytes 1572872 | tf_op jit(solution)/shard_map/ppermute | solution.py:642
  513.8 144.2 %collective-permute-start.11 = (bf16[3,256,1024]{2,1,0:T(8,128)(2,1)S(1)}, bf16[3,256,1024]{2,1,0:T(8,128)(2,1)}, u32[]{:S(2)}, u32[]{:S(2)}) collective-permute-start(bf16[3,256,1024]{2,1,0:T(8,128)(2,1)S(1)} %copy-done.2), channel_id=1, source_target_pairs={{0,1},{1,0},{2,3},{3,2},{4,5},{5,4},{6,7},{7,6},{8,9},{9,8},{10,11... | collective-permute-start | bytes 4718600 | tf_op jit(solution)/shard_map/ppermute | solution.py:642
  514.5 67.4 %collective-permute-start.26 = (bf16[192,512]{1,0:T(8,128)(2,1)}, bf16[192,512]{1,0:T(8,128)(2,1)}, u32[]{:S(2)}, u32[]{:S(2)}) collective-permute-start(bf16[192,512]{1,0:T(8,128)(2,1)} %constant_dynamic-slice_fusion.31), channel_id=1, source_target_pairs={{0,8},{4,12},{8,0},{12,4},{16,24},{20,28},{24,16},{28,20},{1,9},{5... | collective-permute-start | bytes 589832 | tf_op jit(solution)/shard_map/ppermute | solution.py:642
  517.9 68.2 %collective-permute-start.19 = (bf16[192,512]{1,0:T(8,128)(2,1)}, bf16[192,512]{1,0:T(8,128)(2,1)}, u32[]{:S(2)}, u32[]{:S(2)}) collective-permute-start(bf16[192,512]{1,0:T(8,128)(2,1)} %constant_dynamic-slice_fusion.34), channel_id=1, source_target_pairs={{0,4},{4,0},{8,12},{12,8},{16,20},{20,16},{24,28},{28,24},{1,5},{5... | collective-permute-start | bytes 589832 | tf_op jit(solution)/shard_map/ppermute | solution.py:642
  581.9 14.8 %collective-permute-start.43 = (bf16[64,1024]{1,0:T(8,128)(2,1)S(1)}, bf16[64,1024]{1,0:T(8,128)(2,1)S(1)}, u32[]{:S(2)}, u32[]{:S(2)}) collective-permute-start(bf16[64,1024]{1,0:T(8,128)(2,1)S(1)} %add_convert_fusion.38), channel_id=1, source_target_pairs={{0,16},{4,20},{8,24},{12,28},{16,0},{20,4},{24,8},{28,12},{1,17},{... | collective-permute-start | bytes 393224 | tf_op jit(solution)/shard_map/ppermute | solution.py:642
  584.5 13.9 %collective-permute-start.36 = (bf16[64,1024]{1,0:T(8,128)(2,1)S(1)}, bf16[64,1024]{1,0:T(8,128)(2,1)S(1)}, u32[]{:S(2)}, u32[]{:S(2)}) collective-permute-start(bf16[64,1024]{1,0:T(8,128)(2,1)S(1)} %add_convert_fusion.40), channel_id=1, source_target_pairs={{0,16},{4,20},{8,24},{12,28},{16,0},{20,4},{24,8},{28,12},{1,17},{... | collective-permute-start | bytes 393224 | tf_op jit(solution)/shard_map/ppermute | solution.py:642
  602.4 26.4 %collective-permute-start.44 = (bf16[64,1024]{1,0:T(8,128)(2,1)S(1)}, bf16[64,1024]{1,0:T(8,128)(2,1)S(1)}, u32[]{:S(2)}, u32[]{:S(2)}) collective-permute-start(bf16[64,1024]{1,0:T(8,128)(2,1)S(1)} %add_convert_fusion.37), channel_id=1, source_target_pairs={{0,2},{2,0},{1,3},{3,1},{4,6},{6,4},{5,7},{7,5},{8,10},{10,8},{9,1... | collective-permute-start | bytes 393224 | tf_op jit(solution)/shard_map/ppermute | solution.py:642
  602.5 28.4 %collective-permute-start.37 = (bf16[64,1024]{1,0:T(8,128)(2,1)S(1)}, bf16[64,1024]{1,0:T(8,128)(2,1)S(1)}, u32[]{:S(2)}, u32[]{:S(2)}) collective-permute-start(bf16[64,1024]{1,0:T(8,128)(2,1)S(1)} %add_convert_fusion.39), channel_id=1, source_target_pairs={{0,8},{4,12},{8,0},{12,4},{16,24},{20,28},{24,16},{28,20},{1,9},{5... | collective-permute-start | bytes 393224 | tf_op jit(solution)/shard_map/ppermute | solution.py:642
  626.7 11.5 %collective-permute-start.18 = (bf16[128,512]{1,0:T(8,128)(2,1)S(1)}, bf16[128,512]{1,0:T(8,128)(2,1)S(1)}, u32[]{:S(2)}, u32[]{:S(2)}) collective-permute-start(bf16[128,512]{1,0:T(8,128)(2,1)S(1)} %maximum_select_fusion.34), channel_id=1, source_target_pairs={{0,2},{2,0},{1,3},{3,1},{4,6},{6,4},{5,7},{7,5},{8,10},{10,8},{9,1... | collective-permute-start | bytes 393224 | tf_op jit(solution)/shard_map/ppermute | solution.py:642
  631.1 13.9 %collective-permute-start.45 = (bf16[128,1024]{1,0:T(8,128)(2,1)S(1)}, bf16[128,1024]{1,0:T(8,128)(2,1)S(1)}, u32[]{:S(2)}, u32[]{:S(2)}) collective-permute-start(bf16[128,1024]{1,0:T(8,128)(2,1)S(1)} %maximum_select_fusion.28), channel_id=1, source_target_pairs={{0,8},{4,12},{8,0},{12,4},{16,24},{20,28},{24,16},{28,20},{1,9},{5... | collective-permute-start | bytes 786440 | tf_op jit(solution)/shard_map/ppermute | solution.py:642
  645.4 9.5 %collective-permute-start.39 = (bf16[256,1024]{1,0:T(8,128)(2,1)S(1)}, bf16[256,1024]{1,0:T(8,128)(2,1)S(1)}, u32[]{:S(2)}, u32[]{:S(2)}) collective-permute-start(bf16[256,1024]{1,0:T(8,128)(2,1)S(1)} %maximum_select_fusion.15), channel_id=1, source_target_pairs={{0,2},{2,0},{1,3},{3,1},{4,6},{6,4},{5,7},{7,5},{8,10},{10,8},{9,1... | collective-permute-start | bytes 1572872 | tf_op jit(solution)/shard_map/ppermute | solution.py:642
  (87 other events, 716.6 us)

commit v3 on v2

v3 whole, which is shorter than its diff:
```python
import functools

import jax
import jax.numpy as jnp
from jax import lax
from jax.experimental import pallas as pl
from jax.experimental.pallas import tpu as pltpu
from jax.sharding import PartitionSpec as P

HD = 128
RATE = 3
EPS = 1e-05
NEG = -1000000000.0
LOG2E = 1.4426950408889634
SCALE = HD ** (-0.5)
GELU_ROOT = 0.7978845608028654
GELU_CUBE = 0.044715

ORDER = (
    "ffn", "hidden", "own", "ffn3", "output", "other", "f1", "f2", "grads", "evict", "f1",
    "query", "kv", "input", "f1", "kv", "f2", "kv", "f1", "f2", "oq", "evict2", "kv", "compr",
    "f1", "kv", "oq", "f2", "oq", "compress", "kv", "f2", "oq", "f1", "compress", "oq", "f2",
    "kv", "compress", "oq", "compress", "f1", "oq", "compress", "f2",
)

PATHS = {
    "f1": "xyz/yzx",
    "f2": "zyx/yxz",
    "kv": "xzy/zxy",
    "oq": "zxy/xyz",
    "compress": "yz/zy",
}

COST = 1e8
VMEM_WIDE = 40

LOW = jnp.bfloat16
WIDE = jnp.float32
NN = (((1,), (0,)), ((), ()))
NT = (((1,), (1,)), ((), ()))
TN = (((0,), (0,)), ((), ()))


def dot(first, second, dims=NN):
    return lax.dot_general(first, second, dims, preferred_element_type=WIDE)


def norm_stats(values):
    centre = values - jnp.mean(values, axis=-1, keepdims=True)
    inverse = lax.rsqrt(jnp.mean(centre * centre, axis=-1, keepdims=True) + EPS)
    return (centre * inverse, inverse)


def norm_back(grad_normed, normed, inverse, gain_vector):
    scaled = grad_normed * gain_vector
    return inverse * (
        scaled
        - jnp.mean(scaled, axis=-1, keepdims=True)
        - normed * jnp.mean(scaled * normed, axis=-1, keepdims=True)
    )


def per_stream(array_shape):
    block = (1,) + tuple(array_shape[1:])
    zeros = (0,) * (len(block) - 1)
    return pl.BlockSpec(block, lambda s: (s,) + zeros)


def whole(array_shape):
    return pl.BlockSpec(memory_space=pltpu.VMEM)


def whole_block(array_shape):
    zeros = (0,) * len(array_shape)
    return pl.BlockSpec(tuple(array_shape), lambda *_: zeros)


def scalars():
    return pl.BlockSpec(memory_space=pltpu.SMEM)


def shaped(shape, dtype=LOW):
    return jax.ShapeDtypeStruct(tuple(shape), dtype)


class Chain:
    def __init__(self):
        self.last = None

    def call(self, kernel, grid, in_specs, out_specs, out_shape, scratch=(), vmem=16, alias=None, us=1.0):
        last = self.last
        count = len(in_specs)

        def ordered(*refs):
            kernel(*refs[:count], *refs[count + 1 :])

        def run(*args):
            specs = list(in_specs)
            args = list(args)
            body = kernel
            if last is not None:
                specs.append(pl.BlockSpec(memory_space=pl.ANY))
                args.append(last)
                body = ordered
            outs = pl.pallas_call(
                body,
                grid=grid,
                in_specs=specs,
                out_specs=out_specs,
                out_shape=out_shape,
                scratch_shapes=list(scratch),
                input_output_aliases=alias or {},
                compiler_params=pltpu.CompilerParams(vmem_limit_bytes=vmem * 1024 * 1024),
                cost_estimate=pl.CostEstimate(
                    flops=int(us * COST), bytes_accessed=0, transcendentals=0
                ),
            )(*args)
            if not alias:
                self.last = outs[0] if isinstance(outs, (list, tuple)) else outs
            return outs

        return run


META_TIER, META_HEAD, META_DP, META_STREAMS = 0, 1, 2, 3


def any_spec():
    return pl.BlockSpec(memory_space=pl.ANY)


def query_kernel(meta_ref, x_ref, gain_ref, bias_ref, w_ref, unit_ref, low_ref, *outs):
    for stream in range(x_ref.shape[0]):
        normed, _ = norm_stats(x_ref[stream].astype(WIDE))
        unit_ref[stream] = normed.astype(LOW)
        low = (normed * gain_ref[...] + bias_ref[...]).astype(LOW)
        low_ref[stream] = low
        outs[stream][...] = dot(low, w_ref[...]).astype(LOW)


def query_rows(chain, meta, x, gain, bias, w):
    streams, rows, width = x.shape
    outs = [shaped(x.shape), shaped(x.shape)]
    outs += [shaped((rows, w.shape[1]))] * streams
    unit, low, *queries = chain.call(
        query_kernel,
        (1,),
        [scalars()] + [whole(v.shape) for v in (x, gain, bias, w)],
        [whole(o.shape) for o in outs],
        outs,
        us=3,
    )(meta, x, gain, bias, w)
    return unit, low, queries


def key_value_kernel(low_ref, wk_ref, wv_ref, k_ref, v_ref):
    k_ref[0] = dot(low_ref[0], wk_ref[...]).astype(LOW)
    v_ref[0] = dot(low_ref[0], wv_ref[...]).astype(LOW)


def key_values(chain, low, wk, wv):
    outs = [shaped(low.shape[:2] + wk.shape[1:])] * 2
    return chain.call(
        key_value_kernel,
        (low.shape[0],),
        [per_stream(low.shape), whole(wk.shape), whole(wv.shape)],
        [per_stream(o.shape) for o in outs],
        outs,
        us=2.5,
    )(low, wk, wv)


def stored_kernel(x_ref, gain_ref, bias_ref, wk_ref, wv_ref, unit_ref, k_ref, v_ref):
    normed, _ = norm_stats(x_ref[0, 0].astype(WIDE))
    unit_ref[0] = normed.astype(LOW)
    low = (normed * gain_ref[...] + bias_ref[...]).astype(LOW)
    k_ref[0] = dot(low, wk_ref[...]).astype(LOW)
    v_ref[0] = dot(low, wv_ref[...]).astype(LOW)


def stored_rows(chain, x, gain, bias, wk, wv):
    streams, _, slots, width = x.shape
    outs = [shaped((streams, slots, width))] + [shaped((streams, slots, wk.shape[1]))] * 2
    return chain.call(
        stored_kernel,
        (streams,),
        [per_stream(x.shape)] + [whole(v.shape) for v in (gain, bias, wk, wv)],
        [per_stream(o.shape) for o in outs],
        outs,
        us=6,
    )(x, gain, bias, wk, wv)


def slot_masks(own, meta_ref, stream, streams, slots, rows):
    tier = meta_ref[META_TIER]
    length = meta_ref[META_STREAMS + stream]
    filled = meta_ref[META_STREAMS + streams + stream]
    memory_ok = lax.broadcasted_iota(jnp.int32, (slots, rows), 0) < filled
    key_row = lax.broadcasted_iota(jnp.int32, (rows, rows), 0)
    segment_ok = (tier * rows + key_row) < length
    if own:
        query_row = lax.broadcasted_iota(jnp.int32, (rows, rows), 1)
        segment_ok = segment_ok & (key_row <= query_row)
    return memory_ok, segment_ok


def by_tier(own, meta_ref, body):
    if own:
        body(True)
        return

    @pl.when(meta_ref[META_TIER] == 0)
    def _():
        body(True)

    @pl.when(meta_ref[META_TIER] != 0)
    def _():
        body(False)


def put_packed(ref, row, value):
    count, width = value.shape
    for part in range(3):
        low = value.astype(LOW)
        ref[row + part * count : row + (part + 1) * count, :width] = low
        value = value - low.astype(WIDE)


def get_packed(ref, row, count, width):
    parts = [
        ref[row + part * count : row + (part + 1) * count, :width].astype(WIDE) for part in range(3)
    ]
    return parts[0] + (parts[1] + parts[2])


def packed_rows(count):
    return -(-3 * count // 16) * 16


def attend_kernel(own, stream, streams, meta_ref, q_ref, km_ref, vm_ref, ks_ref, vs_ref, out_ref, totals):
    slots, rows = km_ref.shape[1], q_ref.shape[0]
    heads = q_ref.shape[1] // HD

    def body(with_segment):
        memory_ok, segment_ok = slot_masks(own, meta_ref, stream, streams, slots, rows)
        for head in range(heads):
            cols = slice(head * HD, (head + 1) * HD)
            query = q_ref[:, cols]
            scores = jnp.where(
                memory_ok, dot(km_ref[0, :, cols], query, NT) * (SCALE * LOG2E), NEG
            )
            top = jnp.max(scores, axis=0, keepdims=True)
            if with_segment:
                near = jnp.where(
                    segment_ok, dot(ks_ref[0, :, cols], query, NT) * (SCALE * LOG2E), NEG
                )
                top = jnp.maximum(top, jnp.max(near, axis=0, keepdims=True))
            raw = jnp.exp2(scores - top)
            spent = jnp.sum(raw, axis=0, keepdims=True)
            mixed = dot(vm_ref[0, :, cols], raw.astype(LOW), TN)
            if with_segment:
                raw_near = jnp.exp2(near - top)
                spent = spent + jnp.sum(raw_near, axis=0, keepdims=True)
                mixed = mixed + dot(vs_ref[0, :, cols], raw_near.astype(LOW), TN)
            out_ref[:rows, cols] = (mixed / spent).T.astype(LOW)
            totals[head : head + 1, :] = top + jnp.log2(spent)
        put_packed(out_ref, rows, totals[...])

    by_tier(own, meta_ref, body)


def one_stream(array, stream):
    return pl.BlockSpec((1,) + array.shape[1:], lambda i: (stream, 0, 0))


def attend(chain, own, stream, meta, q, km, vm, ks, vs):
    rows, features = q.shape
    heads = features // HD
    out = shaped((rows + packed_rows(heads), features))
    return chain.call(
        functools.partial(attend_kernel, own, stream, km.shape[0]),
        (1,),
        [scalars(), whole(q.shape)] + [one_stream(a, stream) for a in (km, vm, ks, vs)],
        whole(out.shape),
        out,
        scratch=[pltpu.VMEM((heads, rows), WIDE)],
        us=2.6,
    )(meta, q, km, vm, ks, vs)


def merge_kernel(w_ref, own_ref, other_ref, low_ref, total_ref, part_ref):
    rows, features = low_ref.shape
    heads = features // HD
    first = get_packed(own_ref, rows, heads, rows)
    second = get_packed(other_ref, rows, heads, rows)
    top = jnp.maximum(first, second)
    total = top + jnp.log2(jnp.exp2(first - top) + jnp.exp2(second - top))
    total_ref[...] = total
    share_own, share_other = jnp.exp2(first - total), jnp.exp2(second - total)
    for head in range(heads):
        cols = slice(head * HD, (head + 1) * HD)
        column_own = jnp.broadcast_to(share_own[head : head + 1], (HD, rows)).T
        column_other = jnp.broadcast_to(share_other[head : head + 1], (HD, rows)).T
        merged = (
            own_ref[:rows, cols].astype(WIDE) * column_own
            + other_ref[:rows, cols].astype(WIDE) * column_other
        )
        low_ref[:, cols] = merged.astype(LOW)
    part_ref[...] = dot(low_ref[...], w_ref[...]).astype(LOW)


def merge(chain, rows, own, other, w):
    features = own.shape[1]
    outs = [
        shaped((rows, features)),
        shaped((features // HD, rows), WIDE),
        shaped((rows, w.shape[1])),
    ]
    args = (w, own, other)
    return chain.call(
        merge_kernel,
        (1,),
        [whole(v.shape) for v in args],
        [whole(o.shape) for o in outs],
        outs,
        us=1.0,
    )(*args)


def evicted_kernel(streams, meta_ref, memory_ref, evicted_ref):
    part = evicted_ref.shape[2]
    start = pl.multiple_of(meta_ref[META_HEAD] * part, part)
    filled = meta_ref[META_STREAMS + streams + pl.program_id(0)]
    ok = lax.broadcasted_iota(jnp.int32, (evicted_ref.shape[1], 1), 0) < filled
    rows = memory_ref[0, 0, :, pl.ds(start, part)].astype(WIDE)
    evicted_ref[0] = jnp.where(ok, rows, 0.0).astype(LOW)


def evicted_rows(chain, meta, memories):
    streams, _, slots, width = memories.shape
    out = (streams, slots, width // 2)
    return chain.call(
        functools.partial(evicted_kernel, streams),
        (streams,),
        [scalars(), per_stream(memories.shape)],
        per_stream(out),
        shaped(out),
        us=2,
    )(meta, memories)


def copied_kernel(in_ref, out_ref):
    out_ref[...] = in_ref[...]


def copied(chain, array):
    return chain.call(
        copied_kernel, (1,), [whole(array.shape)], whole(array.shape), shaped(array.shape)
    )(array)


def valid_rows(meta_ref, streams, rows):
    place = lax.broadcasted_iota(jnp.int32, (streams * rows, 1), 0)
    ok = None
    for stream in range(streams):
        inside = (
            (place >= stream * rows)
            & (place < stream * rows + meta_ref[META_STREAMS + stream] - meta_ref[META_TIER] * rows)
            & (place < (stream + 1) * rows)
        )
        ok = inside if ok is None else ok | inside
    return ok


def side_of(meta_ref, bit):
    axis, step = bit
    if axis == "tier":
        return meta_ref[META_TIER]
    return lax.rem(lax.div(meta_ref[META_DP], jnp.int32(step)), jnp.int32(2))


def pair_side(meta_ref, bits):
    first, second = (side_of(meta_ref, bit) for bit in bits)
    return jnp.where(meta_ref[META_HEAD] == 0, first, second)


def ffn_kernel(streams, bits, meta_ref, *refs):
    x_ref, a_ref, b_ref, cot_ref, gain_ref, bias_ref, wi_ref, wo_ref = refs[:8]
    act_ref, back_ref = refs[8:10]
    parts, (low_ref, turned_ref, grad_ref, back_acc) = refs[10:-4], refs[-4:]
    step = pl.program_id(0)
    units = wi_ref.shape[1]

    @pl.when(step == 0)
    def _():
        hidden = x_ref[...].astype(WIDE) + (a_ref[...].astype(WIDE) + b_ref[...].astype(WIDE))
        normed, _ = norm_stats(hidden)
        low = (normed * gain_ref[...] + bias_ref[...]).astype(LOW)
        low_ref[...] = low
        turned_ref[...] = low.T
        ok = valid_rows(meta_ref, streams, x_ref.shape[0] // streams)
        grad_ref[...] = jnp.where(ok, cot_ref[...].astype(WIDE), 0.0).astype(LOW)

    lifted = dot(low_ref[...], wi_ref[...])
    square = lifted * lifted
    bent = jnp.tanh(GELU_ROOT * lifted * (1.0 + GELU_CUBE * square))
    half = 0.5 * (1.0 + bent)
    activated = (lifted * half).astype(LOW)
    act_ref[...] = activated
    slope = half + 0.5 * lifted * (1.0 - bent * bent) * (
        GELU_ROOT * (1.0 + 3.0 * GELU_CUBE * square)
    )
    grad_out = dot(activated, grad_ref[...], TN).astype(LOW)
    grad_lifted = (slope * dot(grad_ref[...], wo_ref[...], NT)).astype(LOW)
    grad_in = dot(turned_ref[...], grad_lifted).astype(LOW)
    place = pl.multiple_of((step % 2) * units, units)
    for part in range(2):
        sent, kept = parts[2 * part : 2 * part + 2]
        side = pair_side(meta_ref, bits[part])
        for out_ref, in_ref, which in ((kept, sent, 0), (sent, kept, 1)):

            @pl.when((step // 2 == part) & (side == which))
            def _():
                out_ref[pl.ds(place, units), :] = grad_out
                in_ref[:, pl.ds(place, units)] = grad_in

    more = dot(grad_lifted, wi_ref[...], NT)

    @pl.when(step == 0)
    def _():
        back_acc[...] = more

    @pl.when(step != 0)
    def _():
        back_acc[...] += more

    @pl.when(step == pl.num_programs(0) - 1)
    def _():
        back_ref[...] = back_acc[...].astype(LOW)


def ffn(chain, streams, orders, meta, whole_args, w_in, w_out):
    rows, width = whole_args[0].shape
    units = w_in.shape[1]
    steps = 4
    block = units // steps
    outs = [shaped((rows, units)), shaped((rows, width))]
    parts = [shaped((units // 2, width))] * 4
    turned = pltpu.VMEM((width, rows), LOW)
    return chain.call(
        functools.partial(ffn_kernel, streams, tuple((p[0][0], p[1][0]) for p in orders)),
        (steps,),
        [scalars()]
        + [whole(v.shape) for v in whole_args]
        + [
            pl.BlockSpec((width, block), lambda j: (0, j)),
            pl.BlockSpec((block, width), lambda j: (j, 0)),
        ],
        [pl.BlockSpec((rows, block), lambda j: (0, j)), whole((rows, width))]
        + [whole(o.shape) for o in parts],
        outs + parts,
        scratch=[
            pltpu.VMEM((rows, width), LOW),
            turned,
            pltpu.VMEM((rows, width), LOW),
            pltpu.VMEM((rows, width), WIDE),
        ],
        vmem=32,
        us=24,
    )(meta, *whole_args, w_in, w_out)


def ffn_out_kernel(act_ref, w_ref, out_ref, acc):
    step = pl.program_id(0)
    more = dot(act_ref[...], w_ref[...])

    @pl.when(step == 0)
    def _():
        acc[...] = more

    @pl.when(step != 0)
    def _():
        acc[...] += more

    @pl.when(step == pl.num_programs(0) - 1)
    def _():
        out_ref[...] = acc[...].astype(LOW)


def ffn_out(chain, act, w):
    rows, units = act.shape
    width = w.shape[1]
    steps = 4
    block = units // steps
    return chain.call(
        ffn_out_kernel,
        (steps,),
        [pl.BlockSpec((rows, block), lambda j: (0, j)), pl.BlockSpec((block, width), lambda j: (j, 0))],
        whole((rows, width)),
        shaped((rows, width)),
        scratch=[pltpu.VMEM((rows, width), WIDE)],
        us=4,
    )(act, w)


def output_kernel(meta_ref, x_ref, a_ref, b_ref, own_ref, other_ref, out_ref):
    rows = x_ref.shape[1]
    place = meta_ref[META_TIER] * rows + lax.broadcasted_iota(jnp.int32, (rows, 1), 0)
    ok = place < meta_ref[META_STREAMS + pl.program_id(0)]
    hidden = x_ref[0].astype(WIDE) + (a_ref[0].astype(WIDE) + b_ref[0].astype(WIDE))
    result = hidden + (own_ref[0].astype(WIDE) + other_ref[0].astype(WIDE))
    out_ref[0] = jnp.where(ok, result, 0.0).astype(LOW)


def output_rows(chain, meta, *streamed):
    shape = streamed[0].shape
    return chain.call(
        output_kernel,
        (shape[0],),
        [scalars()] + [per_stream(v.shape) for v in streamed],
        per_stream(shape),
        shaped(shape),
        us=3,
    )(meta, *streamed)


def hidden_back_kernel(
    meta_ref,
    x_ref,
    a_ref,
    b_ref,
    back_ref,
    back_other_ref,
    cot_ref,
    merged_ref,
    total_ref,
    w_ref,
    gain_ref,
    grad_hidden_ref,
    grad_merged_ref,
    grad_w_ref,
    vector_ref,
    w_acc,
    stats,
):
    stream = pl.program_id(0)
    rows = x_ref.shape[1]
    hidden = x_ref[0].astype(WIDE) + (a_ref[0].astype(WIDE) + b_ref[0].astype(WIDE))
    normed, inverse = norm_stats(hidden)
    place = meta_ref[META_TIER] * rows + lax.broadcasted_iota(jnp.int32, (rows, 1), 0)
    ok = place < meta_ref[META_STREAMS + stream]
    back = back_ref[0].astype(WIDE) + back_other_ref[0].astype(WIDE)
    grad_out = jnp.where(ok, cot_ref[0].astype(WIDE), 0.0)
    grad_hidden = grad_out + norm_back(back, normed, inverse, gain_ref[...])
    grad_hidden_ref[0] = grad_hidden
    low = grad_hidden.astype(LOW)
    merged = merged_ref[0]
    grad_merged = dot(low, w_ref[...], NT).astype(LOW)
    grad_merged_ref[0, :rows, :] = grad_merged
    heads = merged.shape[1] // HD
    stats[:heads, :] = total_ref[0]
    product = grad_merged.astype(WIDE) * merged.astype(WIDE)
    for head in range(heads):
        turned = product[:, head * HD : (head + 1) * HD].T
        stats[heads + head : heads + head + 1, :] = jnp.sum(turned, axis=0, keepdims=True)
    put_packed(grad_merged_ref.at[0], rows, stats[...])
    grad_w = dot(merged, low, TN)
    gain_part = jnp.sum(back * normed, axis=0, keepdims=True)
    bias_part = jnp.sum(back, axis=0, keepdims=True)

    @pl.when(stream == 0)
    def _():
        w_acc[...] = grad_w
        vector_ref[0:1, :] = gain_part
        vector_ref[1:2, :] = bias_part

    @pl.when(stream != 0)
    def _():
        w_acc[...] += grad_w
        vector_ref[0:1, :] += gain_part
        vector_ref[1:2, :] += bias_part

    @pl.when(stream == pl.num_programs(0) - 1)
    def _():
        grad_w_ref[...] = w_acc[...].astype(LOW)


def hidden_back(chain, meta, x, a, b, back, back_other, cot, merged, total, w, gain):
    streams, rows, width = x.shape
    heads = merged.shape[2] // HD
    outs = [
        shaped(x.shape, WIDE),
        shaped((streams, rows + packed_rows(2 * heads), merged.shape[2])),
        shaped(w.shape),
        shaped((2, width), WIDE),
    ]
    streamed = (x, a, b, back, back_other, cot, merged, total)
    return chain.call(
        hidden_back_kernel,
        (streams,),
        [scalars()] + [per_stream(v.shape) for v in streamed] + [whole(w.shape), whole(gain.shape)],
        [per_stream(o.shape) for o in outs[:2]] + [whole(o.shape) for o in outs[2:]],
        outs,
        scratch=[pltpu.VMEM(w.shape, WIDE), pltpu.VMEM((2 * heads, rows), WIDE)],
        us=6.5,
        vmem=VMEM_WIDE,
    )(meta, *streamed, w, gain)


def attend_back_kernel(own, meta_ref, q_ref, gm_ref, km_ref, vm_ref, ks_ref, vs_ref, *refs):
    if own:
        gq_ref, gkm_ref, gvm_ref, gks_ref, gvs_ref = refs
        before = None
    else:
        before, (gq_ref, gkm_ref, gvm_ref, gks_ref, gvs_ref) = refs[:4], refs[4:]
    streams = pl.num_programs(0)
    stream = pl.program_id(0)
    slots, rows = km_ref.shape[1], q_ref.shape[1]
    heads = q_ref.shape[2] // HD
    stats = get_packed(gm_ref.at[0], rows, 2 * heads, rows)

    def put(ref, index, cols, value):
        if before is not None:
            value = value + before[index][0, :, cols]
        ref[0, :, cols] = value.astype(ref.dtype)

    def body(with_segment):
        memory_ok, segment_ok = slot_masks(own, meta_ref, stream, streams, slots, rows)
        for head in range(heads):
            cols = slice(head * HD, (head + 1) * HD)
            query = q_ref[0, :, cols]
            grad = gm_ref[0, :rows, cols]
            total = stats[head : head + 1, :]
            delta = stats[heads + head : heads + head + 1, :]

            def tier(key, value, ok):
                scores = jnp.where(ok, dot(key, query, NT) * (SCALE * LOG2E), NEG)
                weights = jnp.exp2(scores - total)
                grad_scores = (weights * (dot(value, grad, NT) - delta)).astype(LOW)
                return (
                    dot(key, grad_scores, TN),
                    dot(grad_scores, query) * SCALE,
                    dot(weights.astype(LOW), grad),
                )

            turned, grad_key, grad_value = tier(km_ref[0, :, cols], vm_ref[0, :, cols], memory_ok)
            put(gkm_ref, 0, cols, grad_key)
            put(gvm_ref, 1, cols, grad_value)
            if with_segment:
                more, grad_key, grad_value = tier(
                    ks_ref[0, :, cols], vs_ref[0, :, cols], segment_ok
                )
                turned = turned + more
                put(gks_ref, 2, cols, grad_key)
                put(gvs_ref, 3, cols, grad_value)
            else:
                gks_ref[0, :, cols] = before[2][0, :, cols].astype(gks_ref.dtype)
                gvs_ref[0, :, cols] = before[3][0, :, cols].astype(gvs_ref.dtype)
            gq_ref[0, :, cols] = (turned * SCALE).T.astype(LOW)

    by_tier(own, meta_ref, body)


def attend_back(chain, own, meta, q, gm, km, vm, ks, vs, before=()):
    kind = WIDE if own else LOW
    outs = [shaped(q.shape)] + [shaped(a.shape, kind) for a in (km, vm, ks, vs)]
    return chain.call(
        functools.partial(attend_back_kernel, own),
        (q.shape[0],),
        [scalars()] + [per_stream(a.shape) for a in (q, gm, km, vm, ks, vs, *before)],
        [per_stream(o.shape) for o in outs],
        outs,
        us=10,
        vmem=VMEM_WIDE,
    )(meta, q, gm, km, vm, ks, vs, *before)


def key_value_kernel_back(
    bits, meta_ref, unit_ref, stored_ref, gks_ref, gvs_ref, gkm_ref, gvm_ref,
    wk_ref, wv_ref, gain_ref, bias_ref, column_ref, sent_ref, kept_ref, k_acc, v_acc, sums
):
    stream = pl.program_id(0)
    width, features = wk_ref.shape

    @pl.when(stream == 0)
    def _():
        k_acc[...] = jnp.zeros_like(k_acc)
        v_acc[...] = jnp.zeros_like(v_acc)
        sums[...] = jnp.zeros_like(sums)

    unit, stored = unit_ref[0].T, stored_ref[0].T
    gks, gvs, gkm, gvm = gks_ref[0], gvs_ref[0], gkm_ref[0], gvm_ref[0]
    k_acc[...] += dot(unit, gks) + dot(stored, gkm)
    v_acc[...] += dot(unit, gvs) + dot(stored, gvm)
    for place, pair in enumerate(((gks, gkm), (gvs, gvm))):
        for piece in pair:
            sums[place : place + 1, :] += jnp.sum(piece.astype(WIDE), axis=0, keepdims=True)

    @pl.when(stream == pl.num_programs(0) - 1)
    def _():
        wk, wv = wk_ref[...].astype(WIDE), wv_ref[...].astype(WIDE)
        column_ref[:, 0:1] = jnp.sum(wk * k_acc[...] + wv * v_acc[...], axis=1, keepdims=True)
        column_ref[:, 1:2] = jnp.sum(wk * sums[0:1, :] + wv * sums[1:2, :], axis=1, keepdims=True)
        half = width // 2
        side = pair_side(meta_ref, bits)
        for ref, which in ((sent_ref, 1 - side), (kept_ref, side)):
            rows = pl.ds(pl.multiple_of(which * half, half), half)
            gain, bias = gain_ref[rows, :], bias_ref[rows, :]
            ref[:, :features] = (gain * k_acc[rows, :] + bias * sums[0:1, :]).astype(LOW)
            ref[:, features:] = (gain * v_acc[rows, :] + bias * sums[1:2, :]).astype(LOW)


def key_value_grads(chain, orders, meta, streamed, fixed):
    width, features = fixed[0].shape
    outs = [shaped((width, 2), WIDE)] + [shaped((width // 2, 2 * features))] * 2
    acc = pltpu.VMEM((width, features), WIDE)
    return chain.call(
        functools.partial(key_value_kernel_back, tuple(order[0] for order in orders)),
        (streamed[0].shape[0],),
        [scalars()] + [per_stream(v.shape) for v in streamed] + [whole(v.shape) for v in fixed],
        [whole(o.shape) for o in outs],
        outs,
        scratch=[acc, acc, pltpu.VMEM((2, features), WIDE)],
        vmem=VMEM_WIDE,
        us=10,
    )(meta, *streamed, *fixed)


def query_kernel_back(
    bits, meta_ref, unit_ref, own_ref, came_ref, gks_ref, gvs_ref,
    wq_ref, wk_ref, wv_ref, gwo_ref, gain_ref, bias_ref, column_in, column_ref, normed_ref,
    sent_ref, kept_ref, q_acc, sums
):
    stream = pl.program_id(0)
    width, features = wq_ref.shape

    @pl.when(stream == 0)
    def _():
        q_acc[...] = jnp.zeros_like(q_acc)
        sums[...] = jnp.zeros_like(sums)

    grad = (own_ref[0].astype(WIDE) + came_ref[0].astype(WIDE)).astype(LOW)
    q_acc[...] += dot(unit_ref[0], grad, TN)
    sums[...] += jnp.sum(grad.astype(WIDE), axis=0, keepdims=True)
    normed_ref[0] = (
        dot(grad, wq_ref[...], NT) + dot(gks_ref[0], wk_ref[...], NT) + dot(gvs_ref[0], wv_ref[...], NT)
    ).astype(LOW)

    @pl.when(stream == pl.num_programs(0) - 1)
    def _():
        wq = wq_ref[...].astype(WIDE)
        column_ref[:, 0:1] = column_in[:, 0:1] + jnp.sum(wq * q_acc[...], axis=1, keepdims=True)
        column_ref[:, 1:2] = column_in[:, 1:2] + jnp.sum(wq * sums[...], axis=1, keepdims=True)
        query = (gain_ref[...] * q_acc[...] + bias_ref[...] * sums[...]).astype(LOW)
        half = width // 2

        def put(out_ref, query_ref):
            out_ref[...] = gwo_ref[...]
            query_ref[:, :features] = query[:half]
            query_ref[:, features:] = query[half:]

        side = pair_side(meta_ref, bits)

        @pl.when(side == 0)
        def _():
            put(kept_ref, sent_ref)

        @pl.when(side != 0)
        def _():
            put(sent_ref, kept_ref)


def query_grads(chain, orders, meta, streamed, fixed):
    width, features = fixed[0].shape
    unit = streamed[0]
    outs = [shaped((width, 2), WIDE), shaped(unit.shape)]
    outs += [shaped((width // 2, 2 * features))] * 2
    return chain.call(
        functools.partial(query_kernel_back, tuple(order[0] for order in orders)),
        (unit.shape[0],),
        [scalars()] + [per_stream(v.shape) for v in streamed] + [whole(v.shape) for v in fixed],
        [whole(outs[0].shape), per_stream(unit.shape)] + [whole(o.shape) for o in outs[2:]],
        outs,
        scratch=[pltpu.VMEM((width, features), WIDE), pltpu.VMEM((1, features), WIDE)],
        vmem=VMEM_WIDE,
        us=9,
    )(meta, *streamed, *fixed)


def input_back_kernel(x_ref, own_ref, other_ref, hidden_ref, gain_ref, out_ref):
    normed, inverse = norm_stats(x_ref[0].astype(WIDE))
    grad = own_ref[0].astype(WIDE) + other_ref[0].astype(WIDE)
    out_ref[0] = (hidden_ref[0] + norm_back(grad, normed, inverse, gain_ref[...])).astype(LOW)


def input_back(chain, x, own, other, grad_hidden, gain):
    streamed = (x, own, other, grad_hidden)
    return chain.call(
        input_back_kernel,
        (x.shape[0],),
        [per_stream(v.shape) for v in streamed] + [whole(gain.shape)],
        per_stream(x.shape),
        shaped(x.shape),
        us=4,
    )(*streamed, gain)


def compress_kernel(bits, meta_ref, memory_ref, came_ref, rest_ref, w_ref, cot_ref, out_ref, *refs):
    sent_ref, kept_ref, acc, grads = refs
    stream = pl.program_id(0)
    streams = pl.num_programs(0)
    head = meta_ref[META_HEAD]
    mine = meta_ref[META_TIER] == 0
    slots, part = came_ref.shape[1], came_ref.shape[2]
    count = out_ref.shape[1]
    place = lax.broadcasted_iota(jnp.int32, (count, slots), 0)
    slot = lax.broadcasted_iota(jnp.int32, (count, slots), 1)
    length = meta_ref[META_STREAMS + stream]
    filled = jnp.where(mine, meta_ref[META_STREAMS + streams + stream], slots)
    ok = lax.broadcasted_iota(jnp.int32, (count, 1), 0) < lax.div(length, jnp.int32(RATE))
    cot = jnp.where(ok, cot_ref[0].astype(WIDE), 0.0).astype(LOW)

    @pl.when(stream == 0)
    def _():
        acc[...] = jnp.zeros_like(acc)

    picks = []
    for shift in range(RATE):
        chosen = (slot == place * RATE + shift) & (slot < filled)
        picks.append(jnp.where(chosen, 1.0, 0.0).astype(LOW))
    result = jnp.zeros(out_ref.shape[1:], WIDE)
    for ref, side in ((came_ref, head), (rest_ref, 1 - head)):
        start = pl.multiple_of(side * part, part)
        stored = jnp.where(mine, memory_ref[0, 0, :, pl.ds(start, part)].astype(WIDE), ref[0].astype(WIDE))
        stored = stored.astype(LOW)
        for shift in range(RATE):
            rows = dot(picks[shift], stored).astype(LOW)
            result = result + dot(rows, w_ref[shift, pl.ds(start, part), :])
            acc[shift, pl.ds(start, part), :] += dot(rows, cot, TN)
    out_ref[0] = jnp.where(ok, result, 0.0).astype(LOW)

    @pl.when(stream == streams - 1)
    def _():
        width = w_ref.shape[1]
        for shift in range(RATE):
            grads[shift * width : (shift + 1) * width, :] = acc[shift].astype(LOW)
        half = sent_ref.shape[0]
        side = pair_side(meta_ref, bits)
        for ref, which in ((sent_ref, 1 - side), (kept_ref, side)):
            ref[...] = grads[pl.ds(pl.multiple_of(which * half, half), half), :]


def compress(chain, orders, meta, memories, came, rest, w, cot):
    flat = (w.shape[0] * w.shape[1], w.shape[2])
    outs = [shaped(cot.shape)] + [shaped((flat[0] // 2, flat[1]))] * 2
    bits = tuple(order[0] for order in orders)
    return chain.call(
        functools.partial(compress_kernel, bits),
        (cot.shape[0],),
        [scalars()]
        + [per_stream(v.shape) for v in (memories, came, rest)]
        + [whole(w.shape), per_stream(cot.shape)],
        [per_stream(cot.shape)] + [whole(o.shape) for o in outs[1:]],
        outs,
        scratch=[pltpu.VMEM(w.shape, WIDE), pltpu.VMEM(flat, LOW)],
        us=5,
    )(meta, memories, came, rest, w, cot)


def bits_of():
    size = lax.axis_size("dp")
    bits = [("tier", 1)]
    step = 1
    while step < size:
        bits.append(("dp", step))
        step *= 2
    return bits


def swap(value, bit):
    axis, step = bit
    return lax.ppermute(value, axis, [(i, i ^ step) for i in range(lax.axis_size(axis))])


def swap_head(value):
    return swap(value, ("head", 1))


def swap_tier(value):
    return swap(value, ("tier", 1))


def swap_pair(value, bits):
    axes = ("dp", "tier", "head")
    sizes = [lax.axis_size(axis) for axis in axes]
    pairs = []
    for dp in range(sizes[0]):
        for tier in range(sizes[1]):
            for head in range(sizes[2]):
                axis, step = bits[head]
                to_dp = dp ^ step if axis == "dp" else dp
                to_tier = tier ^ step if axis == "tier" else tier
                pairs.append(
                    (
                        (dp * sizes[1] + tier) * sizes[2] + head,
                        (to_dp * sizes[1] + to_tier) * sizes[2] + head,
                    )
                )
    return lax.ppermute(value, axes, pairs)


def total_of(first, second):
    return (first.astype(WIDE) + second.astype(WIDE)).astype(LOW)


def scatter_kernel(bits, extra, meta_ref, kept, came, *refs):
    if extra:
        own, other, *refs = refs
        refs[-1][...] = own[...] + other[...]
    half = kept.shape[0] // 2
    side = pair_side(meta_ref, bits)
    for ref, which in zip(refs, (1 - side, side)):
        rows = pl.ds(pl.multiple_of(which * half, half), half)
        ref[...] = total_of(kept[rows, :], came[rows, :])


def add_kernel(bits, extra, meta_ref, kept, came, *refs):
    if extra:
        own, other, *refs = refs
        refs[-1][...] = own[...] + other[...]
    refs[0][...] = total_of(kept[...], came[...])


def gather_kernel(bits, extra, meta_ref, held, came, *refs):
    if extra:
        own, other, *refs = refs
        refs[-1][...] = own[...] + other[...]
    half = held.shape[0]
    side = pair_side(meta_ref, bits)
    refs[0][pl.ds(pl.multiple_of(side * half, half), half), :] = held[...]
    refs[0][pl.ds(pl.multiple_of((1 - side) * half, half), half), :] = came[...]


class Reduce:
    def __init__(self, chain, meta, orders, sent, kept, vector=None):
        self.chain, self.meta, self.orders = chain, meta, orders
        self.stages = len(orders[0])
        self.depth = min(3, self.stages - 1)
        self.kept = kept
        self.stage = 0
        self.vector = vector
        self.vector_bits = [("head", 1)] + bits_of()
        self.send(sent, 0)

    def bits(self, level):
        return tuple(order[level] for order in self.orders)

    def send(self, array, level):
        self.came = swap_pair(array, self.bits(level))
        self.vector_came = None
        if self.vector is not None and self.vector_bits:
            self.vector_came = swap(self.vector, self.vector_bits.pop(0))

    def run(self, kernel, level, outs):
        args = [self.meta, self.kept, self.came]
        extra = self.vector_came is not None
        if extra:
            args += [self.vector, self.vector_came]
            outs = outs + [shaped(self.vector.shape, WIDE)]
        result = self.chain.call(
            functools.partial(kernel, self.bits(level), extra),
            (1,),
            [scalars()] + [whole(v.shape) for v in args[1:]],
            [whole(o.shape) for o in outs],
            outs,
            vmem=8,
        )(*args)
        if extra:
            *result, self.vector = result
        return result

    def ready(self):
        return self.stage >= self.stages + self.depth - 1

    def step(self):
        depth, stage, stages = self.depth, self.stage, self.stages
        self.stage += 1
        rows, width = self.kept.shape
        if stage < depth - 1:
            sent, self.kept = self.run(
                scatter_kernel, stage + 1, [shaped((rows // 2, width))] * 2
            )
            self.send(sent, stage + 1)
        elif stage < stages:
            (self.kept,) = self.run(add_kernel, stage, [shaped((rows, width))])
            self.send(self.kept, stage + 1 if stage + 1 < stages else depth - 1)
        else:
            level = depth - 1 - (stage - stages)
            (self.kept,) = self.run(gather_kernel, level, [shaped((2 * rows, width))])
            self.send(self.kept, level - 1)


def finish_kernel(bits, write, carried, meta_ref, held, came, *refs):
    write(pair_side(meta_ref, bits), held, came, refs[carried:])


def finish(group, write, out_shapes, out_specs, carried=()):
    args = [group.meta, group.kept, group.came, *carried]
    count = len(carried)
    return group.chain.call(
        functools.partial(finish_kernel, group.bits(0), write, count),
        (1,),
        [scalars(), whole(group.kept.shape), whole(group.came.shape)] + [any_spec()] * count,
        out_specs,
        out_shapes,
        vmem=24,
        alias={3 + i: i for i in range(count)},
        us=3,
    )(*args)


def write_rows(side, held, came, outs):
    half = held.shape[0]
    for ref, which in ((held, side), (came, 1 - side)):
        outs[0][pl.ds(pl.multiple_of(which * half, half), half), :] = ref[...].astype(WIDE)


def finish_ffn(group, part, out_shape, in_shape, carried=()):
    specs = [
        pl.BlockSpec((out_shape[0] // 2, out_shape[1]), lambda i: (part, 0)),
        pl.BlockSpec((in_shape[0], in_shape[1] // 2), lambda i: (0, part)),
    ]

    def write(side, held, came, outs):
        for out_ref, in_ref, which in ((held, came, 0), (came, held, 1)):

            @pl.when(side == which)
            def _():
                outs[0][...] = out_ref[...].astype(WIDE)
                outs[1][...] = in_ref[...].astype(WIDE)

    return finish(group, write, [shaped(out_shape, WIDE), shaped(in_shape, WIDE)], specs, carried)


def finish_key_value(group, width, features):
    shapes = [shaped((width, features), WIDE)] * 2

    def write(side, held, came, outs):
        half = held.shape[0]
        for ref, which in ((held, side), (came, 1 - side)):
            rows = pl.ds(pl.multiple_of(which * half, half), half)
            outs[0][rows, :] = ref[:, :features].astype(WIDE)
            outs[1][rows, :] = ref[:, features:].astype(WIDE)

    return finish(group, write, shapes, [whole_block(v.shape) for v in shapes])


def finish_out_query(group, width, features):
    shapes = [shaped((features, width), WIDE), shaped((width, features), WIDE)]

    def write(side, held, came, outs):
        def put(out_ref, query_ref):
            half = out_ref.shape[0]
            outs[0][...] = out_ref[...].astype(WIDE)
            outs[1][:half, :] = query_ref[:, :features].astype(WIDE)
            outs[1][half:, :] = query_ref[:, features:].astype(WIDE)

        @pl.when(side == 0)
        def _():
            put(held, came)

        @pl.when(side != 0)
        def _():
            put(came, held)

    return finish(group, write, shapes, [whole_block(v.shape) for v in shapes])


def finish_compress(group, shape):
    flat = (shape[0] * shape[1], shape[2])
    return finish(group, write_rows, [shaped(flat, WIDE)], [whole_block(flat)])[0].reshape(shape)


def on_device(
    inputs,
    memories,
    seg_len,
    mem_count,
    w_query,
    w_key,
    w_value,
    w_attn_out,
    w_ffn_in,
    w_ffn_out,
    w_compress,
    gain_attn,
    bias_attn,
    gain_ffn,
    bias_ffn,
    cotan_output,
    cotan_compressed,
):
    tier_index = lax.axis_index("tier")
    streams, rows, width = inputs.shape
    features = w_query.shape[1]
    hidden_units = w_ffn_in.shape[1]
    counts = mem_count[:, 0]
    place = jnp.stack([tier_index, lax.axis_index("head"), lax.axis_index("dp")])
    meta = jnp.concatenate([place, seg_len, counts], 0).astype(jnp.int32)
    gain_row, bias_row = gain_attn[None], bias_attn[None]
    gain_second, bias_second = gain_ffn[None], bias_ffn[None]
    chain = Chain()

    unit, low, queries = query_rows(chain, meta, inputs, gain_row, bias_row, w_query)
    queries_other = [swap_tier(q) for q in queries]
    keys, values = key_values(chain, low, w_key, w_value)
    stored, memory_keys, memory_values = stored_rows(
        chain, memories, gain_row, bias_row, w_key, w_value
    )
    tiers = (memory_keys, memory_values, keys, values)
    own, came = [], []
    for stream in range(streams):
        came.append(swap_tier(attend(chain, False, stream, meta, queries_other[stream], *tiers)))
        own.append(attend(chain, True, stream, meta, queries[stream], *tiers))
    merged, totals, attended = zip(
        *[merge(chain, rows, mine, other, w_attn_out) for mine, other in zip(own, came)]
    )
    merged, totals, attended = jnp.stack(merged), jnp.stack(totals), jnp.stack(attended)
    attended_other = swap_head(attended)

    tier, low_bit, *more = bits_of()
    high_bit, more = more[0], more[1:]
    axes = {"x": tier, "y": low_bit, "z": high_bit}
    orders = {
        name: tuple(tuple(axes[axis] for axis in path) + tuple(more) for path in paths.split("/"))
        for name, paths in PATHS.items()
    }
    flat = (streams * rows, width)
    hidden_args = (
        inputs.reshape(flat),
        attended.reshape(flat),
        attended_other.reshape(flat),
        cotan_output.reshape(flat),
        gain_second,
        bias_second,
    )
    groups, got = {}, {}

    def begin(name, sent, kept, vector=None):
        groups[name] = Reduce(chain, meta, orders[name], sent, kept, vector)

    def run_ffn():
        names = ("f1", "f2")
        got["act"], back, *parts = ffn(
            chain, streams, [orders[name] for name in names], meta, hidden_args, w_ffn_in, w_ffn_out
        )
        got["back"] = back.reshape(inputs.shape)
        got["back_other"] = swap_head(got["back"])
        for place, name in enumerate(names):
            begin(name, *parts[2 * place : 2 * place + 2])

    def run_ffn3():
        got["ffn"] = ffn_out(chain, got["act"], w_ffn_out).reshape(inputs.shape)
        got["ffn_other"] = swap_head(got["ffn"])

    def run_hidden():
        got["hidden"], got["gm"], got["gwo"], vectors_ffn = hidden_back(
            chain, meta, inputs, attended, attended_other, got["back"], got["back_other"],
            cotan_output, merged, totals, w_attn_out, gain_second,
        )
        got["gm_other"] = swap_tier(got["gm"])
        got["vectors"] = 0.5 * vectors_ffn

    def run_own():
        got["queries"] = jnp.stack(queries)
        got["own"], *got["sums"] = attend_back(chain, True, meta, got["queries"], got["gm"], *tiers)

    def run_other():
        got["other"], *got["grads"] = attend_back(
            chain, False, meta, jnp.stack(queries_other), got["gm_other"], *tiers,
            before=tuple(got["sums"]),
        )
        got["came"] = swap_tier(got["other"])

    def run_output():
        got["output"] = output_rows(
            chain, meta, inputs, attended, attended_other, got["ffn"], got["ffn_other"]
        )

    def run_grads():
        grad_km, grad_vm, grad_ks, grad_vs = got["grads"]
        got["column"], *parts = key_value_grads(
            chain, orders["kv"], meta, (unit, stored, grad_ks, grad_vs, grad_km, grad_vm),
            (w_key, w_value, gain_attn[:, None], bias_attn[:, None]),
        )
        begin("kv", *parts)

    def run_query():
        _, _, grad_ks, grad_vs = got["grads"]
        column, got["normed"], *parts = query_grads(
            chain, orders["oq"], meta, (unit, got["own"], got["came"], grad_ks, grad_vs),
            (
                w_query, w_key, w_value, got["gwo"], gain_attn[:, None], bias_attn[:, None],
                got["column"],
            ),
        )
        got["normed_other"] = swap_head(got["normed"])
        begin("oq", *parts, jnp.concatenate([column.T, got["vectors"]], axis=0))

    def run_evict():
        got["evicted"] = lax.ppermute(evicted_rows(chain, meta, memories), "tier", [(0, 1)])

    def run_evict2():
        got["evicted"] = copied(chain, got["evicted"])
        got["evicted_other"] = swap_head(got["evicted"])

    def run_input():
        got["grad_inputs"] = input_back(
            chain, inputs, got["normed"], got["normed_other"], got["hidden"], gain_row
        )

    def run_compress():
        got["compressed"], *parts = compress(
            chain, orders["compress"], meta, memories, got["evicted"], got["evicted_other"],
            w_compress, cotan_compressed,
        )
        begin("compress", *parts)

    def end(name):
        group = groups.pop(name)
        out_shape, in_shape = w_ffn_out.shape, w_ffn_in.shape
        if name == "f1":
            got["ffn_grads"] = finish_ffn(group, 0, out_shape, in_shape)
        elif name == "f2":
            got["ffn_grads"] = finish_ffn(group, 1, out_shape, in_shape, got["ffn_grads"])
        elif name == "kv":
            got["kv"] = finish_key_value(group, width, features)
        elif name == "oq":
            got["oq"] = finish_out_query(group, width, features)
            got["vector"] = group.vector
        else:
            got["compress"] = finish_compress(group, w_compress.shape)

    runs = {
        "ffn": run_ffn, "ffn3": run_ffn3, "hidden": run_hidden, "own": run_own,
        "other": run_other, "output": run_output, "grads": run_grads, "query": run_query,
        "evict": run_evict, "evict2": run_evict2, "input": run_input, "compr": run_compress,
    }
    for name in ORDER:
        if name in runs:
            runs[name]()
        elif name in groups and groups[name].ready():
            end(name)
        elif name in groups:
            groups[name].step()
    while groups:
        for name in list(groups):
            if groups[name].ready():
                end(name)
            else:
                groups[name].step()
    vectors = got["vector"]
    return (
        got["output"],
        got["compressed"],
        got["grad_inputs"],
        got["oq"][1],
        *got["kv"],
        got["oq"][0],
        got["ffn_grads"][1],
        got["ffn_grads"][0],
        got["compress"],
        vectors[0],
        vectors[1],
        vectors[2],
        vectors[3],
    )


def solution(mesh):
    return jax.shard_map(
        on_device,
        mesh=mesh,
        in_specs=(
            P("dp", "tier", None),
            P("dp", "tier", None, None),
            P("dp"),
            P("dp", "tier"),
            P(None, "head"),
            P(None, "head"),
            P(None, "head"),
            P("head", None),
            P(None, "head"),
            P("head", None),
            P(None, None, ("tier", "head")),
            P(),
            P(),
            P(),
            P(),
            P("dp", "tier", None),
            P("dp", None, ("tier", "head")),
        ),
        out_specs=(
            P("dp", "tier", None),
            P("dp", None, ("tier", "head")),
            P("dp", "tier", None),
            P(None, "head"),
            P(None, "head"),
            P(None, "head"),
            P("head", None),
            P(None, "head"),
            P("head", None),
            P(None, None, ("tier", "head")),
            P(),
            P(),
            P(),
            P(),
        ),
        check_vma=False,
    )
```

time: 670 us -> 466 us (0.70)
  the two profiles are of different devices: /device:TPU:0 before, /device:TPU:15 now
where the time goes in v3:
time: 466 us; the launch traced here: 456 us
  waiting for transfers between devices  199 us (43%)
  Pallas kernels  166 us (36%)
  starting transfers between devices  51.4 us (11%)
  local copies, waits for them, and re-layouts  37.7 us (8%)
    pallas_call x57, Pallas kernels, run(): pl.pallas_call(body, grid=grid, in_specs=specs, out_specs=out_specs, out_...  166 us
    ppermute x33, waiting for transfers between devices, swap_pair(): return lax.ppermute(value, axes, pairs)  135 us
    ppermute x18, waiting for transfers between devices, swap(): lax.ppermute(value, axis, [(i, i ^ step) for i in range(lax.axis_size(axi...  64.3 us
    unnamed x166, local copies, waits for them, and re-layouts  34.8 us
    ppermute x33, starting transfers between devices, swap_pair(): return lax.ppermute(value, axes, pairs)  33.7 us
    ppermute x18, starting transfers between devices, swap(): lax.ppermute(value, axis, [(i, i ^ step) for i in range(lax.axis_size(axi...  16.4 us
  transfers between devices with their start and end apart: 52, of which 22 were waited for; matrix products, arithmetic and copies ran while one was open for 1% of the time, Pallas kernels for 27%

profile of v3, /device:TPU:15, one launch (start us, length us, event | category | flops | bytes accessed | tf_op | source)
XLA Modules:
  0.0 456.5 jit_solution(15822028407941304154)
XLA Ops:
  5.4 2.2 shard_map.272
  9.5 2.2 shard_map.273
  11.6 5.3 %shard_map.274 = (bf16[3,512,1024]{2,1,0:T(8,128)(2,1)S(1)}, bf16[3,512,512]{2,1,0:T(8,128)(2,1)S(1)}, bf16[3,512,512]{2,1,0:T(8,128)(2,1)S(1)}) custom-call(bf16[3,1,512,1024]{3,2,1,0:T(8,128)(2,1)S(1)} %copy-done.3, f32[1,1024]{1,0:T(1,128)S(1)} %bitcast.59, f32[1,1024]{1,0:T(1,128)S(1)} %bitcast.63, bf16[1024,512]{1,0:T(8,128)(2,1)S(1)} %copy-done.8, ...), custom_call_target="tpu_custom_call" | custom-call | flops 600000000 | tf_op jit(solution)/shard_map/pallas_call | solution.py:105
  17.0 2.4 shard_map.275.refs_6_
  19.4 1.5 collective-permute-start.1
  20.9 2.6 shard_map.276.refs_6_.refs_1_
  23.6 2.6 shard_map.277.refs_6_
  26.6 2.6 shard_map.278.refs_6_.refs_1_
  29.2 2.4 shard_map.279.refs_6_
  33.2 2.6 shard_map.280.refs_3_.refs_1_
  36.5 1.5 collective-permute-done.4.refs_2_
  38.8 5.2 %collective-permute-done.5.refs_2_ = bf16[272,512]{1,0:T(8,128)(2,1)S(1)} collective-permute-done((bf16[272,512]{1,0:T(8,128)(2,1)S(1)}, bf16[272,512]{1,0:T(8,128)(2,1)S(1)}, u32[]{:S(2)}, u32[]{:S(2)}) %collective-permute-start.5) | collective-permute-done | bytes 278560 | tf_op jit(solution)/shard_map/ppermute | solution.py:882
  45.0 1.6 collective-permute-start.6
  46.6 3.0 collective-permute-done.6.refs_3_
  49.7 28.5 %shard_map.284 = (bf16[768,2048]{1,0:T(8,128)(2,1)S(1)}, bf16[768,1024]{1,0:T(8,128)(2,1)S(1)}, bf16[1024,1024]{1,0:T(8,128)(2,1)S(1)}, bf16[1024,1024]{1,0:T(8,...) custom-call(s32[9]{0:T(128)S(1)} %concatenate.6.meta_ref.refs_0_, ...), custom_call_target="tpu_custom_call" | custom-call | flops 2400000000 | tf_op jit(solution)/shard_map/pallas_call | solution.py:105
  87.2 7.3 %shard_map.285 = (f32[3,256,1024]{2,1,0:T(8,128)}, bf16[3,288,512]{2,1,0:T(8,128)(2,1)S(1)}, bf16[512,1024]{1,0:T(8,128)(2,1)S(1)}, f32[2,1024]{1,0:T(2,128)S(1)}) custom-call(s32[9]{0:T(128)S(1)} %concatenate.6.meta_ref.refs_0_, bf16[3,256,1024]{2,1,0:T(8,128)(2,1)S(1)} %copy-done.1, bf16[3,256,1024]{2,1,0:T(8,128)(2,1)S(1)} %pad_maximum_fusion.refs_2_, ...), custom_call_target="tpu_custom_call" | custom-call | flops 650000000 | tf_op jit(solution)/shard_map/pallas_call | solution.py:105
  95.5 10.3 %shard_map.286 = (bf16[3,256,512]{2,1,0:T(8,128)(2,1)S(1)}, f32[3,512,512]{2,1,0:T(8,128)S(1)}, f32[3,512,512]{2,1,0:T(8,128)}, f32[3,256,512]{2,1,0:T(8,128)S(1)}, f32[3,256,512]{2,1,0:T(8,128)S(1)}) custom-call(s32[9]{0:T(128)S(1)} %concatenate.6.meta_ref.refs_0_, bf16[3,256,512]{2,1,0:T(8,128)(2,1)S(1)} %pad_maximum_fusion.1.refs_1_, ...), custom_call_target="tpu_custom_call" | custom-call | flops 1000000000 | tf_op jit(solution)/shard_map/pallas_call | solution.py:105
  105.9 4.2 copy-done.17
  110.1 5.4 %shard_map.287.refs_6_ = bf16[768,1024]{1,0:T(8,128)(2,1)S(1)} custom-call(bf16[768,2048]{1,0:T(8,128)(2,1)S(1)} %copy-done.17, bf16[2048,1024]{1,0:T(8,128)(2,1)S(1)} %copy-done.7, bf16[3,256,512]{2,1,0:T(8,128)(2,1)S(1)} %get-tuple-element.120.refs_2_), custom_call_target="tpu_custom_call" | custom-call | flops 400000000 | tf_op jit(solution)/shard_map/pallas_call | solution.py:105
  116.3 2.7 collective-permute-done.8.refs_5_
  119.0 2.9 shard_map.288.refs_11_
  122.0 14.7 %collective-permute-done.9.refs_2_ = bf16[3,288,512]{2,1,0:T(8,128)(2,1)S(1)} collective-permute-done((bf16[3,288,512]{2,1,0:T(8,128)(2,1)S(1)}, bf16[3,288,512]{2,1,0:T(8,128)(2,1)S(1)}, u32[]{:S(2)}, u32[]{:S(2)}) %collective-permute-start.9) | collective-permute-done | bytes 884768 | tf_op jit(solution)/shard_map/ppermute | solution.py:882
  136.7 8.7 %shard_map.289 = (bf16[3,256,512]{2,1,0:T(8,128)(2,1)}, bf16[3,512,512]{2,1,0:T(8,128)(2,1)S(1)}, bf16[3,512,512]{2,1,0:T(8,128)(2,1)S(1)}, bf16[3,256,512]{2,1,0:T(8,128)(2,1)S(1)}, bf16[3,256,512]{2,1,0:T(8,128)(2,1)S(1)}) custom-call(s32[9]{0:T(128)S(1)} %concatenate.6.meta_ref.refs_0_, bf16[3,256,512]{2,1,0:T(8,128)(2,1)S(1)} %pad_maximum_fusion.3.refs_1_, ...), custom_call_target="tpu_custom_call" | custom-call | flops 1000000000 | tf_op jit(solution)/shard_map/pallas_call | solution.py:105
  145.4 4.6 %shard_map.290 = (bf16[512,1024]{1,0:T(8,128)(2,1)}, bf16[512,1024]{1,0:T(8,128)(2,1)S(1)}) custom-call(s32[9]{0:T(128)S(1)} %concatenate.6.meta_ref.refs_0_, bf16[1024,1024]{1,0:T(8,128)(2,1)S(1)} %copy-done.37, bf16[1024,1024]{1,0:T(8,128)(2,1)} %collective-permute-done.11.refs_2_, bf16[3,256,512]{2,1,0:T(8,128)(2,1)} %get-tuple-element.133.refs_3_), custom_call_target="tpu_custom_call" | custom-call | flops 100000000 | tf_op jit(solution)/shard_map/pallas_call | solution.py:105
  151.1 2.8 collective-permute-start.13
  155.2 1.6 copy-done.35
  156.8 2.2 shard_map.291
  162.5 9.0 %shard_map.292 = (f32[1024,2]{1,0:T(8,128)S(1)}, bf16[512,1024]{1,0:T(8,128)(2,1)S(1)}, bf16[512,1024]{1,0:T(8,128)(2,1)S(1)}) custom-call(s32[9]{0:T(128)S(1)} %concatenate.6.meta_ref.refs_0_, bf16[3,256,1024]{2,1,0:T(8,128)(2,1)S(1)} %copy-done.15, bf16[3,512,1024]{2,1,0:T(8,128)(2,1)} %copy-done.18, bf16[3,256,512]{2,1,0:T(8,128)(2,1)S(1)} %copy-done.31, ...), custom_call_target="tpu_custom_call" | custom-call | flops 1000000000 | tf_op jit(solution)/shard_map/pallas_call | solution.py:105
  171.7 2.4 shard_map.293.refs_3_
  174.1 1.6 shard_map.294
  176.3 7.7 %shard_map.295 = (f32[1024,2]{1,0:T(8,128)S(1)}, bf16[3,256,1024]{2,1,0:T(8,128)(2,1)S(1)}, bf16[512,1024]{1,0:T(8,128)(2,1)}, bf16[512,1024]{1,0:T(8,128)(2,1)S(1)}) custom-call(s32[9]{0:T(128)S(1)} %concatenate.6.meta_ref.refs_0_, bf16[3,256,1024]{2,1,0:T(8,128)(2,1)} %copy-done.14, bf16[3,256,512]{2,1,0:T(8,128)(2,1)S(1)} %copy-done.29, ...), custom_call_target="tpu_custom_call" | custom-call | flops 900000000 | tf_op jit(solution)/shard_map/pallas_call | solution.py:105
  184.0 2.7 collective-permute-start.21
  188.6 2.2 collective-permute-start.20
  190.9 15.4 %collective-permute-done.18.refs_2_ = bf16[512,1024]{1,0:T(8,128)(2,1)S(1)} collective-permute-done((bf16[512,1024]{1,0:T(8,128)(2,1)S(1)}, bf16[512,1024]{1,0:T(8,128)(2,1)S(1)}, u32[]{:S(2)}, u32[]{:S(2)}) %collective-permute-start.18) | collective-permute-done | bytes 1048608 | tf_op jit(solution)/shard_map/ppermute | solution.py:909
  208.6 3.5 shard_map.297.refs_3_
  212.1 45.3 %collective-permute-done.20.refs_2_ = bf16[256,1024]{1,0:T(8,128)(2,1)S(1)} collective-permute-done((bf16[256,1024]{1,0:T(8,128)(2,1)S(1)}, bf16[256,1024]{1,0:T(8,128)(2,1)S(1)}, u32[]{:S(2)}, u32[]{:S(2)}) %collective-permute-start.20) | collective-permute-done | bytes 524320 | tf_op jit(solution)/shard_map/ppermute | solution.py:909
  259.5 2.2 collective-permute-start.23
  267.2 4.3 collective-permute-done.24.refs_2_
  274.7 2.7 collective-permute-done.22.refs_2_
  280.3 4.5 collective-permute-start.26
  285.0 16.2 %collective-permute-done.26.refs_2_ = bf16[128,1024]{1,0:T(8,128)(2,1)S(1)} collective-permute-done((bf16[128,1024]{1,0:T(8,128)(2,1)S(1)}, bf16[128,1024]{1,0:T(8,128)(2,1)S(1)}, u32[]{:S(2)}, u32[]{:S(2)}) %collective-permute-start.26) | collective-permute-done | bytes 262176 | tf_op jit(solution)/shard_map/ppermute | solution.py:909
  302.0 8.7 %shard_map.307 = (bf16[3,170,256]{2,1,0:T(8,128)(2,1)}, bf16[1536,256]{1,0:T(8,128)(2,1)S(1)}, bf16[1536,256]{1,0:T(8,128)(2,1)S(1)}) custom-call(s32[9]{0:T(128)S(1)} %concatenate.6.meta_ref.refs_0_, bf16[3,1,512,1024]{3,2,1,0:T(8,128)(2,1)S(1)} %copy-done.5, bf16[3,512,512]{2,1,0:T(8,128)(2,1)S(1)} %shard_map.305.refs_3_.refs_2_, ...), custom_call_target="tpu_custom_call" | custom-call | flops 500000000 | tf_op jit(solution)/shard_map/pallas_call | solution.py:105
  310.7 2.4 collective-permute-start.38
  315.3 1.5 collective-permute-start.37
  321.4 2.0 collective-permute-done.32.refs_4_
  324.5 15.4 %collective-permute-done.31.refs_2_ = bf16[128,1024]{1,0:T(8,128)(2,1)S(1)} collective-permute-done((bf16[128,1024]{1,0:T(8,128)(2,1)S(1)}, bf16[128,1024]{1,0:T(8,128)(2,1)S(1)}, u32[]{:S(2)}, u32[]{:S(2)}) %collective-permute-start.31) | collective-permute-done | bytes 262176 | tf_op jit(solution)/shard_map/ppermute | solution.py:909
  342.6 8.3 %collective-permute-start.34 = (bf16[128,1024]{1,0:T(8,128)(2,1)S(1)}, bf16[128,1024]{1,0:T(8,128)(2,1)S(1)}, u32[]{:S(2)}, u32[]{:S(2)}) collective-permute-start(bf16[128,1024]{1,0:T(8,128)(2,1)S(1)} %get-tuple-element.162.refs_3_.refs_1_), channel_id=1, source_target_pairs={{0,16},{1,17},{2,18},{3,19},{4,20},{5,21},{6,22},{7,23},{8,24},{9,... | collective-permute-start | bytes 786440 | tf_op jit(solution)/shard_map/ppermute | solution.py:909
  351.2 10.1 %collective-permute-done.35.refs_4_ = f32[4,1024]{1,0:T(4,128)S(1)} collective-permute-done((f32[4,1024]{1,0:T(4,128)S(1)}, f32[4,1024]{1,0:T(4,128)S(1)}, u32[]{:S(2)}, u32[]{:S(2)}) %collective-permute-start.35) | collective-permute-done | bytes 16416 | tf_op jit(solution)/shard_map/ppermute | solution.py:882
  361.9 2.3 collective-permute-start.39
  366.2 2.2 collective-permute-start.40
  369.1 23.8 %collective-permute-done.40.refs_4_ = f32[4,1024]{1,0:T(4,128)S(1)} collective-permute-done((f32[4,1024]{1,0:T(4,128)S(1)}, f32[4,1024]{1,0:T(4,128)S(1)}, u32[]{:S(2)}, u32[]{:S(2)}) %collective-permute-start.40) | collective-permute-done | bytes 16416 | tf_op jit(solution)/shard_map/ppermute | solution.py:882
  395.8 2.8 shard_map.321
  398.5 9.0 %collective-permute-done.44.refs_2_ = bf16[768,256]{1,0:T(8,128)(2,1)S(1)} collective-permute-done((bf16[768,256]{1,0:T(8,128)(2,1)S(1)}, bf16[768,256]{1,0:T(8,128)(2,1)S(1)}, u32[]{:S(2)}, u32[]{:S(2)}) %collective-permute-start.44) | collective-permute-done | bytes 393248 | tf_op jit(solution)/shard_map/ppermute | solution.py:909
  407.6 1.6 copy-done.38
  409.9 15.2 %collective-permute-done.43.refs_2_ = bf16[256,1024]{1,0:T(8,128)(2,1)S(1)} collective-permute-done((bf16[256,1024]{1,0:T(8,128)(2,1)S(1)}, bf16[256,1024]{1,0:T(8,128)(2,1)S(1)}, u32[]{:S(2)}, u32[]{:S(2)}) %collective-permute-start.43) | collective-permute-done | bytes 524320 | tf_op jit(solution)/shard_map/ppermute | solution.py:909
  425.8 5.9 %collective-permute-done.49.refs_2_ = bf16[768,256]{1,0:T(8,128)(2,1)S(1)} collective-permute-done((bf16[768,256]{1,0:T(8,128)(2,1)S(1)}, bf16[768,256]{1,0:T(8,128)(2,1)S(1)}, u32[]{:S(2)}, u32[]{:S(2)}) %collective-permute-start.49) | collective-permute-done | bytes 393248 | tf_op jit(solution)/shard_map/ppermute | solution.py:909
  433.0 4.5 shard_map.325
  437.5 1.9 collective-permute-done.47.refs_2_
  439.4 3.4 copy-done.2
  442.8 2.8 shard_map.326
  445.7 1.6 copy-done.39
  447.2 2.4 shard_map.327.refs_5_
  449.7 1.9 copy-done.20
  451.6 4.5 shard_map.328
  (275 shorter events, 66.3 us)
Async XLA Ops:
  7.7 9.3 %collective-permute-start = (bf16[256,512]{1,0:T(8,128)(2,1)S(1)}, bf16[256,512]{1,0:T(8,128)(2,1)S(1)}, u32[]{:S(2)}, u32[]{:S(2)}) collective-permute-start(bf16[256,512]{1,0:T(8,128)(2,1)S(1)} %get-tuple-element.97.refs_1_), channel_id=1, source_target_pairs={{0,2},{2,0},{1,3},{3,1},{4,6},{6,4},{5,7},{7,5},{8,10},{10,8},{9,1... | collective-permute-start | bytes 786440 | tf_op jit(solution)/shard_map/ppermute | solution.py:882
  8.0 15.6 %collective-permute-start.3 = (bf16[256,512]{1,0:T(8,128)(2,1)S(1)}, bf16[256,512]{1,0:T(8,128)(2,1)S(1)}, u32[]{:S(2)}, u32[]{:S(2)}) collective-permute-start(bf16[256,512]{1,0:T(8,128)(2,1)S(1)} %get-tuple-element.106.refs_1_), channel_id=1, source_target_pairs={{0,2},{2,0},{1,3},{3,1},{4,6},{6,4},{5,7},{7,5},{8,10},{10,8},{9,1... | collective-permute-start | bytes 786440 | tf_op jit(solution)/shard_map/ppermute | solution.py:882
  9.2 20.0 %collective-permute-start.2 = (bf16[256,512]{1,0:T(8,128)(2,1)S(1)}, bf16[256,512]{1,0:T(8,128)(2,1)S(1)}, u32[]{:S(2)}, u32[]{:S(2)}) collective-permute-start(bf16[256,512]{1,0:T(8,128)(2,1)S(1)} %get-tuple-element.105.refs_1_), channel_id=1, source_target_pairs={{0,2},{2,0},{1,3},{3,1},{4,6},{6,4},{5,7},{7,5},{8,10},{10,8},{9,1... | collective-permute-start | bytes 786440 | tf_op jit(solution)/shard_map/ppermute | solution.py:882
  19.4 16.4 %collective-permute-start.1 = (bf16[272,512]{1,0:T(8,128)(2,1)S(1)}, bf16[272,512]{1,0:T(8,128)(2,1)S(1)}, u32[]{:S(2)}, u32[]{:S(2)}) collective-permute-start(bf16[272,512]{1,0:T(8,128)(2,1)S(1)} %shard_map.275.refs_6_), channel_id=1, source_target_pairs={{0,2},{2,0},{1,3},{3,1},{4,6},{6,4},{5,7},{7,5},{8,10},{10,8},{9,1... | collective-permute-start | bytes 835592 | tf_op jit(solution)/shard_map/ppermute | solution.py:882
  26.2 11.8 %collective-permute-start.4 = (bf16[272,512]{1,0:T(8,128)(2,1)S(1)}, bf16[272,512]{1,0:T(8,128)(2,1)S(1)}, u32[]{:S(2)}, u32[]{:S(2)}) collective-permute-start(bf16[272,512]{1,0:T(8,128)(2,1)S(1)} %shard_map.277.refs_6_), channel_id=1, source_target_pairs={{0,2},{2,0},{1,3},{3,1},{4,6},{6,4},{5,7},{7,5},{8,10},{10,8},{9,1... | collective-permute-start | bytes 835592 | tf_op jit(solution)/shard_map/ppermute | solution.py:882
  31.6 12.4 %collective-permute-start.5 = (bf16[272,512]{1,0:T(8,128)(2,1)S(1)}, bf16[272,512]{1,0:T(8,128)(2,1)S(1)}, u32[]{:S(2)}, u32[]{:S(2)}) collective-permute-start(bf16[272,512]{1,0:T(8,128)(2,1)S(1)} %shard_map.279.refs_6_), channel_id=1, source_target_pairs={{0,2},{2,0},{1,3},{3,1},{4,6},{6,4},{5,7},{7,5},{8,10},{10,8},{9,1... | collective-permute-start | bytes 835592 | tf_op jit(solution)/shard_map/ppermute | solution.py:882
  45.0 4.7 %collective-permute-start.6 = (bf16[3,256,1024]{2,1,0:T(8,128)(2,1)S(1)}, bf16[3,256,1024]{2,1,0:T(8,128)(2,1)S(1)}, u32[]{:S(2)}, u32[]{:S(2)}) collective-permute-start(bf16[3,256,1024]{2,1,0:T(8,128)(2,1)S(1)} %pad_maximum_fusion.refs_2_), channel_id=1, source_target_pairs={{0,1},{1,0},{2,3},{3,2},{4,5},{5,4},{6,7},{7,6},{8,9},{9,8},{10,11... | collective-permute-start | bytes 4718600 | tf_op jit(solution)/shard_map/ppermute | solution.py:882
  49.7 28.5 %copy-start.11 = (bf16[3,256,1024]{2,1,0:T(8,128)(2,1)}, bf16[3,256,1024]{2,1,0:T(8,128)(2,1)S(1)}, u32[]{:S(2)}) copy-start(bf16[3,256,1024]{2,1,0:T(8,128)(2,1)S(1)} %collective-permute-done.6.refs_3_) | copy-start | bytes 4718596
  82.1 3.4 collective-permute-start.7
  84.0 61.3 %collective-permute-start.11 = (bf16[1024,1024]{1,0:T(8,128)(2,1)}, bf16[1024,1024]{1,0:T(8,128)(2,1)}, u32[]{:S(2)}, u32[]{:S(2)}) collective-permute-start(bf16[1024,1024]{1,0:T(8,128)(2,1)} %copy-done.80), channel_id=1, source_target_pairs={{0,2},{1,5},{2,0},{3,7},{4,6},{5,1},{6,4},{7,3},{8,10},{9,13},{10,... | collective-permute-start | bytes 6291464 | tf_op jit(solution)/shard_map/ppermute | solution.py:909
  115.6 3.5 collective-permute-start.8
  115.8 39.4 %collective-permute-start.10 = (bf16[1024,1024]{1,0:T(8,128)(2,1)}, bf16[1024,1024]{1,0:T(8,128)(2,1)}, u32[]{:S(2)}, u32[]{:S(2)}) collective-permute-start(bf16[1024,1024]{1,0:T(8,128)(2,1)} %get-tuple-element.130), channel_id=1, source_target_pairs={{0,8},{1,5},{2,10},{3,7},{4,12},{5,1},{6,14},{7,3},{8,0},{9,13},{1... | collective-permute-start | bytes 6291464 | tf_op jit(solution)/shard_map/ppermute | solution.py:909
  116.0 20.7 %collective-permute-start.9 = (bf16[3,288,512]{2,1,0:T(8,128)(2,1)S(1)}, bf16[3,288,512]{2,1,0:T(8,128)(2,1)S(1)}, u32[]{:S(2)}, u32[]{:S(2)}) collective-permute-start(bf16[3,288,512]{2,1,0:T(8,128)(2,1)S(1)} %get-tuple-element.118.refs_2_), channel_id=1, source_target_pairs={{0,2},{2,0},{1,3},{3,1},{4,6},{6,4},{5,7},{7,5},{8,10},{10,8},{9,1... | collective-permute-start | bytes 2654216 | tf_op jit(solution)/shard_map/ppermute | solution.py:882
  116.3 20.3 %copy-start.46 = (f32[3,256,512]{2,1,0:T(8,128)S(1)}, f32[3,256,512]{2,1,0:T(8,128)}, u32[]{:S(2)}) copy-start(f32[3,256,512]{2,1,0:T(8,128)} %copy-done.45) | copy-start | bytes 4718596
  151.0 23.0 %collective-permute-start.14 = (bf16[512,1024]{1,0:T(8,128)(2,1)}, bf16[512,1024]{1,0:T(8,128)(2,1)}, u32[]{:S(2)}, u32[]{:S(2)}) collective-permute-start(bf16[512,1024]{1,0:T(8,128)(2,1)} %get-tuple-element.134.refs_3_), channel_id=1, source_target_pairs={{0,4},{1,9},{2,6},{3,11},{4,0},{5,13},{6,2},{7,15},{8,12},{9,1},{1... | collective-permute-start | bytes 3145736 | tf_op jit(solution)/shard_map/ppermute | solution.py:909
  151.1 24.7 %collective-permute-start.13 = (bf16[3,256,512]{2,1,0:T(8,128)(2,1)}, bf16[3,256,512]{2,1,0:T(8,128)(2,1)}, u32[]{:S(2)}, u32[]{:S(2)}) collective-permute-start(bf16[3,256,512]{2,1,0:T(8,128)(2,1)} %get-tuple-element.133.refs_3_), channel_id=1, source_target_pairs={{0,2},{2,0},{1,3},{3,1},{4,6},{6,4},{5,7},{7,5},{8,10},{10,8},{9,1... | collective-permute-start | bytes 2359304 | tf_op jit(solution)/shard_map/ppermute | solution.py:882
  159.0 12.6 %copy-start.54 = (bf16[512,1024]{1,0:T(8,128)(2,1)}, bf16[512,1024]{1,0:T(8,128)(2,1)S(1)}, u32[]{:S(2)}) copy-start(bf16[512,1024]{1,0:T(8,128)(2,1)S(1)} %get-tuple-element.144.refs_1_) | copy-start | bytes 3145732
  159.0 12.6 %copy-start.68 = (bf16[512,1024]{1,0:T(8,128)(2,1)}, bf16[512,1024]{1,0:T(8,128)(2,1)S(1)}, u32[]{:S(2)}) copy-start(bf16[512,1024]{1,0:T(8,128)(2,1)S(1)} %get-tuple-element.135.refs_11_) | copy-start | bytes 3145732
  176.3 11.0 %copy-start.69 = (bf16[512,1024]{1,0:T(8,128)(2,1)S(1)}, bf16[512,1024]{1,0:T(8,128)(2,1)}, u32[]{:S(2)}) copy-start(bf16[512,1024]{1,0:T(8,128)(2,1)} %copy-done.68) | copy-start | bytes 3145732
  176.3 30.0 %copy-start.59 = (bf16[512,1024]{1,0:T(8,128)(2,1)S(1)}, bf16[512,1024]{1,0:T(8,128)(2,1)}, u32[]{:S(2)}) copy-start(bf16[512,1024]{1,0:T(8,128)(2,1)} %copy-done.58) | copy-start | bytes 3145732
  176.3 32.3 %copy-start.19 = (f32[3,256,1024]{2,1,0:T(8,128)S(1)}, f32[3,256,1024]{2,1,0:T(8,128)}, u32[]{:S(2)}) copy-start(f32[3,256,1024]{2,1,0:T(8,128)} %get-tuple-element.119.refs_7_.refs_3_) | copy-start | bytes 9437188
  184.0 28.1 %copy-start.40 = (f32[1024,2]{1,0:T(8,128)}, f32[1024,2]{1,0:T(8,128)S(1)}, u32[]{:S(2)}) copy-start(f32[1024,2]{1,0:T(8,128)S(1)} %get-tuple-element.142.refs_3_) | copy-start | bytes 24580
  184.0 28.1 %copy-start.56 = (bf16[512,1024]{1,0:T(8,128)(2,1)}, bf16[512,1024]{1,0:T(8,128)(2,1)S(1)}, u32[]{:S(2)}) copy-start(bf16[512,1024]{1,0:T(8,128)(2,1)S(1)} %get-tuple-element.140.refs_1_) | copy-start | bytes 3145732
  184.0 23.2 %collective-permute-start.21 = (bf16[3,256,1024]{2,1,0:T(8,128)(2,1)S(1)}, bf16[3,256,1024]{2,1,0:T(8,128)(2,1)S(1)}, u32[]{:S(2)}, u32[]{:S(2)}) collective-permute-start(bf16[3,256,1024]{2,1,0:T(8,128)(2,1)S(1)} %get-tuple-element.150.refs_1_), channel_id=1, source_target_pairs={{0,1},{1,0},{2,3},{3,2},{4,5},{5,4},{6,7},{7,6},{8,9},{9,8},{10,11... | collective-permute-start | bytes 4718600 | tf_op jit(solution)/shard_map/ppermute | solution.py:882
  186.7 19.6 %collective-permute-start.18 = (bf16[512,1024]{1,0:T(8,128)(2,1)S(1)}, bf16[512,1024]{1,0:T(8,128)(2,1)S(1)}, u32[]{:S(2)}, u32[]{:S(2)}) collective-permute-start(bf16[512,1024]{1,0:T(8,128)(2,1)S(1)} %copy-done.82), channel_id=1, source_target_pairs={{0,2},{1,9},{2,0},{3,11},{4,6},{5,13},{6,4},{7,15},{8,10},{9,1},{1... | collective-permute-start | bytes 3145736 | tf_op jit(solution)/shard_map/ppermute | solution.py:909
  187.3 76.1 %collective-permute-start.17 = (bf16[512,1024]{1,0:T(8,128)(2,1)S(1)}, bf16[512,1024]{1,0:T(8,128)(2,1)S(1)}, u32[]{:S(2)}, u32[]{:S(2)}) collective-permute-start(bf16[512,1024]{1,0:T(8,128)(2,1)S(1)} %copy-done.69), channel_id=1, source_target_pairs={{0,4},{1,3},{2,6},{3,1},{4,0},{5,7},{6,2},{7,5},{8,12},{9,11},{10,... | collective-permute-start | bytes 3145736 | tf_op jit(solution)/shard_map/ppermute | solution.py:909
  187.3 92.8 %collective-permute-start.12 = (bf16[3,512,512]{2,1,0:T(8,128)(2,1)}, bf16[3,512,512]{2,1,0:T(8,128)(2,1)S(1)}, u32[]{:S(2)}, u32[]{:S(2)}) collective-permute-start(bf16[3,512,512]{2,1,0:T(8,128)(2,1)} %shard_map.293.refs_3_), channel_id=1, source_target_pairs={{0,2},{1,3},{4,6},{5,7},{8,10},{9,11},{12,14},{13,15},{16,18},{17,... | collective-permute-start | bytes 4718600 | tf_op jit(solution)/shard_map/ppermute | solution.py:1211
  188.6 68.8 %collective-permute-start.20 = (bf16[256,1024]{1,0:T(8,128)(2,1)S(1)}, bf16[256,1024]{1,0:T(8,128)(2,1)S(1)}, u32[]{:S(2)}, u32[]{:S(2)}) collective-permute-start(bf16[256,1024]{1,0:T(8,128)(2,1)S(1)} %get-tuple-element.139.refs_13_), channel_id=1, source_target_pairs={{0,8},{1,3},{2,10},{3,1},{4,12},{5,7},{6,14},{7,5},{8,0},{9,11},{1... | collective-permute-start | bytes 1572872 | tf_op jit(solution)/shard_map/ppermute | solution.py:909
  207.1 55.6 %collective-permute-start.19 = (bf16[256,1024]{1,0:T(8,128)(2,1)S(1)}, bf16[256,1024]{1,0:T(8,128)(2,1)S(1)}, u32[]{:S(2)}, u32[]{:S(2)}) collective-permute-start(bf16[256,1024]{1,0:T(8,128)(2,1)S(1)} %get-tuple-element.148.refs_5_), channel_id=1, source_target_pairs={{0,8},{1,3},{2,10},{3,1},{4,12},{5,7},{6,14},{7,5},{8,0},{9,11},{1... | collective-permute-start | bytes 1572872 | tf_op jit(solution)/shard_map/ppermute | solution.py:909
  207.2 71.4 %collective-permute-start.15 = (bf16[512,1024]{1,0:T(8,128)(2,1)}, bf16[512,1024]{1,0:T(8,128)(2,1)}, u32[]{:S(2)}, u32[]{:S(2)}) collective-permute-start(bf16[512,1024]{1,0:T(8,128)(2,1)} %get-tuple-element.141), channel_id=1, source_target_pairs={{0,8},{1,3},{2,10},{3,1},{4,12},{5,7},{6,14},{7,5},{8,0},{9,11},{1... | collective-permute-start | bytes 3145736 | tf_op jit(solution)/shard_map/ppermute | solution.py:909
  259.5 14.0 %collective-permute-start.23 = (bf16[256,1024]{1,0:T(8,128)(2,1)S(1)}, bf16[256,1024]{1,0:T(8,128)(2,1)}, u32[]{:S(2)}, u32[]{:S(2)}) collective-permute-start(bf16[256,1024]{1,0:T(8,128)(2,1)S(1)} %shard_map.298.refs_3_.refs_1_), channel_id=1, source_target_pairs={{0,16},{1,17},{2,18},{3,19},{4,20},{5,21},{6,22},{7,23},{8,24},{9,... | collective-permute-start | bytes 1572872 | tf_op jit(solution)/shard_map/ppermute | solution.py:909
  265.7 11.7 %collective-permute-start.22 = (bf16[256,1024]{1,0:T(8,128)(2,1)}, bf16[256,1024]{1,0:T(8,128)(2,1)}, u32[]{:S(2)}, u32[]{:S(2)}) collective-permute-start(bf16[256,1024]{1,0:T(8,128)(2,1)} %get-tuple-element.153.refs_3_), channel_id=1, source_target_pairs={{0,2},{1,9},{2,0},{3,11},{4,6},{5,13},{6,4},{7,15},{8,10},{9,1},{1... | collective-permute-start | bytes 1572872 | tf_op jit(solution)/shard_map/ppermute | solution.py:909
  266.3 5.2 %collective-permute-start.24 = (bf16[128,1024]{1,0:T(8,128)(2,1)S(1)}, bf16[128,1024]{1,0:T(8,128)(2,1)S(1)}, u32[]{:S(2)}, u32[]{:S(2)}) collective-permute-start(bf16[128,1024]{1,0:T(8,128)(2,1)S(1)} %get-tuple-element.151.refs_3_), channel_id=1, source_target_pairs={{0,4},{1,5},{2,6},{3,7},{4,0},{5,1},{6,2},{7,3},{8,12},{9,13},{10,... | collective-permute-start | bytes 786440 | tf_op jit(solution)/shard_map/ppermute | solution.py:909
  271.5 7.0 %collective-permute-start.16 = (f32[4,1024]{1,0:T(4,128)S(1)}, f32[4,1024]{1,0:T(4,128)S(1)}, u32[]{:S(2)}, u32[]{:S(2)}) collective-permute-start(f32[4,1024]{1,0:T(4,128)S(1)} %pad_maximum_fusion.4.refs_3_), channel_id=1, source_target_pairs={{0,1},{1,0},{2,3},{3,2},{4,5},{5,4},{6,7},{7,6},{8,9},{9,8},{10,11... | collective-permute-start | bytes 49160 | tf_op jit(solution)/shard_map/ppermute | solution.py:882
  280.1 21.8 %copy-start.5 = (bf16[3,1,512,1024]{3,2,1,0:T(8,128)(2,1)S(1)}, bf16[3,1,512,1024]{3,2,1,0:T(8,128)(2,1)}, u32[]{:S(2)}) copy-start(bf16[3,1,512,1024]{3,2,1,0:T(8,128)(2,1)} %refs_1_.11) | copy-start | bytes 9437188
  280.2 21.7 %copy-start.44 = (bf16[3,1024,256]{2,1,0:T(8,128)(2,1)S(1)}, bf16[3,1024,256]{2,1,0:T(8,128)(2,1)}, u32[]{:S(2)}) copy-start(bf16[3,1024,256]{2,1,0:T(8,128)(2,1)} %refs_4_.3) | copy-start | bytes 4718596
  280.2 21.7 %copy-start.72 = (bf16[3,170,256]{2,1,0:T(8,128)(2,1)S(1)}, bf16[3,170,256]{2,1,0:T(8,128)(2,1)}, u32[]{:S(2)}) copy-start(bf16[3,170,256]{2,1,0:T(8,128)(2,1)} %refs_5_.1) | copy-start | bytes 783364
  280.2 21.7 %collective-permute-start.25 = (bf16[3,512,512]{2,1,0:T(8,128)(2,1)S(1)}, bf16[3,512,512]{2,1,0:T(8,128)(2,1)S(1)}, u32[]{:S(2)}, u32[]{:S(2)}) collective-permute-start(bf16[3,512,512]{2,1,0:T(8,128)(2,1)S(1)} %shard_map.305.refs_3_.refs_2_), channel_id=1, source_target_pairs={{0,1},{1,0},{2,3},{3,2},{4,5},{5,4},{6,7},{7,6},{8,9},{9,8},{10,11... | collective-permute-start | bytes 4718600 | tf_op jit(solution)/shard_map/ppermute | solution.py:882
  280.3 20.9 %collective-permute-start.26 = (bf16[128,1024]{1,0:T(8,128)(2,1)S(1)}, bf16[128,1024]{1,0:T(8,128)(2,1)S(1)}, u32[]{:S(2)}, u32[]{:S(2)}) collective-permute-start(bf16[128,1024]{1,0:T(8,128)(2,1)S(1)} %shard_map.301.refs_3_.refs_1_), channel_id=1, source_target_pairs={{0,16},{1,17},{2,18},{3,19},{4,20},{5,21},{6,22},{7,23},{8,24},{9,... | collective-permute-start | bytes 786440 | tf_op jit(solution)/shard_map/ppermute | solution.py:909
  284.8 28.3 %collective-permute-start.30 = (bf16[256,1024]{1,0:T(8,128)(2,1)S(1)}, bf16[256,1024]{1,0:T(8,128)(2,1)S(1)}, u32[]{:S(2)}, u32[]{:S(2)}) collective-permute-start(bf16[256,1024]{1,0:T(8,128)(2,1)S(1)} %shard_map.302.refs_3_.refs_1_), channel_id=1, source_target_pairs={{0,8},{1,3},{2,10},{3,1},{4,12},{5,7},{6,14},{7,5},{8,0},{9,11},{1... | collective-permute-start | bytes 1572872 | tf_op jit(solution)/shard_map/ppermute | solution.py:909
  284.8 32.0 %collective-permute-start.27 = (bf16[256,1024]{1,0:T(8,128)(2,1)S(1)}, bf16[256,1024]{1,0:T(8,128)(2,1)S(1)}, u32[]{:S(2)}, u32[]{:S(2)}) collective-permute-start(bf16[256,1024]{1,0:T(8,128)(2,1)S(1)} %get-tuple-element.155.refs_1_), channel_id=1, source_target_pairs={{0,2},{1,5},{2,0},{3,7},{4,6},{5,1},{6,4},{7,3},{8,10},{9,13},{10,... | collective-permute-start | bytes 1572872 | tf_op jit(solution)/shard_map/ppermute | solution.py:909
  284.9 33.4 %collective-permute-start.33 = (bf16[256,1024]{1,0:T(8,128)(2,1)S(1)}, bf16[256,1024]{1,0:T(8,128)(2,1)S(1)}, u32[]{:S(2)}, u32[]{:S(2)}) collective-permute-start(bf16[256,1024]{1,0:T(8,128)(2,1)S(1)} %shard_map.303.refs_5_.refs_1_), channel_id=1, source_target_pairs={{0,16},{1,17},{2,18},{3,19},{4,20},{5,21},{6,22},{7,23},{8,24},{9,... | collective-permute-start | bytes 1572872 | tf_op jit(solution)/shard_map/ppermute | solution.py:909
  301.8 12.9 %collective-permute-start.29 = (bf16[128,1024]{1,0:T(8,128)(2,1)S(1)}, bf16[128,1024]{1,0:T(8,128)(2,1)S(1)}, u32[]{:S(2)}, u32[]{:S(2)}) collective-permute-start(bf16[128,1024]{1,0:T(8,128)(2,1)S(1)} %shard_map.306.refs_6_.refs_1_), channel_id=1, source_target_pairs={{0,4},{1,5},{2,6},{3,7},{4,0},{5,1},{6,2},{7,3},{8,12},{9,13},{10,... | collective-permute-start | bytes 786440 | tf_op jit(solution)/shard_map/ppermute | solution.py:909
  310.7 29.8 %collective-permute-start.38 = (bf16[1536,256]{1,0:T(8,128)(2,1)S(1)}, bf16[1536,256]{1,0:T(8,128)(2,1)S(1)}, u32[]{:S(2)}, u32[]{:S(2)}) collective-permute-start(bf16[1536,256]{1,0:T(8,128)(2,1)S(1)} %get-tuple-element.165), channel_id=1, source_target_pairs={{0,4},{1,9},{2,6},{3,11},{4,0},{5,13},{6,2},{7,15},{8,12},{9,1},{1... | collective-permute-start | bytes 2359304 | tf_op jit(solution)/shard_map/ppermute | solution.py:909
  313.1 3.7 collective-permute-start.28
  315.3 25.9 %collective-permute-start.37 = (bf16[256,1024]{1,0:T(8,128)(2,1)S(1)}, bf16[256,1024]{1,0:T(8,128)(2,1)S(1)}, u32[]{:S(2)}, u32[]{:S(2)}) collective-permute-start(bf16[256,1024]{1,0:T(8,128)(2,1)S(1)} %shard_map.309.refs_5_.refs_1_), channel_id=1, source_target_pairs={{0,8},{1,3},{2,10},{3,1},{4,12},{5,7},{6,14},{7,5},{8,0},{9,11},{1... | collective-permute-start | bytes 1572872 | tf_op jit(solution)/shard_map/ppermute | solution.py:909
  318.9 23.0 %collective-permute-start.36 = (bf16[256,1024]{1,0:T(8,128)(2,1)S(1)}, bf16[256,1024]{1,0:T(8,128)(2,1)S(1)}, u32[]{:S(2)}, u32[]{:S(2)}) collective-permute-start(bf16[256,1024]{1,0:T(8,128)(2,1)S(1)} %shard_map.311.refs_5_.refs_1_), channel_id=1, source_target_pairs={{0,2},{1,9},{2,0},{3,11},{4,6},{5,13},{6,4},{7,15},{8,10},{9,1},{1... | collective-permute-start | bytes 1572872 | tf_op jit(solution)/shard_map/ppermute | solution.py:909
  319.5 20.4 %collective-permute-start.31 = (bf16[128,1024]{1,0:T(8,128)(2,1)S(1)}, bf16[128,1024]{1,0:T(8,128)(2,1)S(1)}, u32[]{:S(2)}, u32[]{:S(2)}) collective-permute-start(bf16[128,1024]{1,0:T(8,128)(2,1)S(1)} %get-tuple-element.160.refs_3_), channel_id=1, source_target_pairs={{0,4},{1,9},{2,6},{3,11},{4,0},{5,13},{6,2},{7,15},{8,12},{9,1},{1... | collective-permute-start | bytes 786440 | tf_op jit(solution)/shard_map/ppermute | solution.py:909
  320.5 3.0 collective-permute-start.32
  323.4 40.9 %collective-permute-start.42 = (bf16[512,1024]{1,0:T(8,128)(2,1)S(1)}, bf16[512,1024]{1,0:T(8,128)(2,1)S(1)}, u32[]{:S(2)}, u32[]{:S(2)}) collective-permute-start(bf16[512,1024]{1,0:T(8,128)(2,1)S(1)} %shard_map.308.refs_3_.refs_1_), channel_id=1, source_target_pairs={{0,4},{1,9},{2,6},{3,11},{4,0},{5,13},{6,2},{7,15},{8,12},{9,1},{1... | collective-permute-start | bytes 3145736 | tf_op jit(solution)/shard_map/ppermute | solution.py:909
  342.5 51.0 %collective-permute-start.46 = (bf16[512,1024]{1,0:T(8,128)(2,1)S(1)}, bf16[512,1024]{1,0:T(8,128)(2,1)S(1)}, u32[]{:S(2)}, u32[]{:S(2)}) collective-permute-start(bf16[512,1024]{1,0:T(8,128)(2,1)S(1)} %shard_map.315.refs_5_.refs_1_), channel_id=1, source_target_pairs={{0,4},{1,3},{2,6},{3,1},{4,0},{5,7},{6,2},{7,5},{8,12},{9,11},{10,... | collective-permute-start | bytes 3145736 | tf_op jit(solution)/shard_map/ppermute | solution.py:909
  342.6 18.7 %collective-permute-start.34 = (bf16[128,1024]{1,0:T(8,128)(2,1)S(1)}, bf16[128,1024]{1,0:T(8,128)(2,1)S(1)}, u32[]{:S(2)}, u32[]{:S(2)}) collective-permute-start(bf16[128,1024]{1,0:T(8,128)(2,1)S(1)} %get-tuple-element.162.refs_3_.refs_1_), channel_id=1, source_target_pairs={{0,16},{1,17},{2,18},{3,19},{4,20},{5,21},{6,22},{7,23},{8,24},{9,... | collective-permute-start | bytes 786440 | tf_op jit(solution)/shard_map/ppermute | solution.py:909
  350.9 15.3 %collective-permute-start.41 = (bf16[768,256]{1,0:T(8,128)(2,1)S(1)}, bf16[768,256]{1,0:T(8,128)(2,1)S(1)}, u32[]{:S(2)}, u32[]{:S(2)}) collective-permute-start(bf16[768,256]{1,0:T(8,128)(2,1)S(1)} %get-tuple-element.166.refs_3_), channel_id=1, source_target_pairs={{0,8},{1,5},{2,10},{3,7},{4,12},{5,1},{6,14},{7,3},{8,0},{9,13},{1... | collective-permute-start | bytes 1179656 | tf_op jit(solution)/shard_map/ppermute | solution.py:909
  351.2 10.1 %collective-permute-start.35 = (f32[4,1024]{1,0:T(4,128)S(1)}, f32[4,1024]{1,0:T(4,128)S(1)}, u32[]{:S(2)}, u32[]{:S(2)}) collective-permute-start(f32[4,1024]{1,0:T(4,128)S(1)} %get-tuple-element.163.refs_3_), channel_id=1, source_target_pairs={{0,8},{4,12},{8,0},{12,4},{16,24},{20,28},{24,16},{28,20},{1,9},{5... | collective-permute-start | bytes 49160 | tf_op jit(solution)/shard_map/ppermute | solution.py:882
  361.9 31.0 %collective-permute-start.39 = (bf16[128,1024]{1,0:T(8,128)(2,1)S(1)}, bf16[128,1024]{1,0:T(8,128)(2,1)S(1)}, u32[]{:S(2)}, u32[]{:S(2)}) collective-permute-start(bf16[128,1024]{1,0:T(8,128)(2,1)S(1)} %get-tuple-element.167.refs_3_.refs_1_), channel_id=1, source_target_pairs={{0,4},{1,9},{2,6},{3,11},{4,0},{5,13},{6,2},{7,15},{8,12},{9,1},{1... | collective-permute-start | bytes 786440 | tf_op jit(solution)/shard_map/ppermute | solution.py:909
  364.2 31.6 %collective-permute-start.45 = (bf16[512,1024]{1,0:T(8,128)(2,1)S(1)}, bf16[512,1024]{1,0:T(8,128)(2,1)S(1)}, u32[]{:S(2)}, u32[]{:S(2)}) collective-permute-start(bf16[512,1024]{1,0:T(8,128)(2,1)S(1)} %shard_map.314.refs_3_.refs_1_), channel_id=1, source_target_pairs={{0,2},{1,9},{2,0},{3,11},{4,6},{5,13},{6,4},{7,15},{8,10},{9,1},{1... | collective-permute-start | bytes 3145736 | tf_op jit(solution)/shard_map/ppermute | solution.py:909
  365.0 68.1 %collective-permute-start.48 = (bf16[1024,1024]{1,0:T(8,128)(2,1)S(1)}, bf16[1024,1024]{1,0:T(8,128)(2,1)S(1)}, u32[]{:S(2)}, u32[]{:S(2)}) collective-permute-start(bf16[1024,1024]{1,0:T(8,128)(2,1)S(1)} %shard_map.317.refs_3_.refs_1_), channel_id=1, source_target_pairs={{0,2},{1,5},{2,0},{3,7},{4,6},{5,1},{6,4},{7,3},{8,10},{9,13},{10,... | collective-permute-start | bytes 6291464 | tf_op jit(solution)/shard_map/ppermute | solution.py:909
  366.2 26.7 %collective-permute-start.40 = (f32[4,1024]{1,0:T(4,128)S(1)}, f32[4,1024]{1,0:T(4,128)S(1)}, u32[]{:S(2)}, u32[]{:S(2)}) collective-permute-start(f32[4,1024]{1,0:T(4,128)S(1)} %get-tuple-element.168.refs_3_), channel_id=1, source_target_pairs={{0,16},{4,20},{8,24},{12,28},{16,0},{20,4},{24,8},{28,12},{1,17},{... | collective-permute-start | bytes 49160 | tf_op jit(solution)/shard_map/ppermute | solution.py:882
  394.2 55.4 %collective-permute-start.50 = (bf16[1024,1024]{1,0:T(8,128)(2,1)S(1)}, bf16[1024,1024]{1,0:T(8,128)(2,1)S(1)}, u32[]{:S(2)}, u32[]{:S(2)}) collective-permute-start(bf16[1024,1024]{1,0:T(8,128)(2,1)S(1)} %shard_map.320.refs_3_.refs_1_), channel_id=1, source_target_pairs={{0,8},{1,5},{2,10},{3,7},{4,12},{5,1},{6,14},{7,3},{8,0},{9,13},{1... | collective-permute-start | bytes 6291464 | tf_op jit(solution)/shard_map/ppermute | solution.py:909
  394.3 30.8 %collective-permute-start.43 = (bf16[256,1024]{1,0:T(8,128)(2,1)S(1)}, bf16[256,1024]{1,0:T(8,128)(2,1)S(1)}, u32[]{:S(2)}, u32[]{:S(2)}) collective-permute-start(bf16[256,1024]{1,0:T(8,128)(2,1)S(1)} %get-tuple-element.170.refs_3_.refs_1_), channel_id=1, source_target_pairs={{0,2},{1,5},{2,0},{3,7},{4,6},{5,1},{6,4},{7,3},{8,10},{9,13},{10,... | collective-permute-start | bytes 1572872 | tf_op jit(solution)/shard_map/ppermute | solution.py:909
  395.8 11.8 %collective-permute-start.44 = (bf16[768,256]{1,0:T(8,128)(2,1)S(1)}, bf16[768,256]{1,0:T(8,128)(2,1)S(1)}, u32[]{:S(2)}, u32[]{:S(2)}) collective-permute-start(bf16[768,256]{1,0:T(8,128)(2,1)S(1)} %shard_map.318.refs_5_.refs_1_), channel_id=1, source_target_pairs={{0,16},{1,17},{2,18},{3,19},{4,20},{5,21},{6,22},{7,23},{8,24},{9,... | collective-permute-start | bytes 1179656 | tf_op jit(solution)/shard_map/ppermute | solution.py:909
  409.8 21.9 %collective-permute-start.49 = (bf16[768,256]{1,0:T(8,128)(2,1)S(1)}, bf16[768,256]{1,0:T(8,128)(2,1)S(1)}, u32[]{:S(2)}, u32[]{:S(2)}) collective-permute-start(bf16[768,256]{1,0:T(8,128)(2,1)S(1)} %shard_map.322.refs_3_.refs_1_), channel_id=1, source_target_pairs={{0,8},{1,5},{2,10},{3,7},{4,12},{5,1},{6,14},{7,3},{8,0},{9,13},{1... | collective-permute-start | bytes 1179656 | tf_op jit(solution)/shard_map/ppermute | solution.py:909
  425.7 13.7 %collective-permute-start.47 = (bf16[512,1024]{1,0:T(8,128)(2,1)S(1)}, bf16[512,1024]{1,0:T(8,128)(2,1)S(1)}, u32[]{:S(2)}, u32[]{:S(2)}) collective-permute-start(bf16[512,1024]{1,0:T(8,128)(2,1)S(1)} %shard_map.323.refs_3_.refs_1_), channel_id=1, source_target_pairs={{0,8},{1,3},{2,10},{3,1},{4,12},{5,7},{6,14},{7,5},{8,0},{9,11},{1... | collective-permute-start | bytes 3145736 | tf_op jit(solution)/shard_map/ppermute | solution.py:909
  432.3 13.3 %collective-permute-start.51 = (bf16[1536,256]{1,0:T(8,128)(2,1)S(1)}, bf16[1536,256]{1,0:T(8,128)(2,1)S(1)}, u32[]{:S(2)}, u32[]{:S(2)}) collective-permute-start(bf16[1536,256]{1,0:T(8,128)(2,1)S(1)} %shard_map.324.refs_3_.refs_1_), channel_id=1, source_target_pairs={{0,4},{1,9},{2,6},{3,11},{4,0},{5,13},{6,2},{7,15},{8,12},{9,1},{1... | collective-permute-start | bytes 2359304 | tf_op jit(solution)/shard_map/ppermute | solution.py:909
  (71 other events, 263.1 us)
